TPU v7x, 32 devices: a whole 2x2x4 slice. The times are simulated.
32 devices in a mesh: groups: 2 (over x), shard: 16 (over z, y, core).
Axes of the slice: x: 2, y: 2, z: 4, core: 2. Of those that a mesh axis runs over, the one named last changes fastest.
Arguments:
- embed: bfloat16 [65536, 768], P(('groups', 'shard')), parts along dimension 0, may hold values from -6 to 6
- seed_mask: int32 [65536], P(('groups', 'shard')), parts along dimension 0, may hold values 0 or 1
- seed_class: int32 [65536], P(('groups', 'shard')), parts along dimension 0, may hold values from 0 to 255
- partner: int32 [32, 16], P(('groups', 'shard')), parts along dimension 0, may hold values from 0 to 7
- pair_local: int32 [2048], P(('groups', 'shard')), parts along dimension 0, may hold values from 0 to 7, as said below
- pair_peer: int32 [2048], P(('groups', 'shard')), parts along dimension 0, may hold values from 0 to 15, as said below
Outputs:
- labels: float32 [65536, 256], P(('groups', 'shard')), parts along dimension 0
There are 2 independent parts, one for each index of `groups`. A program takes and returns all parts, laid end to end along the dimension named above; each array names one. Nothing has to cross between parts.
Inputs may be any that keep to these rules, and one draw needn't show every extreme that they name: `pair_peer`: row r belongs to device r // 64 of shard, and its partner device is never that device itself; each device has pairs with the device after it and with the device before it, counted round. No two pairs of one device have both the same pair_local and the same pair_peer.
All inputs are finite; a program needn't handle non-finite values. No bound on the sum of `seed_mask` on one device may be relied on, other than what follows from the above.
Results may differ from a plain program's by a relative error of at most 0.0011.
Values may be sent and summed in bfloat16 or wider, within the bound.
No kernel may reach another device: no remote copies, remote signals or barrier semaphores. Data moves between devices by JAX's collectives and lax.ppermute only.
A program may use at most 128 MiB of HBM per device.

v0:
```python
import jax
import jax.numpy as jnp
from jax import lax
from jax.sharding import PartitionSpec as P

C = 256
TILE = 256
ITERS = 2


sharpness = 1.0
mixing = 0.8


def body(embed, seed_mask, seed_class, partner, pair_local, pair_peer):
    shards = lax.axis_size("shard")
    features = embed.shape[1]
    local_tiles = embed.reshape(-1, TILE, features)
    tile_count = local_tiles.shape[0]
    send_index = partner.reshape(-1)
    remote = lax.all_to_all(
        local_tiles[send_index], "shard", split_axis=0, concat_axis=0, tiled=True
    )
    local_squared_norm = jnp.sum(jnp.square(local_tiles.astype(jnp.float32)), axis=2)
    remote_norms = jnp.sum(jnp.square(remote.astype(jnp.float32)), axis=2)
    pair_count = pair_local.shape[0]
    block_share = 8
    block_count = pair_count // block_share
    local_blocks = pair_local.reshape(block_count, block_share)
    peer_blocks = pair_peer.reshape(block_count, block_share)
    positions = jnp.arange(block_count, dtype=jnp.int32)
    tile_ids = jnp.arange(tile_count, dtype=jnp.int32)
    shard_ids = jnp.arange(shards, dtype=jnp.int32)
    send_hot = (send_index[:, None] == tile_ids[None, :]).astype(jnp.float32)

    def kernel_block(local_index, peer_index):
        inner = jnp.einsum(
            "pad,pbd->pab",
            local_tiles[local_index],
            remote[peer_index],
            preferred_element_type=jnp.float32,
        )
        exponent = (
            2.0 * features
            - local_squared_norm[local_index][:, :, None]
            - remote_norms[peer_index][:, None, :]
            + 2.0 * inner
        ) * (sharpness / features)
        return jnp.exp(exponent).astype(jnp.bfloat16)

    def hot_rows(local_index, peer_index):
        local_onehot_labels = (local_index[:, None] == tile_ids[None, :]).astype(jnp.float32)
        peer_hot = (peer_index[:, None] == shard_ids[None, :]).astype(jnp.float32)
        return (local_onehot_labels, peer_hot)

    def degree_step(running, indices):
        local_index, peer_index = indices
        kernel = kernel_block(local_index, peer_index)
        local_onehot_labels, peer_hot = hot_rows(local_index, peer_index)
        row_sums = jnp.sum(kernel.astype(jnp.float32), axis=2)
        column_sums = jnp.sum(kernel.astype(jnp.float32), axis=1)
        local_degree = running[0] + jnp.einsum(
            "pt,pa->ta", local_onehot_labels, row_sums, precision=lax.Precision.HIGHEST
        )
        slot_degree = running[1] + jnp.einsum(
            "ps,pb->sb", peer_hot, column_sums, precision=lax.Precision.HIGHEST
        )
        return ((local_degree, slot_degree), kernel)

    initial = (jnp.zeros((tile_count, TILE), jnp.float32), jnp.zeros((shards, TILE), jnp.float32))
    (local_degree, slot_degree), kernel_matrices = lax.scan(
        degree_step, initial, (local_blocks, peer_blocks)
    )

    def block_kernel(position):
        return kernel_matrices[position]

    classes = jnp.arange(C)
    seeded = (seed_mask == 1)[:, None]
    target = jnp.where(seeded & (seed_class[:, None] == classes[None, :]), 1.0, 0.0).astype(
        jnp.float32
    )
    labels = jnp.where(seeded, target, 1.0 / C)
    back_sums = lax.all_to_all(slot_degree, "shard", split_axis=0, concat_axis=0, tiled=True)
    degree = (
        1.0
        + local_degree
        + jnp.einsum("st,sb->tb", send_hot, back_sums, precision=lax.Precision.HIGHEST)
    )
    for sweep in range(ITERS):
        rounded = labels.astype(jnp.bfloat16).reshape(tile_count, TILE, -1)
        incoming = lax.all_to_all(
            rounded[send_index], "shard", split_axis=0, concat_axis=0, tiled=True
        )

        def label_step(running, indices):
            position, local_index, peer_index = indices
            kernel = block_kernel(position)
            local_onehot_labels, peer_hot = hot_rows(local_index, peer_index)
            gathered_labels = jnp.einsum(
                "pab,pbc->pac", kernel, incoming[peer_index], preferred_element_type=jnp.float32
            )
            pushed = jnp.einsum(
                "pab,pac->pbc", kernel, rounded[local_index], preferred_element_type=jnp.float32
            )
            local_sum = running[0] + jnp.einsum(
                "nq,nfd->qfd", local_onehot_labels, gathered_labels, precision=lax.Precision.HIGHEST
            )
            slot_sum = running[1] + jnp.einsum(
                "ps,pbc->sbc", peer_hot, pushed, precision=lax.Precision.HIGHEST
            )
            return ((local_sum, slot_sum), None)

        zeros_pair = (
            jnp.zeros((tile_count, TILE, C), jnp.float32),
            jnp.zeros((shards, TILE, C), jnp.float32),
        )
        local_sum, slot_sum = lax.scan(
            label_step, zeros_pair, (positions, local_blocks, peer_blocks)
        )[0]
        returned = lax.all_to_all(slot_sum, "shard", split_axis=0, concat_axis=0, tiled=True)
        summed = local_sum + jnp.einsum(
            "st,sbc->tbc", send_hot, returned, precision=lax.Precision.HIGHEST
        )
        averaged = (labels + summed.reshape(labels.shape)) / degree.reshape(-1)[:, None]
        blended = mixing * averaged + (1.0 - mixing) * target
        squared = blended * blended
        labels = squared / jnp.sum(squared, axis=1, keepdims=True)
    return labels


def solution(mesh):
    in_specs = (
        P(("groups", "shard"), None),
        P(("groups", "shard")),
        P(("groups", "shard")),
        P(("groups", "shard"), None),
        P(("groups", "shard")),
        P(("groups", "shard")),
    )
    out_specs = P(("groups", "shard"), None)
    return jax.shard_map(body, mesh=mesh, in_specs=in_specs, out_specs=out_specs, check_vma=False)
```

profile of v0, /device:TPU:13, one launch (start us, length us, event | category | flops | bytes accessed | tf_op | source)
XLA Modules:
  0.0 919.9 jit_solution(5706238330702639379)
XLA Ops:
  0.7 5.4 gather_fusion.8
  6.1 6.8 all-to-all-start
  20.0 130.3 %all-to-all-done = bf16[16,256,768]{2,1,0:T(8,128)(2,1)} async-done(((bf16[16,256,768]{2,1,0:T(8,128)(2,1)}), bf16[16,256,768]{2,1,0:T(8,128)(2,1)}, u32[]{:S(2)}, u32[]{:S(2)}) %all-to-all-start) | async-done | bytes 6291488 | tf_op jit(solution)/shard_map/all_to_all | solution.py:21
  150.3 4.9 all-to-all-start.1
  155.2 4.1 multiply_reduce_fusion
  159.3 133.7 %while.45 = (s32[]{:T(128)}, f32[8,256]{1,0:T(8,128)S(1)}, f32[16,256]{1,0:T(8,128)S(1)}, bf16[8,8,256,256]{3,2,1,0:T(8,128)(2,1)}, s32[8,8]{1,0:T(8,128)S(1)}, ...) while((s32[]{:T(128)}, f32[8,256]{1,0:T(8,128)S(1)}, ...), condition=%wide.region_5.6_spmd.clone, body=%wide.region_2.5_spmd.clone.sunk | while | flops 810103040 | bytes 22176400 | solution.py:71
  161.8 5.2 gather_fusion.1
  168.0 5.2 convert_reduce_fusion.3
  178.5 5.2 gather_fusion.1
  184.8 5.2 convert_reduce_fusion.3
  195.1 5.2 gather_fusion.1
  201.4 5.2 convert_reduce_fusion.3
  211.8 5.2 gather_fusion.1
  218.1 5.2 convert_reduce_fusion.3
  228.5 5.2 gather_fusion.1
  234.8 5.2 convert_reduce_fusion.3
  245.2 5.2 gather_fusion.1
  251.5 5.2 convert_reduce_fusion.3
  261.9 5.2 gather_fusion.1
  268.2 5.2 convert_reduce_fusion.3
  278.6 5.2 gather_fusion.1
  284.9 5.2 convert_reduce_fusion.3
  293.6 6.0 all-to-all-start.3
  299.6 165.0 %while.46 = (s32[]{:T(128)}, f32[8,256,256]{2,0,1:T(8,128)}, f32[16,256,256]{2,0,1:T(8,128)}, s32[8,8]{1,0:T(8,128)S(1)}, s32[8]{0:T(128)S(1)}, /*index=5*/bf16[...) while((s32[]{:T(128)}, f32[8,256,256]{2,0,1:T(8,128)}, ...), condition=%wide.region_7.8_spmd.clone.clone, body=%wide.region_6.7_spmd.clone.clone.sunk | while | flops 693635328 | bytes 63982308 | solution.py:118
  305.9 3.6 select_add_fusion.8
  313.3 3.5 select_add_fusion.9
  325.1 5.2 select_add_fusion.8
  334.2 3.5 select_add_fusion.9
  345.9 5.2 select_add_fusion.8
  355.0 3.5 select_add_fusion.9
  366.7 5.2 select_add_fusion.8
  375.8 3.5 select_add_fusion.9
  387.5 5.2 select_add_fusion.8
  396.6 3.5 select_add_fusion.9
  408.4 5.2 select_add_fusion.8
  417.4 3.5 select_add_fusion.9
  429.2 5.2 select_add_fusion.8
  438.2 3.5 select_add_fusion.9
  450.0 5.2 select_add_fusion.8
  459.1 3.5 select_add_fusion.9
  464.6 6.6 copy.50
  471.2 6.2 all-to-all-start.2
  477.7 92.2 %all-to-all-done.2 = f32[16,256,256]{2,1,0:T(8,128)} async-done(((f32[16,256,256]{2,1,0:T(8,128)}), f32[16,256,256]{2,1,0:T(8,128)}, u32[]{:S(2)}, u32[]{:S(2)}) %all-to-all-start.2) | async-done | bytes 4194336 | tf_op jit(solution)/shard_map/all_to_all | solution.py:121
  569.8 8.6 fusion.107
  582.3 4.9 all-to-all-start.4
  587.2 47.4 %all-to-all-done.4 = bf16[16,256,256]{2,1,0:T(8,128)(2,1)S(1)} async-done(((bf16[16,256,256]{2,1,0:T(8,128)(2,1)}), bf16[16,256,256]{2,1,0:T(8,128)(2,1)S(1)}, u32[]{:S(2)}, u32[]{:S(2)}) %all-to-all-start.4) | async-done | bytes 2097184 | tf_op jit(solution)/shard_map/all_to_all | solution.py:92
  634.6 165.5 %while.47 = (s32[]{:T(128)}, f32[8,256,256]{2,0,1:T(8,128)}, f32[16,256,256]{2,0,1:T(8,128)}, s32[8,8]{1,0:T(8,128)S(1)}, s32[8]{0:T(128)S(1)}, /*index=5*/bf16[...) while((s32[]{:T(128)}, f32[8,256,256]{2,0,1:T(8,128)}, ...), condition=%wide.region_10.11_spmd.clone.clone, body=%wide.region_9.10_spmd.clone.clone.sunk | while | flops 691013888 | bytes 88089424 | solution.py:118
  640.4 3.6 select_add_fusion.10
  659.7 5.2 select_add_fusion.10
  680.6 5.2 select_add_fusion.10
  701.5 5.2 select_add_fusion.10
  711.1 3.5 select_add_fusion.11
  722.4 5.2 select_add_fusion.10
  743.2 5.2 select_add_fusion.10
  752.8 3.5 select_add_fusion.11
  764.1 5.2 select_add_fusion.10
  785.0 5.2 select_add_fusion.10
  794.6 3.5 select_add_fusion.11
  800.1 6.6 copy.57
  806.8 4.9 all-to-all-start.5
  811.7 3.7 copy.52
  815.5 88.6 %all-to-all-done.5 = f32[16,256,256]{2,1,0:T(8,128)} async-done(((f32[16,256,256]{2,1,0:T(8,128)}), f32[16,256,256]{2,1,0:T(8,128)}, u32[]{:S(2)}, u32[]{:S(2)}) %all-to-all-start.5) | async-done | bytes 4194336 | tf_op jit(solution)/shard_map/all_to_all | solution.py:121
  904.1 7.8 fusion.77
  914.1 5.8 fusion.85
  (440 shorter events, 246.8 us)
Async XLA Ops:
  6.1 6.9 copy-start.21
  6.1 7.0 copy-start
  6.1 144.2 %all-to-all-start = ((bf16[16,256,768]{2,1,0:T(8,128)(2,1)}), bf16[16,256,768]{2,1,0:T(8,128)(2,1)}, u32[]{:S(2)}, u32[]{:S(2)}) async-start(bf16[16,256,768]{2,1,0:T(8,128)(2,1)} %gather_fusion.8), calls=%async_computation | async-start | bytes 12582912 | tf_op jit(solution)/shard_map/all_to_all | solution.py:21
  14.0 5.9 copy-start.17
  150.3 143.3 %all-to-all-start.1 = ((bf16[16,256,256]{2,1,0:T(8,128)(2,1)}), bf16[16,256,256]{2,1,0:T(8,128)(2,1)}, u32[]{:S(2)}, u32[]{:S(2)}) async-start(bf16[16,256,256]{2,1,0:T(8,128)(2,1)} %gather_fusion.9), calls=%async_computation.1 | async-start | bytes 4194304 | tf_op jit(solution)/shard_map/all_to_all | solution.py:92
  293.6 177.6 %all-to-all-start.3 = ((f32[16,1,256]{2,1,0:T(1,128)}), f32[16,1,256]{2,1,0:T(1,128)S(1)}, u32[]{:S(2)}, u32[]{:S(2)}) async-start(f32[16,1,256]{2,1,0:T(1,128)} %all_to_all.26), calls=%async_computation.3 | async-start | bytes 32768 | tf_op jit(solution)/shard_map/all_to_all | solution.py:84
  310.8 2.5 copy-start.1
  316.9 2.0 copy-start.2
  331.7 2.5 copy-start.1
  337.7 2.0 copy-start.2
  352.5 2.5 copy-start.1
  358.5 2.0 copy-start.2
  373.3 2.5 copy-start.1
  379.3 2.0 copy-start.2
  394.1 2.5 copy-start.1
  414.9 2.5 copy-start.1
  421.0 2.0 copy-start.2
  435.7 2.5 copy-start.1
  441.8 2.0 copy-start.2
  456.6 2.5 copy-start.1
  462.6 2.0 copy-start.2
  471.2 6.2 copy-start.20
  471.2 98.6 %copy-start.7 = (f32[8,256,256]{2,0,1:T(8,128)S(1)}, f32[8,256,256]{2,0,1:T(8,128)}, u32[]{:S(2)}) copy-start(f32[8,256,256]{2,0,1:T(8,128)} %get-tuple-element.234) | copy-start | bytes 6291460
  471.2 98.6 %all-to-all-start.2 = ((f32[16,256,256]{2,1,0:T(8,128)}), f32[16,256,256]{2,1,0:T(8,128)}, u32[]{:S(2)}, u32[]{:S(2)}) async-start(f32[16,256,256]{2,1,0:T(8,128)} %copy.50), calls=%async_computation.2 | async-start | bytes 8388608 | tf_op jit(solution)/shard_map/all_to_all | solution.py:121
  477.6 100.8 %copy-start.13 = (f32[8,256]{0,1:T(8,128)}, f32[8,256]{0,1:T(8,128)S(1)}, u32[]{:S(2)}) copy-start(f32[8,256]{0,1:T(8,128)S(1)} %copy.53) | copy-start | bytes 24580
  582.3 52.3 %all-to-all-start.4 = ((bf16[16,256,256]{2,1,0:T(8,128)(2,1)}), bf16[16,256,256]{2,1,0:T(8,128)(2,1)S(1)}, u32[]{:S(2)}, u32[]{:S(2)}) async-start(bf16[16,256,256]{2,1,0:T(8,128)(2,1)} %gather_fusion.10), calls=%async_computation.4 | async-start | bytes 4194304 | tf_op jit(solution)/shard_map/all_to_all | solution.py:92
  634.6 3.5 copy-start.9
  645.9 2.5 copy-start.3
  648.4 5.5 copy-start.6
  648.4 5.5 copy-start.10
  653.9 3.5 copy-start.9
  666.8 2.5 copy-start.3
  669.3 5.5 copy-start.6
  669.3 5.5 copy-start.10
  674.8 3.5 copy-start.9
  687.7 2.5 copy-start.3
  690.2 5.5 copy-start.6
  690.2 5.5 copy-start.10
  695.7 3.5 copy-start.9
  708.6 2.5 copy-start.3
  711.1 5.5 copy-start.6
  711.1 5.5 copy-start.10
  716.6 3.5 copy-start.9
  729.4 2.5 copy-start.3
  731.9 5.5 copy-start.6
  731.9 5.5 copy-start.10
  737.5 3.5 copy-start.9
  750.3 2.5 copy-start.3
  752.8 5.5 copy-start.6
  752.8 5.5 copy-start.10
  758.3 3.5 copy-start.9
  771.2 2.5 copy-start.3
  773.7 5.5 copy-start.6
  773.7 5.5 copy-start.10
  779.2 3.5 copy-start.9
  792.1 2.5 copy-start.3
  794.6 5.5 copy-start.6
  794.6 5.5 copy-start.10
  806.8 97.4 %all-to-all-start.5 = ((f32[16,256,256]{2,1,0:T(8,128)}), f32[16,256,256]{2,1,0:T(8,128)}, u32[]{:S(2)}, u32[]{:S(2)}) async-start(f32[16,256,256]{2,1,0:T(8,128)} %copy.57), calls=%async_computation.5 | async-start | bytes 8388608 | tf_op jit(solution)/shard_map/all_to_all | solution.py:121
  811.7 92.4 %copy-start.8 = (f32[8,256,256]{2,0,1:T(8,128)S(1)}, f32[8,256,256]{2,0,1:T(8,128)}, u32[]{:S(2)}) copy-start(f32[8,256,256]{2,0,1:T(8,128)} %get-tuple-element.238) | copy-start | bytes 6291460
  811.7 92.4 %copy-start.14 = (f32[8,256]{0,1:T(8,128)S(1)}, f32[8,256]{0,1:T(8,128)}, u32[]{:S(2)}) copy-start(f32[8,256]{0,1:T(8,128)} %copy-done.13) | copy-start | bytes 24580
  912.0 2.1 copy-start.11
  912.0 2.1 copy-start.16
  912.0 2.1 copy-start.18
  (21 other events, 30.1 us)
where the time goes:
time: 923 us; the launch traced here: 920 us
  waiting for transfers between devices  359 us (39%)
  matrix products  255 us (28%)
  local copies, waits for them, and re-layouts  223 us (24%)
  starting transfers between devices  33.7 us (4%)
  loops' own time  30.1 us (3%)
  other arithmetic  19 us (2%)
    all_to_all x2, waiting for transfers between devices, body(): lax.all_to_all(slot_sum, 'shard', split_axis=0, concat_axis=0, tiled=True)  181 us
    all_to_all x1, waiting for transfers between devices, body(): lax.all_to_all(local_tiles[send_index], 'shard', split_axis=0, concat_axi...  130 us
    dot_general x16, matrix products, label_step(): jnp.einsum('nq,nfd->qfd', local_onehot_labels, gathered_labels, precision...  80.3 us
    dot_general x16, matrix products, label_step(): jnp.einsum('ps,pbc->sbc', peer_hot, pushed, precision=lax.Precision.HIGHEST)  56.2 us
    while x128, local copies, waits for them, and re-layouts  49.7 us
    all_to_all x2, waiting for transfers between devices, body(): lax.all_to_all(rounded[send_index], 'shard', split_axis=0, concat_axis=0,...  47.4 us
    dot_general x8, matrix products, kernel_block(): jnp.einsum('pad,pbd->pab', local_tiles[local_index], remote[peer_index],...  41.5 us
    gather x8, local copies, waits for them, and re-layouts, kernel_block(): remote[peer_index]  41.2 us
  transfers between devices with their start and end apart: 6, of which 4 were waited for; matrix products, arithmetic and copies ran while one was open for 31% of the time, Pallas kernels for 0%

commit v1 on v0

v1 whole, which is shorter than its diff:
```python
import math

import jax
import jax.numpy as jnp
from jax import lax
from jax.experimental import pallas as pl
from jax.experimental.pallas import tpu as pltpu
from jax.sharding import PartitionSpec as P

C = 256
TILE = 256
ITERS = 2
WINDOW = 4

sharpness = 1.0
mixing = 0.8

LOG2E = math.log2(math.e)


def slot_kernel(sel, eloc, erem, bloc, brem, lloc, lrem, gin, kout, pout, gout, *, scale):
    step = pl.program_id(0)
    count = sel[0]

    @pl.when(step == 0)
    def _():
        pout[...] = jnp.zeros_like(pout)

    @pl.when((step == 0) & (count == 0))
    def _():
        gout[...] = gin[...]
        kout[...] = jnp.zeros_like(kout)

    @pl.when(step < count)
    def _():
        inner = lax.dot_general(
            eloc[0], erem[...], (((1,), (1,)), ((), ())), preferred_element_type=jnp.float32
        )
        k = jnp.exp2(inner * scale + (bloc[0] + brem[...])).astype(jnp.bfloat16)
        kout[0] = k
        gout[0] = gin[0] + jnp.dot(k, lrem[...], preferred_element_type=jnp.float32)
        pout[...] += lax.dot_general(
            k, lloc[0], (((0,), (0,)), ((), ())), preferred_element_type=jnp.float32
        )


def push_kernel(sel, kref, lloc, pout):
    step = pl.program_id(0)

    @pl.when(step == 0)
    def _():
        pout[...] = jnp.zeros_like(pout)

    @pl.when(step < sel[0])
    def _():
        pout[...] += lax.dot_general(
            kref[0], lloc[0], (((0,), (0,)), ((), ())), preferred_element_type=jnp.float32
        )


def gather_kernel(sel, kref, lrem, gin, gout):
    step = pl.program_id(0)
    count = sel[0]

    @pl.when((step == 0) & (count == 0))
    def _():
        gout[...] = gin[...]

    @pl.when(step < count)
    def _():
        gout[0] = gin[0] + jnp.dot(kref[0], lrem[...], preferred_element_type=jnp.float32)


def body(embed, seed_mask, seed_class, partner, pair_local, pair_peer):
    n = lax.axis_size("shard")
    me = lax.axis_index("shard")
    features = embed.shape[1]
    tiles = embed.reshape(-1, TILE, features)
    count_t = tiles.shape[0]
    mine = partner.reshape(-1)
    half = n // 2
    order = []
    for k in range(half):
        order.append(half + k)
        if k + 1 < half:
            order.append(k + 1)

    def swap(value, s):
        return lax.ppermute(value, "shard", [(q, q ^ s) for q in range(n)])

    tile_ids = jnp.arange(count_t, dtype=jnp.int32)
    shard_ids = jnp.arange(n, dtype=jnp.int32)
    active = jnp.any(
        (pair_peer[None, None, :] == shard_ids[:, None, None])
        & (pair_local[None, None, :] == tile_ids[None, :, None]),
        axis=2,
    )
    counts = jnp.sum(active.astype(jnp.int32), axis=1)
    place = jnp.sum(
        (active[:, None, :] & (tile_ids[None, None, :] < tile_ids[None, :, None])).astype(jnp.int32), axis=2
    )
    wanted = jnp.minimum(tile_ids[None, :], jnp.maximum(counts - 1, 0)[:, None])
    listed = jnp.sum(
        jnp.where(active[:, None, :] & (place[:, None, :] == wanted[:, :, None]), tile_ids[None, None, :], 0),
        axis=2,
    )
    selection = jnp.concatenate([counts[:, None], listed], axis=1).astype(jnp.int32)

    norms = jnp.sum(jnp.square(tiles.astype(jnp.float32)), axis=2)
    bias = (1.0 - norms * (1.0 / features)) * (sharpness * LOG2E)
    seeded = seed_mask == 1
    classes = jnp.where(seeded, seed_class, -1).reshape(count_t, TILE)
    meta = jnp.stack([bias, classes.astype(jnp.float32)], axis=1)
    meta_in = lax.all_to_all(meta[mine], "shard", split_axis=0, concat_axis=0, tiled=True)
    class_ids = jnp.arange(C, dtype=jnp.float32)

    def first_labels(ids):
        return jnp.where(
            ids[..., None] < 0, 1.0 / C, (ids[..., None] == class_ids).astype(jnp.float32)
        )

    labels = first_labels(classes.astype(jnp.float32))
    target = jnp.where(seeded.reshape(count_t, TILE)[..., None], labels, 0.0)
    rounded = labels.astype(jnp.bfloat16)
    rounded_in = first_labels(meta_in[:, 1]).astype(jnp.bfloat16)
    bias_column = bias[:, :, None]

    block = (1, TILE, C)

    def at_list(g, sel):
        return (sel[1 + g], 0, 0)

    def at_place(g, sel):
        return (jnp.minimum(g, jnp.maximum(sel[0] - 1, 0)), 0, 0)

    def whole(g, sel):
        return (0, 0)

    estimate = pl.CostEstimate(flops=int(2e9), bytes_accessed=int(8e6), transcendentals=0)
    light = pl.CostEstimate(flops=int(1e9), bytes_accessed=int(4e6), transcendentals=0)

    def slot_call(sel, erem, brem, lrem, total):
        return pl.pallas_call(
            lambda *refs: slot_kernel(*refs, scale=2.0 * sharpness * LOG2E / features),
            grid_spec=pltpu.PrefetchScalarGridSpec(
                num_scalar_prefetch=1,
                grid=(count_t,),
                in_specs=[
                    pl.BlockSpec((1, TILE, features), at_list),
                    pl.BlockSpec((TILE, features), whole),
                    pl.BlockSpec((1, TILE, 1), at_list),
                    pl.BlockSpec((1, TILE), whole),
                    pl.BlockSpec(block, at_list),
                    pl.BlockSpec((TILE, C), whole),
                    pl.BlockSpec(block, at_list),
                ],
                out_specs=[
                    pl.BlockSpec((1, TILE, TILE), at_place),
                    pl.BlockSpec((TILE, C), whole),
                    pl.BlockSpec(block, at_list),
                ],
            ),
            out_shape=[
                jax.ShapeDtypeStruct((count_t, TILE, TILE), jnp.bfloat16),
                jax.ShapeDtypeStruct((TILE, C), jnp.float32),
                jax.ShapeDtypeStruct((count_t, TILE, C), jnp.float32),
            ],
            input_output_aliases={7: 2},
            cost_estimate=estimate,
            name="slot",
        )(sel, tiles, erem, bias_column, brem, rounded, lrem, total)

    def push_call(sel, kernel, own):
        return pl.pallas_call(
            push_kernel,
            grid_spec=pltpu.PrefetchScalarGridSpec(
                num_scalar_prefetch=1,
                grid=(count_t,),
                in_specs=[pl.BlockSpec((1, TILE, TILE), at_place), pl.BlockSpec(block, at_list)],
                out_specs=pl.BlockSpec((TILE, C), whole),
            ),
            out_shape=jax.ShapeDtypeStruct((TILE, C), jnp.float32),
            cost_estimate=light,
            name="push",
        )(sel, kernel, own)

    def gather_call(sel, kernel, lrem, total):
        return pl.pallas_call(
            gather_kernel,
            grid_spec=pltpu.PrefetchScalarGridSpec(
                num_scalar_prefetch=1,
                grid=(count_t,),
                in_specs=[
                    pl.BlockSpec((1, TILE, TILE), at_place),
                    pl.BlockSpec((TILE, C), whole),
                    pl.BlockSpec(block, at_list),
                ],
                out_specs=pl.BlockSpec(block, at_list),
            ),
            out_shape=jax.ShapeDtypeStruct((count_t, TILE, C), jnp.float32),
            input_output_aliases={3: 0},
            cost_estimate=light,
            name="gather",
        )(sel, kernel, lrem, total)

    def add_push(total, arrived, slot):
        place = (mine[slot], 0, 0)
        old = lax.dynamic_slice(total, place, (1, TILE, C))
        return lax.dynamic_update_slice(total, old + arrived.astype(jnp.float32)[None], place)

    def slice_of(array, index):
        return lax.dynamic_index_in_dim(array, index, 0, keepdims=False)

    zeros = jnp.zeros((count_t, TILE, C), jnp.float32)
    degree = None

    gathered, returned = zeros, zeros
    received = []
    for k, s in enumerate(order):
        out = slice_of(tiles, mine[me ^ s])
        if k >= WINDOW:
            out, received[k - WINDOW] = lax.optimization_barrier((out, received[k - WINDOW]))
        received.append(swap(out, s))
    kernels, selections = {}, {}
    pushes = []
    for k, s in enumerate(order):
        peer = me ^ s
        sel = slice_of(selection, peer)
        remote_meta = slice_of(meta_in, peer)
        kernel, push, gathered = slot_call(
            sel, received[k], remote_meta[:1], slice_of(rounded_in, peer), gathered
        )
        kernels[s], selections[s] = kernel, sel
        pushes.append(swap(push.astype(jnp.float16), s))
    for k, s in enumerate(order):
        returned = add_push(returned, pushes[k], me ^ s)

    def update(labels, summed, degree):
        averaged = (labels + summed) / degree
        blended = mixing * averaged + (1.0 - mixing) * target
        squared = blended * blended
        return squared / jnp.sum(squared, axis=2, keepdims=True)

    summed = gathered + returned
    degree = 1.0 + jnp.sum(summed, axis=2, keepdims=True)
    labels = update(labels, summed, degree)

    for _ in range(1, ITERS):
        rounded = labels.astype(jnp.bfloat16)
        gathered, returned = zeros, zeros
        incoming, pushes = [], []
        for k, s in enumerate(order):
            out = slice_of(rounded, mine[me ^ s])
            push = push_call(selections[s], kernels[s], rounded).astype(jnp.float16)
            if k >= WINDOW:
                out, incoming[k - WINDOW] = lax.optimization_barrier((out, incoming[k - WINDOW]))
                push, pushes[k - WINDOW] = lax.optimization_barrier((push, pushes[k - WINDOW]))
            incoming.append(swap(out, s))
            pushes.append(swap(push, s))
        for k, s in enumerate(order):
            gathered = gather_call(selections[s], kernels[s], incoming[k], gathered)
            returned = add_push(returned, pushes[k], me ^ s)
        labels = update(labels, gathered + returned, degree)
    return labels.reshape(embed.shape[0], C)


def solution(mesh):
    in_specs = (
        P(("groups", "shard"), None),
        P(("groups", "shard")),
        P(("groups", "shard")),
        P(("groups", "shard"), None),
        P(("groups", "shard")),
        P(("groups", "shard")),
    )
    out_specs = P(("groups", "shard"), None)
    return jax.shard_map(body, mesh=mesh, in_specs=in_specs, out_specs=out_specs, check_vma=False)
```

time: 923 us -> 591 us (0.64)
  waiting for transfers between devices: 359 us -> 60.1 us
  matrix products: 255 us -> 0 us
  Pallas kernels: 0 us -> 249 us
  local copies, waits for them, and re-layouts: 223 us -> 25.2 us
  starting transfers between devices: 33.7 us -> 139 us
  other arithmetic: 19 us -> 79.1 us
  loops' own time: 30.1 us -> 0 us
  between operations: 0.29 us -> 29.3 us
    all_to_all x6 -> x1, waiting for transfers between devices: 359 us -> 10.2 us  [body(): lax.all_to_all(meta[mine], 'shard', split_axis=0, concat_axis=0, tiled=True)]
    dot_general x91 -> x0, matrix products: 255 us -> none  [the longest x16 80.3 us: label_step(): jnp.einsum('nq,nfd->qfd', local_onehot_labels, gathered_labels, precision...]
    pallas_call x0 -> x45, Pallas kernels: none -> 249 us  [the longest x15 106 us: slot_call(): pl.pallas_call(lambda *refs: slot_kernel(*refs, scale=2.0 * sharpness * L...]
    ppermute x0 -> x60, starting transfers between devices: none -> 134 us  [swap(): return lax.ppermute(value, 'shard', [(q, q ^ s) for q in range(n)])]
    gather x67 -> x1, local copies, waits for them, and re-layouts: 122 us -> 1.2 us  [body(): meta[mine]]
    while x130 -> x0, local copies, waits for them, and re-layouts: 63 us -> none
    ppermute x0 -> x60, waiting for transfers between devices: none -> 49.9 us  [swap(): return lax.ppermute(value, 'shard', [(q, q ^ s) for q in range(n)])]
    convert_element_type x10 -> x34, other arithmetic: 7.24 us -> 38.6 us  [the longest x15 18.4 us: body(): push = push_call(selections[s], kernels[s], rounded).astype(jnp.float16)]
  transfers between devices with their start and end apart: 6 -> 61, of which waited for: 4 -> 6; matrix products, arithmetic and copies ran while one was open for 31% -> 11% of each run, Pallas kernels for 0% -> 38%
where the time goes in v1:
time: 591 us; the launch traced here: 582 us
  Pallas kernels  249 us (42%)
  starting transfers between devices  139 us (24%)
  other arithmetic  79.1 us (13%)
  waiting for transfers between devices  60.1 us (10%)
  between operations  29.3 us (5%)
  local copies, waits for them, and re-layouts  25.2 us (4%)
    ppermute x60, starting transfers between devices, swap(): return lax.ppermute(value, 'shard', [(q, q ^ s) for q in range(n)])  134 us
    pallas_call x15, Pallas kernels, slot_call(): pl.pallas_call(lambda *refs: slot_kernel(*refs, scale=2.0 * sharpness * L...  106 us
    pallas_call x15, Pallas kernels, gather_call(): pl.pallas_call(gather_kernel, grid_spec=pltpu.PrefetchScalarGridSpec(num_...  74.6 us
    pallas_call x15, Pallas kernels, push_call(): pl.pallas_call(push_kernel, grid_spec=pltpu.PrefetchScalarGridSpec(num_sc...  68.7 us
    ppermute x60, waiting for transfers between devices, swap(): return lax.ppermute(value, 'shard', [(q, q ^ s) for q in range(n)])  49.9 us
    convert_element_type x15, other arithmetic, body(): push = push_call(selections[s], kernels[s], rounded).astype(jnp.float16)  18.4 us
    dynamic_update_slice x30, other arithmetic, add_push(): lax.dynamic_update_slice(total, old + arrived.astype(jnp.float32)[None],...  17.7 us
    div x1, other arithmetic, update(): return squared / jnp.sum(squared, axis=2, keepdims=True)  16.1 us
  transfers between devices with their start and end apart: 61, of which 6 were waited for; matrix products, arithmetic and copies ran while one was open for 11% of the time, Pallas kernels for 38%

profile of v1, /device:TPU:13, one launch (start us, length us, event | category | flops | bytes accessed | tf_op | source)
XLA Modules:
  0.0 582.3 jit_solution(10566903764711474484)
XLA Ops:
  30.3 5.4 dynamic-slice_bitcast_fusion
  39.8 4.8 all-to-all-start
  55.3 10.2 %all-to-all-done = f32[16,2,256]{2,1,0:T(2,128)S(1)} async-done(((f32[16,2,256]{2,1,0:T(2,128)}), f32[16,2,256]{2,1,0:T(2,128)S(1)}, u32[]{:S(2)}, u32[]{:S(2)}) %all-to-all-start) | async-done | bytes 32800 | tf_op jit(solution)/shard_map/all_to_all | solution.py:114
  70.5 6.7 %slot.15 = (bf16[8,256,256]{2,1,0:T(8,128)(2,1)}, f32[256,256]{1,0:T(8,128)}, f32[8,256,256]{2,1,0:T(8,128)}) custom-call(s32[9]{0:T(128)} %get-tuple-element.227.refs_0_.sel, bf16[8,256,768]{2,1,0:T(8,128)(2,1)} %bitcast.240, bf16[256,768]{1,0:T(8,128)(2,1)} %collective-permute-done.8.refs_2_, ...), custom_call_target="tpu_custom_call", output_to_operand_aliasing={{2}: (7, {})} | custom-call | flops 2000000000 | bytes 8000000 | tf_op jit(solution)/shard_map/slot/pallas_call | solution.py:143
  80.0 6.7 %slot.16 = (bf16[8,256,256]{2,1,0:T(8,128)(2,1)}, f32[256,256]{1,0:T(8,128)}, f32[8,256,256]{2,1,0:T(8,128)}) custom-call(s32[9]{0:T(128)} %get-tuple-element.231.refs_0_.sel, bf16[8,256,768]{2,1,0:T(8,128)(2,1)} %bitcast.241, bf16[256,768]{1,0:T(8,128)(2,1)} %collective-permute-done.4.refs_2_, ...), custom_call_target="tpu_custom_call", output_to_operand_aliasing={{2}: (7, {})} | custom-call | flops 2000000000 | bytes 8000000 | tf_op jit(solution)/shard_map/slot/pallas_call | solution.py:143
  87.7 5.6 collective-permute-start.16
  93.3 6.1 %slot.17 = (bf16[8,256,256]{2,1,0:T(8,128)(2,1)}, f32[256,256]{1,0:T(8,128)}, f32[8,256,256]{2,1,0:T(8,128)}) custom-call(s32[9]{0:T(128)} %get-tuple-element.235.refs_0_.sel, bf16[8,256,768]{2,1,0:T(8,128)(2,1)} %bitcast.242, bf16[256,768]{1,0:T(8,128)(2,1)} %collective-permute-done.refs_2_, ...), custom_call_target="tpu_custom_call", output_to_operand_aliasing={{2}: (7, {})} | custom-call | flops 2000000000 | bytes 8000000 | tf_op jit(solution)/shard_map/slot/pallas_call | solution.py:143
  100.5 4.4 slot.18
  105.9 7.6 %collective-permute-start.18 = (f16[256,256]{1,0:T(8,128)(2,1)S(1)}, f16[256,256]{1,0:T(8,128)(2,1)S(1)}, u32[]{:S(2)}, u32[]{:S(2)}) collective-permute-start(f16[256,256]{1,0:T(8,128)(2,1)S(1)} %convert_element_type.182), channel_id=1, source_target_pairs={{0,2},{1,3},{2,0},{3,1},{4,6},{5,7},{6,4},{7,5},{8,10},{9,11},{10,... | collective-permute-start | bytes 393224 | tf_op jit(solution)/shard_map/ppermute | solution.py:89
  114.2 3.6 collective-permute-start.5
  123.0 15.3 %collective-permute-done.9.refs_2_ = bf16[256,768]{1,0:T(8,128)(2,1)} collective-permute-done((bf16[256,768]{1,0:T(8,128)(2,1)}, bf16[256,768]{1,0:T(8,128)(2,1)}, u32[]{:S(2)}, u32[]{:S(2)}) %collective-permute-start.9) | collective-permute-done | bytes 393248 | tf_op jit(solution)/shard_map/ppermute | solution.py:89
  138.3 6.7 %slot.19 = (bf16[8,256,256]{2,1,0:T(8,128)(2,1)}, f32[256,256]{1,0:T(8,128)}, f32[8,256,256]{2,1,0:T(8,128)}) custom-call(s32[9]{0:T(128)} %get-tuple-element.241.refs_0_.sel, bf16[8,256,768]{2,1,0:T(8,128)(2,1)} %bitcast.244, bf16[256,768]{1,0:T(8,128)(2,1)} %collective-permute-done.9.refs_2_, ...), custom_call_target="tpu_custom_call", output_to_operand_aliasing={{2}: (7, {})} | custom-call | flops 2000000000 | bytes 8000000 | tf_op jit(solution)/shard_map/slot/pallas_call | solution.py:143
  147.7 6.1 %slot.20 = (bf16[8,256,256]{2,1,0:T(8,128)(2,1)}, f32[256,256]{1,0:T(8,128)}, f32[8,256,256]{2,1,0:T(8,128)}) custom-call(s32[9]{0:T(128)} %get-tuple-element.240.refs_0_.sel, bf16[8,256,768]{2,1,0:T(8,128)(2,1)} %bitcast.245, bf16[256,768]{1,0:T(8,128)(2,1)} %collective-permute-done.5.refs_2_, ...), custom_call_target="tpu_custom_call", output_to_operand_aliasing={{2}: (7, {})} | custom-call | flops 2000000000 | bytes 8000000 | tf_op jit(solution)/shard_map/slot/pallas_call | solution.py:143
  154.7 10.5 %collective-permute-start.20 = (f16[256,256]{1,0:T(8,128)(2,1)S(1)}, f16[256,256]{1,0:T(8,128)(2,1)}, u32[]{:S(2)}, u32[]{:S(2)}) collective-permute-start(f16[256,256]{1,0:T(8,128)(2,1)S(1)} %convert_element_type.184), channel_id=1, source_target_pairs={{0,3},{1,2},{2,1},{3,0},{4,7},{5,6},{6,5},{7,4},{8,11},{9,10},{10,... | collective-permute-start | bytes 393224 | tf_op jit(solution)/shard_map/ppermute | solution.py:89
  165.2 8.5 %slot.21 = (bf16[8,256,256]{2,1,0:T(8,128)(2,1)}, f32[256,256]{1,0:T(8,128)}, f32[8,256,256]{2,1,0:T(8,128)}) custom-call(s32[9]{0:T(128)} %get-tuple-element.238.refs_0_.sel, bf16[8,256,768]{2,1,0:T(8,128)(2,1)} %bitcast.246, bf16[256,768]{1,0:T(8,128)(2,1)} %collective-permute-done.1.refs_2_, ...), custom_call_target="tpu_custom_call", output_to_operand_aliasing={{2}: (7, {})} | custom-call | flops 2000000000 | bytes 8000000 | tf_op jit(solution)/shard_map/slot/pallas_call | solution.py:143
  175.3 5.0 slot.22
  181.3 5.8 %collective-permute-start.22 = (f16[256,256]{1,0:T(8,128)(2,1)S(1)}, f16[256,256]{1,0:T(8,128)(2,1)S(1)}, u32[]{:S(2)}, u32[]{:S(2)}) collective-permute-start(f16[256,256]{1,0:T(8,128)(2,1)S(1)} %convert_element_type.186), channel_id=1, source_target_pairs={{0,4},{1,5},{2,6},{3,7},{4,0},{5,1},{6,2},{7,3},{8,12},{9,13},{10,... | collective-permute-start | bytes 393224 | tf_op jit(solution)/shard_map/ppermute | solution.py:89
  195.1 11.5 %collective-permute-done.10.refs_2_ = bf16[256,768]{1,0:T(8,128)(2,1)} collective-permute-done((bf16[256,768]{1,0:T(8,128)(2,1)}, bf16[256,768]{1,0:T(8,128)(2,1)}, u32[]{:S(2)}, u32[]{:S(2)}) %collective-permute-start.10) | collective-permute-done | bytes 393248 | tf_op jit(solution)/shard_map/ppermute | solution.py:89
  206.7 9.5 %slot.23 = (bf16[8,256,256]{2,1,0:T(8,128)(2,1)}, f32[256,256]{1,0:T(8,128)}, f32[8,256,256]{2,1,0:T(8,128)}) custom-call(s32[9]{0:T(128)} %get-tuple-element.236.refs_0_.sel, bf16[8,256,768]{2,1,0:T(8,128)(2,1)} %bitcast.248, bf16[256,768]{1,0:T(8,128)(2,1)} %collective-permute-done.10.refs_2_, ...), custom_call_target="tpu_custom_call", output_to_operand_aliasing={{2}: (7, {})} | custom-call | flops 2000000000 | bytes 8000000 | tf_op jit(solution)/shard_map/slot/pallas_call | solution.py:143
  217.2 6.1 %slot.24 = (bf16[8,256,256]{2,1,0:T(8,128)(2,1)}, f32[256,256]{1,0:T(8,128)}, f32[8,256,256]{2,1,0:T(8,128)}) custom-call(s32[9]{0:T(128)} %get-tuple-element.234.refs_0_.sel, bf16[8,256,768]{2,1,0:T(8,128)(2,1)} %bitcast.249, bf16[256,768]{1,0:T(8,128)(2,1)} %collective-permute-done.6.refs_2_, ...), custom_call_target="tpu_custom_call", output_to_operand_aliasing={{2}: (7, {})} | custom-call | flops 2000000000 | bytes 8000000 | tf_op jit(solution)/shard_map/slot/pallas_call | solution.py:143
  224.3 8.5 %slot.25 = (bf16[8,256,256]{2,1,0:T(8,128)(2,1)}, f32[256,256]{1,0:T(8,128)}, f32[8,256,256]{2,1,0:T(8,128)}) custom-call(s32[9]{0:T(128)} %get-tuple-element.233.refs_0_.sel, bf16[8,256,768]{2,1,0:T(8,128)(2,1)} %bitcast.250, bf16[256,768]{1,0:T(8,128)(2,1)} %collective-permute-done.2.refs_2_, ...), custom_call_target="tpu_custom_call", output_to_operand_aliasing={{2}: (7, {})} | custom-call | flops 2000000000 | bytes 8000000 | tf_op jit(solution)/shard_map/slot/pallas_call | solution.py:143
  234.4 6.3 %slot.26 = (bf16[8,256,256]{2,1,0:T(8,128)(2,1)}, f32[256,256]{1,0:T(8,128)}, f32[8,256,256]{2,1,0:T(8,128)}) custom-call(s32[9]{0:T(128)} %get-tuple-element.232.refs_0_.sel, bf16[8,256,768]{2,1,0:T(8,128)(2,1)} %bitcast.251, bf16[256,768]{1,0:T(8,128)(2,1)} %collective-permute-done.14.refs_2_, ...), custom_call_target="tpu_custom_call", output_to_operand_aliasing={{2}: (7, {})} | custom-call | flops 2000000000 | bytes 8000000 | tf_op jit(solution)/shard_map/slot/pallas_call | solution.py:143
  241.7 7.6 %collective-permute-start.26 = (f16[256,256]{1,0:T(8,128)(2,1)S(1)}, f16[256,256]{1,0:T(8,128)(2,1)S(1)}, u32[]{:S(2)}, u32[]{:S(2)}) collective-permute-start(f16[256,256]{1,0:T(8,128)(2,1)S(1)} %convert_element_type.190), channel_id=1, source_target_pairs={{0,6},{1,7},{2,4},{3,5},{4,2},{5,3},{6,0},{7,1},{8,14},{9,15},{10,... | collective-permute-start | bytes 393224 | tf_op jit(solution)/shard_map/ppermute | solution.py:89
  256.9 14.4 %collective-permute-done.11.refs_2_ = bf16[256,768]{1,0:T(8,128)(2,1)S(1)} collective-permute-done((bf16[256,768]{1,0:T(8,128)(2,1)S(1)}, bf16[256,768]{1,0:T(8,128)(2,1)S(1)}, u32[]{:S(2)}, u32[]{:S(2)}) %collective-permute-start.11) | collective-permute-done | bytes 393248 | tf_op jit(solution)/shard_map/ppermute | solution.py:89
  272.0 10.2 %slot.27 = (bf16[8,256,256]{2,1,0:T(8,128)(2,1)}, f32[256,256]{1,0:T(8,128)}, f32[8,256,256]{2,1,0:T(8,128)}) custom-call(s32[9]{0:T(128)} %get-tuple-element.230.refs_0_.sel, bf16[8,256,768]{2,1,0:T(8,128)(2,1)} %bitcast.252, bf16[256,768]{1,0:T(8,128)(2,1)} %copy-done.4, f32[8,256,1]{2,1,0:T(8,128)} %mul.75.refs_3_, ...), custom_call_target="tpu_custom_call", output_to_operand_aliasing={{2}: (7, {})} | custom-call | flops 2000000000 | bytes 8000000 | tf_op jit(solution)/shard_map/slot/pallas_call | solution.py:143
  283.3 5.0 slot.28
  292.4 10.2 %slot.29 = (bf16[8,256,256]{2,1,0:T(8,128)(2,1)}, f32[256,256]{1,0:T(8,128)}, f32[8,256,256]{2,1,0:T(8,128)}) custom-call(s32[9]{0:T(128)} %get-tuple-element.228.refs_0_.sel, bf16[8,256,768]{2,1,0:T(8,128)(2,1)} %bitcast.254, bf16[256,768]{1,0:T(8,128)(2,1)} %collective-permute-done.3.refs_2_, ...), custom_call_target="tpu_custom_call", output_to_operand_aliasing={{2}: (7, {})} | custom-call | flops 2000000000 | bytes 8000000 | tf_op jit(solution)/shard_map/slot/pallas_call | solution.py:143
  303.7 9.7 %collective-permute-start.29 = (f16[256,256]{1,0:T(8,128)(2,1)S(1)}, f16[256,256]{1,0:T(8,128)(2,1)S(1)}, u32[]{:S(2)}, u32[]{:S(2)}) collective-permute-start(f16[256,256]{1,0:T(8,128)(2,1)S(1)} %convert_element_type.193), channel_id=1, source_target_pairs={{0,15},{1,14},{2,13},{3,12},{4,11},{5,10},{6,9},{7,8},{8,7},{9,6},... | collective-permute-start | bytes 393224 | tf_op jit(solution)/shard_map/ppermute | solution.py:89
  313.6 5.5 collective-permute-done.29
  324.5 6.6 %push.29 = f32[256,256]{1,0:T(8,128)} custom-call(s32[9]{0:T(128)} %get-tuple-element.228.refs_0_.sel, bf16[8,256,256]{2,1,0:T(8,128)(2,1)} %get-tuple-element.168.kref, bf16[8,256,256]{2,1,0:T(8,128)(2,1)} %fusion.3.lloc), custom_call_target="tpu_custom_call" | custom-call | flops 1000000000 | bytes 4000000 | tf_op jit(solution)/shard_map/push/pallas_call | solution.py:174
  332.0 5.4 push.25
  338.4 5.4 push.19
  345.5 4.0 push.20
  354.6 4.0 push.24
  359.7 4.0 push.17
  365.3 4.3 push.18
  370.6 10.5 %collective-permute-start.46 = (f16[256,256]{1,0:T(8,128)(2,1)S(1)}, f16[256,256]{1,0:T(8,128)(2,1)S(1)}, u32[]{:S(2)}, u32[]{:S(2)}) collective-permute-start(f16[256,256]{1,0:T(8,128)(2,1)S(1)} %convert_element_type.198), channel_id=1, source_target_pairs={{0,1},{1,0},{2,3},{3,2},{4,5},{5,4},{6,7},{7,6},{8,9},{9,8},{10,11... | collective-permute-start | bytes 393224 | tf_op jit(solution)/shard_map/ppermute | solution.py:89
  381.1 6.6 %push.27 = f32[256,256]{1,0:T(8,128)} custom-call(s32[9]{0:T(128)} %get-tuple-element.230.refs_0_.sel, bf16[8,256,256]{2,1,0:T(8,128)(2,1)} %get-tuple-element.176.kref, bf16[8,256,256]{2,1,0:T(8,128)(2,1)} %fusion.3.lloc), custom_call_target="tpu_custom_call" | custom-call | flops 1000000000 | bytes 4000000 | tf_op jit(solution)/shard_map/push/pallas_call | solution.py:174
  388.6 6.3 %push.23 = f32[256,256]{1,0:T(8,128)} custom-call(s32[9]{0:T(128)} %get-tuple-element.236.refs_0_.sel, bf16[8,256,256]{2,1,0:T(8,128)(2,1)} %get-tuple-element.187.kref, bf16[8,256,256]{2,1,0:T(8,128)(2,1)} %fusion.3.lloc), custom_call_target="tpu_custom_call" | custom-call | flops 1000000000 | bytes 4000000 | tf_op jit(solution)/shard_map/push/pallas_call | solution.py:174
  396.5 4.3 push.15
  402.4 4.3 push.16
  407.8 4.0 push.26
  436.3 4.8 gather.21.gin
  441.1 5.0 collective-permute-start.49
  446.2 4.8 gather.22.gin
  451.0 4.3 gather.23.gin
  458.3 6.1 %collective-permute-start.35 = (bf16[256,256]{1,0:T(8,128)(2,1)}, bf16[256,256]{1,0:T(8,128)(2,1)}, u32[]{:S(2)}, u32[]{:S(2)}) collective-permute-start(bf16[256,256]{1,0:T(8,128)(2,1)} %get-tuple-element.173), channel_id=1, source_target_pairs={{0,3},{1,2},{2,1},{3,0},{4,7},{5,6},{6,5},{7,4},{8,11},{9,10},{10,... | collective-permute-start | bytes 393224 | tf_op jit(solution)/shard_map/ppermute | solution.py:89
  471.0 3.6 collective-permute-start.54
  474.6 4.8 gather.25.gin
  479.5 4.3 gather.26.gin
  483.8 3.8 collective-permute-start.56
  487.6 6.1 %gather.27.gin = f32[8,256,256]{2,1,0:T(8,128)} custom-call(s32[9]{0:T(128)} %get-tuple-element.238.refs_0_.sel, bf16[8,256,256]{2,1,0:T(8,128)(2,1)} %get-tuple-element.191.kref, bf16[256,256]{1,0:T(8,128)(2,1)} %collective-permute-done.31.lrem, f32[8,256,256]{2,1,0:T(8,128)} %gather.26.gin), custom_call_target="tpu_custom_call", output_to_operand_aliasing={{}: (3, {})} | custom-call | flops 1000000000 | bytes 4000000 | tf_op jit(solution)/shard_map/gather/pallas_call | solution.py:188
  495.4 3.3 gather.28.gin
  498.7 4.7 collective-permute-start.36
  510.8 6.7 %gather.29.gin = f32[8,256,256]{2,1,0:T(8,128)} custom-call(s32[9]{0:T(128)} %get-tuple-element.236.refs_0_.sel, bf16[8,256,256]{2,1,0:T(8,128)(2,1)} %get-tuple-element.187.kref, bf16[256,256]{1,0:T(8,128)(2,1)} %collective-permute-done.40.lrem, f32[8,256,256]{2,1,0:T(8,128)} %gather.28.gin), custom_call_target="tpu_custom_call", output_to_operand_aliasing={{}: (3, {})} | custom-call | flops 1000000000 | bytes 4000000 | tf_op jit(solution)/shard_map/gather/pallas_call | solution.py:188
  518.3 4.3 gather.30.gin
  522.6 5.2 collective-permute-start.41
  527.7 6.0 %gather.31.gin = f32[8,256,256]{2,1,0:T(8,128)} custom-call(s32[9]{0:T(128)} %get-tuple-element.233.refs_0_.sel, bf16[8,256,256]{2,1,0:T(8,128)(2,1)} %get-tuple-element.183.kref, bf16[256,256]{1,0:T(8,128)(2,1)} %copy-done.6, f32[8,256,256]{2,1,0:T(8,128)} %gather.30.gin), custom_call_target="tpu_custom_call", output_to_operand_aliasing={{}: (3, {})} | custom-call | flops 1000000000 | bytes 4000000 | tf_op jit(solution)/shard_map/gather/pallas_call | solution.py:188
  534.4 4.3 gather.32.gin
  538.7 5.6 collective-permute-start.33
  546.9 7.3 %gather.33.gin = f32[8,256,256]{2,1,0:T(8,128)} custom-call(s32[9]{0:T(128)} %get-tuple-element.230.refs_0_.sel, bf16[8,256,256]{2,1,0:T(8,128)(2,1)} %get-tuple-element.176.kref, bf16[256,256]{1,0:T(8,128)(2,1)} %copy-done.8, f32[8,256,256]{2,1,0:T(8,128)} %gather.32.gin), custom_call_target="tpu_custom_call", output_to_operand_aliasing={{}: (3, {})} | custom-call | flops 1000000000 | bytes 4000000 | tf_op jit(solution)/shard_map/gather/pallas_call | solution.py:188
  554.9 3.3 gather.34.gin
  558.9 7.3 %gather.35 = f32[8,256,256]{2,1,0:T(8,128)} custom-call(s32[9]{0:T(128)} %get-tuple-element.228.refs_0_.sel, bf16[8,256,256]{2,1,0:T(8,128)(2,1)} %get-tuple-element.168.kref, bf16[256,256]{1,0:T(8,128)(2,1)} %copy-done.10, f32[8,256,256]{2,1,0:T(8,128)} %gather.34.gin), custom_call_target="tpu_custom_call", output_to_operand_aliasing={{}: (3, {})} | custom-call | flops 1000000000 | bytes 4000000 | tf_op jit(solution)/shard_map/gather/pallas_call | solution.py:188
  566.2 16.1 %fusion.2 = f32[8,256,256]{2,1,0:T(8,128)} fusion(f32[8,256,256]{2,1,0:T(8,128)} %gather.35, f32[8,256,256]{2,1,0:T(8,128)S(1)} %fusion.4, f32[8,256]{1,0:T(8,128)S(1)} %copy-done.21, f32[8,256]{1,0:T(8,128)S(1)} %convert_element_type.170, pred[8,256]{1,0:T(8,128)(4,1)S(1)} %copy-done.26, pred[8,256]{1,0:T(8,128)(4,1)S(1)} %copy-done.24, ...), kind=kOutput, calls=%fused_computation.11 | output fusion | flops 6818047 | bytes 8417280 | tf_op jit(solution)/shard_map/div | solution.py:242
  (269 shorter events, 137.8 us)
Async XLA Ops:
  35.7 13.6 %copy-start.29 = (s32[64]{0:T(128)S(1)}, s32[64]{0:T(128)}, u32[]{:S(2)}) copy-start(s32[64]{0:T(128)} %param.11) | copy-start | bytes 772
  35.7 13.6 %copy-start.30 = (s32[64]{0:T(128)S(1)}, s32[64]{0:T(128)}, u32[]{:S(2)}) copy-start(s32[64]{0:T(128)} %param.10) | copy-start | bytes 772
  35.7 33.3 %collective-permute-start.8 = (bf16[256,768]{1,0:T(8,128)(2,1)}, bf16[256,768]{1,0:T(8,128)(2,1)}, u32[]{:S(2)}, u32[]{:S(2)}) collective-permute-start(bf16[256,768]{1,0:T(8,128)(2,1)} %get-tuple-element.249), channel_id=1, source_target_pairs={{0,8},{1,9},{2,10},{3,11},{4,12},{5,13},{6,14},{7,15},{8,0},{9,1},... | collective-permute-start | bytes 1179656 | tf_op jit(solution)/shard_map/ppermute | solution.py:89
  39.8 25.7 %all-to-all-start = ((f32[16,2,256]{2,1,0:T(2,128)}), f32[16,2,256]{2,1,0:T(2,128)S(1)}, u32[]{:S(2)}, u32[]{:S(2)}) async-start(f32[16,2,256]{2,1,0:T(2,128)} %gather_fusion), calls=%async_computation | async-start | bytes 65536 | tf_op jit(solution)/shard_map/all_to_all | solution.py:114
  44.7 35.3 %collective-permute-start.4 = (bf16[256,768]{1,0:T(8,128)(2,1)}, bf16[256,768]{1,0:T(8,128)(2,1)}, u32[]{:S(2)}, u32[]{:S(2)}) collective-permute-start(bf16[256,768]{1,0:T(8,128)(2,1)} %get-tuple-element.253), channel_id=1, source_target_pairs={{0,1},{1,0},{2,3},{3,2},{4,5},{5,4},{6,7},{7,6},{8,9},{9,8},{10,11... | collective-permute-start | bytes 1179656 | tf_op jit(solution)/shard_map/ppermute | solution.py:89
  45.0 48.3 %collective-permute-start = (bf16[256,768]{1,0:T(8,128)(2,1)}, bf16[256,768]{1,0:T(8,128)(2,1)}, u32[]{:S(2)}, u32[]{:S(2)}) collective-permute-start(bf16[256,768]{1,0:T(8,128)(2,1)} %get-tuple-element.257), channel_id=1, source_target_pairs={{0,9},{1,8},{2,11},{3,10},{4,13},{5,12},{6,15},{7,14},{8,1},{9,0},... | collective-permute-start | bytes 1179656 | tf_op jit(solution)/shard_map/ppermute | solution.py:89
  47.2 53.3 %collective-permute-start.12 = (bf16[256,768]{1,0:T(8,128)(2,1)}, bf16[256,768]{1,0:T(8,128)(2,1)}, u32[]{:S(2)}, u32[]{:S(2)}) collective-permute-start(bf16[256,768]{1,0:T(8,128)(2,1)} %get-tuple-element.246), channel_id=1, source_target_pairs={{0,2},{1,3},{2,0},{3,1},{4,6},{5,7},{6,4},{7,5},{8,10},{9,11},{10,... | collective-permute-start | bytes 1179656 | tf_op jit(solution)/shard_map/ppermute | solution.py:89
  78.2 35.3 %collective-permute-start.15 = (f16[256,256]{1,0:T(8,128)(2,1)S(1)}, f16[256,256]{1,0:T(8,128)(2,1)S(1)}, u32[]{:S(2)}, u32[]{:S(2)}) collective-permute-start(f16[256,256]{1,0:T(8,128)(2,1)S(1)} %convert_element_type.179), channel_id=1, source_target_pairs={{0,8},{1,9},{2,10},{3,11},{4,12},{5,13},{6,14},{7,15},{8,0},{9,1},... | collective-permute-start | bytes 393224 | tf_op jit(solution)/shard_map/ppermute | solution.py:89
  87.7 31.0 %collective-permute-start.16 = (f16[256,256]{1,0:T(8,128)(2,1)S(1)}, f16[256,256]{1,0:T(8,128)(2,1)}, u32[]{:S(2)}, u32[]{:S(2)}) collective-permute-start(f16[256,256]{1,0:T(8,128)(2,1)S(1)} %convert_element_type.180), channel_id=1, source_target_pairs={{0,1},{1,0},{2,3},{3,2},{4,5},{5,4},{6,7},{7,6},{8,9},{9,8},{10,11... | collective-permute-start | bytes 393224 | tf_op jit(solution)/shard_map/ppermute | solution.py:89
  100.4 19.4 %collective-permute-start.17 = (f16[256,256]{1,0:T(8,128)(2,1)S(1)}, f16[256,256]{1,0:T(8,128)(2,1)}, u32[]{:S(2)}, u32[]{:S(2)}) collective-permute-start(f16[256,256]{1,0:T(8,128)(2,1)S(1)} %convert_element_type.181), channel_id=1, source_target_pairs={{0,9},{1,8},{2,11},{3,10},{4,13},{5,12},{6,15},{7,14},{8,1},{9,0},... | collective-permute-start | bytes 393224 | tf_op jit(solution)/shard_map/ppermute | solution.py:89
  105.9 17.1 %collective-permute-start.18 = (f16[256,256]{1,0:T(8,128)(2,1)S(1)}, f16[256,256]{1,0:T(8,128)(2,1)S(1)}, u32[]{:S(2)}, u32[]{:S(2)}) collective-permute-start(f16[256,256]{1,0:T(8,128)(2,1)S(1)} %convert_element_type.182), channel_id=1, source_target_pairs={{0,2},{1,3},{2,0},{3,1},{4,6},{5,7},{6,4},{7,5},{8,10},{9,11},{10,... | collective-permute-start | bytes 393224 | tf_op jit(solution)/shard_map/ppermute | solution.py:89
  113.5 24.7 %collective-permute-start.9 = (bf16[256,768]{1,0:T(8,128)(2,1)}, bf16[256,768]{1,0:T(8,128)(2,1)}, u32[]{:S(2)}, u32[]{:S(2)}) collective-permute-start(bf16[256,768]{1,0:T(8,128)(2,1)} %get-tuple-element.122), channel_id=1, source_target_pairs={{0,10},{1,11},{2,8},{3,9},{4,14},{5,15},{6,12},{7,13},{8,2},{9,3},... | collective-permute-start | bytes 1179656 | tf_op jit(solution)/shard_map/ppermute | solution.py:89
  114.2 33.5 %collective-permute-start.5 = (bf16[256,768]{1,0:T(8,128)(2,1)}, bf16[256,768]{1,0:T(8,128)(2,1)}, u32[]{:S(2)}, u32[]{:S(2)}) collective-permute-start(bf16[256,768]{1,0:T(8,128)(2,1)} %get-tuple-element.119), channel_id=1, source_target_pairs={{0,3},{1,2},{2,1},{3,0},{4,7},{5,6},{6,5},{7,4},{8,11},{9,10},{10,... | collective-permute-start | bytes 1179656 | tf_op jit(solution)/shard_map/ppermute | solution.py:89
  118.7 46.5 %collective-permute-start.1 = (bf16[256,768]{1,0:T(8,128)(2,1)}, bf16[256,768]{1,0:T(8,128)(2,1)}, u32[]{:S(2)}, u32[]{:S(2)}) collective-permute-start(bf16[256,768]{1,0:T(8,128)(2,1)} %get-tuple-element.116), channel_id=1, source_target_pairs={{0,11},{1,10},{2,9},{3,8},{4,15},{5,14},{6,13},{7,12},{8,3},{9,2},... | collective-permute-start | bytes 1179656 | tf_op jit(solution)/shard_map/ppermute | solution.py:89
  119.8 55.5 %collective-permute-start.13 = (bf16[256,768]{1,0:T(8,128)(2,1)}, bf16[256,768]{1,0:T(8,128)(2,1)}, u32[]{:S(2)}, u32[]{:S(2)}) collective-permute-start(bf16[256,768]{1,0:T(8,128)(2,1)} %get-tuple-element.125), channel_id=1, source_target_pairs={{0,4},{1,5},{2,6},{3,7},{4,0},{5,1},{6,2},{7,3},{8,12},{9,13},{10,... | collective-permute-start | bytes 1179656 | tf_op jit(solution)/shard_map/ppermute | solution.py:89
  146.0 41.2 %collective-permute-start.19 = (f16[256,256]{1,0:T(8,128)(2,1)S(1)}, f16[256,256]{1,0:T(8,128)(2,1)}, u32[]{:S(2)}, u32[]{:S(2)}) collective-permute-start(f16[256,256]{1,0:T(8,128)(2,1)S(1)} %convert_element_type.183), channel_id=1, source_target_pairs={{0,10},{1,11},{2,8},{3,9},{4,14},{5,15},{6,12},{7,13},{8,2},{9,3},... | collective-permute-start | bytes 393224 | tf_op jit(solution)/shard_map/ppermute | solution.py:89
  154.7 33.4 %collective-permute-start.20 = (f16[256,256]{1,0:T(8,128)(2,1)S(1)}, f16[256,256]{1,0:T(8,128)(2,1)}, u32[]{:S(2)}, u32[]{:S(2)}) collective-permute-start(f16[256,256]{1,0:T(8,128)(2,1)S(1)} %convert_element_type.184), channel_id=1, source_target_pairs={{0,3},{1,2},{2,1},{3,0},{4,7},{5,6},{6,5},{7,4},{8,11},{9,10},{10,... | collective-permute-start | bytes 393224 | tf_op jit(solution)/shard_map/ppermute | solution.py:89
  175.3 16.5 %collective-permute-start.21 = (f16[256,256]{1,0:T(8,128)(2,1)}, f16[256,256]{1,0:T(8,128)(2,1)}, u32[]{:S(2)}, u32[]{:S(2)}) collective-permute-start(f16[256,256]{1,0:T(8,128)(2,1)} %convert_element_type.185), channel_id=1, source_target_pairs={{0,11},{1,10},{2,9},{3,8},{4,15},{5,14},{6,13},{7,12},{8,3},{9,2},... | collective-permute-start | bytes 393224 | tf_op jit(solution)/shard_map/ppermute | solution.py:89
  181.3 13.7 %collective-permute-start.22 = (f16[256,256]{1,0:T(8,128)(2,1)S(1)}, f16[256,256]{1,0:T(8,128)(2,1)S(1)}, u32[]{:S(2)}, u32[]{:S(2)}) collective-permute-start(f16[256,256]{1,0:T(8,128)(2,1)S(1)} %convert_element_type.186), channel_id=1, source_target_pairs={{0,4},{1,5},{2,6},{3,7},{4,0},{5,1},{6,2},{7,3},{8,12},{9,13},{10,... | collective-permute-start | bytes 393224 | tf_op jit(solution)/shard_map/ppermute | solution.py:89
  187.1 19.5 %collective-permute-start.10 = (bf16[256,768]{1,0:T(8,128)(2,1)}, bf16[256,768]{1,0:T(8,128)(2,1)}, u32[]{:S(2)}, u32[]{:S(2)}) collective-permute-start(bf16[256,768]{1,0:T(8,128)(2,1)} %get-tuple-element.123), channel_id=1, source_target_pairs={{0,12},{1,13},{2,14},{3,15},{4,8},{5,9},{6,10},{7,11},{8,4},{9,5},... | collective-permute-start | bytes 1179656 | tf_op jit(solution)/shard_map/ppermute | solution.py:89
  187.2 30.0 %collective-permute-start.6 = (bf16[256,768]{1,0:T(8,128)(2,1)}, bf16[256,768]{1,0:T(8,128)(2,1)}, u32[]{:S(2)}, u32[]{:S(2)}) collective-permute-start(bf16[256,768]{1,0:T(8,128)(2,1)} %get-tuple-element.120), channel_id=1, source_target_pairs={{0,5},{1,4},{2,7},{3,6},{4,1},{5,0},{6,3},{7,2},{8,13},{9,12},{10,... | collective-permute-start | bytes 1179656 | tf_op jit(solution)/shard_map/ppermute | solution.py:89
  188.1 36.2 %collective-permute-start.2 = (bf16[256,768]{1,0:T(8,128)(2,1)}, bf16[256,768]{1,0:T(8,128)(2,1)}, u32[]{:S(2)}, u32[]{:S(2)}) collective-permute-start(bf16[256,768]{1,0:T(8,128)(2,1)} %get-tuple-element.117), channel_id=1, source_target_pairs={{0,13},{1,12},{2,15},{3,14},{4,9},{5,8},{6,11},{7,10},{8,5},{9,4},... | collective-permute-start | bytes 1179656 | tf_op jit(solution)/shard_map/ppermute | solution.py:89
  191.9 42.6 %collective-permute-start.14 = (bf16[256,768]{1,0:T(8,128)(2,1)}, bf16[256,768]{1,0:T(8,128)(2,1)}, u32[]{:S(2)}, u32[]{:S(2)}) collective-permute-start(bf16[256,768]{1,0:T(8,128)(2,1)} %get-tuple-element.126), channel_id=1, source_target_pairs={{0,6},{1,7},{2,4},{3,5},{4,2},{5,3},{6,0},{7,1},{8,14},{9,15},{10,... | collective-permute-start | bytes 1179656 | tf_op jit(solution)/shard_map/ppermute | solution.py:89
  217.1 32.2 %collective-permute-start.23 = (f16[256,256]{1,0:T(8,128)(2,1)S(1)}, f16[256,256]{1,0:T(8,128)(2,1)}, u32[]{:S(2)}, u32[]{:S(2)}) collective-permute-start(f16[256,256]{1,0:T(8,128)(2,1)S(1)} %convert_element_type.187), channel_id=1, source_target_pairs={{0,12},{1,13},{2,14},{3,15},{4,8},{5,9},{6,10},{7,11},{8,4},{9,5},... | collective-permute-start | bytes 393224 | tf_op jit(solution)/shard_map/ppermute | solution.py:89
  224.3 27.8 %collective-permute-start.24 = (f16[256,256]{1,0:T(8,128)(2,1)S(1)}, f16[256,256]{1,0:T(8,128)(2,1)}, u32[]{:S(2)}, u32[]{:S(2)}) collective-permute-start(f16[256,256]{1,0:T(8,128)(2,1)S(1)} %convert_element_type.188), channel_id=1, source_target_pairs={{0,5},{1,4},{2,7},{3,6},{4,1},{5,0},{6,3},{7,2},{8,13},{9,12},{10,... | collective-permute-start | bytes 393224 | tf_op jit(solution)/shard_map/ppermute | solution.py:89
  234.4 21.4 %collective-permute-start.25 = (f16[256,256]{1,0:T(8,128)(2,1)}, f16[256,256]{1,0:T(8,128)(2,1)}, u32[]{:S(2)}, u32[]{:S(2)}) collective-permute-start(f16[256,256]{1,0:T(8,128)(2,1)} %convert_element_type.189), channel_id=1, source_target_pairs={{0,13},{1,12},{2,15},{3,14},{4,9},{5,8},{6,11},{7,10},{8,5},{9,4},... | collective-permute-start | bytes 393224 | tf_op jit(solution)/shard_map/ppermute | solution.py:89
  241.7 15.2 %collective-permute-start.26 = (f16[256,256]{1,0:T(8,128)(2,1)S(1)}, f16[256,256]{1,0:T(8,128)(2,1)S(1)}, u32[]{:S(2)}, u32[]{:S(2)}) collective-permute-start(f16[256,256]{1,0:T(8,128)(2,1)S(1)} %convert_element_type.190), channel_id=1, source_target_pairs={{0,6},{1,7},{2,4},{3,5},{4,2},{5,3},{6,0},{7,1},{8,14},{9,15},{10,... | collective-permute-start | bytes 393224 | tf_op jit(solution)/shard_map/ppermute | solution.py:89
  249.3 22.0 %collective-permute-start.11 = (bf16[256,768]{1,0:T(8,128)(2,1)S(1)}, bf16[256,768]{1,0:T(8,128)(2,1)S(1)}, u32[]{:S(2)}, u32[]{:S(2)}) collective-permute-start(bf16[256,768]{1,0:T(8,128)(2,1)S(1)} %get-tuple-element.124), channel_id=1, source_target_pairs={{0,14},{1,15},{2,12},{3,13},{4,10},{5,11},{6,8},{7,9},{8,6},{9,7},... | collective-permute-start | bytes 1179656 | tf_op jit(solution)/shard_map/ppermute | solution.py:89
  249.3 34.0 %collective-permute-start.7 = (bf16[256,768]{1,0:T(8,128)(2,1)S(1)}, bf16[256,768]{1,0:T(8,128)(2,1)}, u32[]{:S(2)}, u32[]{:S(2)}) collective-permute-start(bf16[256,768]{1,0:T(8,128)(2,1)S(1)} %get-tuple-element.121), channel_id=1, source_target_pairs={{0,7},{1,6},{2,5},{3,4},{4,3},{5,2},{6,1},{7,0},{8,15},{9,14},{10,... | collective-permute-start | bytes 1179656 | tf_op jit(solution)/shard_map/ppermute | solution.py:89
  252.1 40.3 %collective-permute-start.3 = (bf16[256,768]{1,0:T(8,128)(2,1)S(1)}, bf16[256,768]{1,0:T(8,128)(2,1)}, u32[]{:S(2)}, u32[]{:S(2)}) collective-permute-start(bf16[256,768]{1,0:T(8,128)(2,1)S(1)} %get-tuple-element.118), channel_id=1, source_target_pairs={{0,15},{1,14},{2,13},{3,12},{4,11},{5,10},{6,9},{7,8},{8,7},{9,6},... | collective-permute-start | bytes 1179656 | tf_op jit(solution)/shard_map/ppermute | solution.py:89
  283.2 30.3 %collective-permute-start.27 = (f16[256,256]{1,0:T(8,128)(2,1)S(1)}, f16[256,256]{1,0:T(8,128)(2,1)S(1)}, u32[]{:S(2)}, u32[]{:S(2)}) collective-permute-start(f16[256,256]{1,0:T(8,128)(2,1)S(1)} %convert_element_type.191), channel_id=1, source_target_pairs={{0,14},{1,15},{2,12},{3,13},{4,10},{5,11},{6,8},{7,9},{8,6},{9,7},... | collective-permute-start | bytes 393224 | tf_op jit(solution)/shard_map/ppermute | solution.py:89
  289.3 24.3 %collective-permute-start.28 = (f16[256,256]{1,0:T(8,128)(2,1)S(1)}, f16[256,256]{1,0:T(8,128)(2,1)S(1)}, u32[]{:S(2)}, u32[]{:S(2)}) collective-permute-start(f16[256,256]{1,0:T(8,128)(2,1)S(1)} %convert_element_type.192), channel_id=1, source_target_pairs={{0,7},{1,6},{2,5},{3,4},{4,3},{5,2},{6,1},{7,0},{8,15},{9,14},{10,... | collective-permute-start | bytes 393224 | tf_op jit(solution)/shard_map/ppermute | solution.py:89
  302.6 16.6 %copy-start.1 = (f32[8,256,256]{2,1,0:T(8,128)S(1)}, f32[8,256,256]{2,1,0:T(8,128)}, u32[]{:S(2)}) copy-start(f32[8,256,256]{2,1,0:T(8,128)} %get-tuple-element.152) | copy-start | bytes 6291460
  303.7 15.4 %collective-permute-start.29 = (f16[256,256]{1,0:T(8,128)(2,1)S(1)}, f16[256,256]{1,0:T(8,128)(2,1)S(1)}, u32[]{:S(2)}, u32[]{:S(2)}) collective-permute-start(f16[256,256]{1,0:T(8,128)(2,1)S(1)} %convert_element_type.193), channel_id=1, source_target_pairs={{0,15},{1,14},{2,13},{3,12},{4,11},{5,10},{6,9},{7,8},{8,7},{9,6},... | collective-permute-start | bytes 393224 | tf_op jit(solution)/shard_map/ppermute | solution.py:89
  350.5 75.5 %collective-permute-start.47 = (f16[256,256]{1,0:T(8,128)(2,1)S(1)}, f16[256,256]{1,0:T(8,128)(2,1)S(1)}, u32[]{:S(2)}, u32[]{:S(2)}) collective-permute-start(f16[256,256]{1,0:T(8,128)(2,1)S(1)} %convert_element_type.200), channel_id=1, source_target_pairs={{0,9},{1,8},{2,11},{3,10},{4,13},{5,12},{6,15},{7,14},{8,1},{9,0},... | collective-permute-start | bytes 393224 | tf_op jit(solution)/shard_map/ppermute | solution.py:89
  370.6 56.8 %collective-permute-start.46 = (f16[256,256]{1,0:T(8,128)(2,1)S(1)}, f16[256,256]{1,0:T(8,128)(2,1)S(1)}, u32[]{:S(2)}, u32[]{:S(2)}) collective-permute-start(f16[256,256]{1,0:T(8,128)(2,1)S(1)} %convert_element_type.198), channel_id=1, source_target_pairs={{0,1},{1,0},{2,3},{3,2},{4,5},{5,4},{6,7},{7,6},{8,9},{9,8},{10,11... | collective-permute-start | bytes 393224 | tf_op jit(solution)/shard_map/ppermute | solution.py:89
  407.7 19.7 %collective-permute-start.45 = (f16[256,256]{1,0:T(8,128)(2,1)S(1)}, f16[256,256]{1,0:T(8,128)(2,1)S(1)}, u32[]{:S(2)}, u32[]{:S(2)}) collective-permute-start(f16[256,256]{1,0:T(8,128)(2,1)S(1)} %convert_element_type.196), channel_id=1, source_target_pairs={{0,8},{1,9},{2,10},{3,11},{4,12},{5,13},{6,14},{7,15},{8,0},{9,1},... | collective-permute-start | bytes 393224 | tf_op jit(solution)/shard_map/ppermute | solution.py:89
  422.2 7.0 %collective-permute-start.48 = (f16[256,256]{1,0:T(8,128)(2,1)S(1)}, f16[256,256]{1,0:T(8,128)(2,1)S(1)}, u32[]{:S(2)}, u32[]{:S(2)}) collective-permute-start(f16[256,256]{1,0:T(8,128)(2,1)S(1)} %convert_element_type.202), channel_id=1, source_target_pairs={{0,2},{1,3},{2,0},{3,1},{4,6},{5,7},{6,4},{7,5},{8,10},{9,11},{10,... | collective-permute-start | bytes 393224 | tf_op jit(solution)/shard_map/ppermute | solution.py:89
  423.3 9.9 %collective-permute-start.38 = (bf16[256,256]{1,0:T(8,128)(2,1)S(1)}, bf16[256,256]{1,0:T(8,128)(2,1)S(1)}, u32[]{:S(2)}, u32[]{:S(2)}) collective-permute-start(bf16[256,256]{1,0:T(8,128)(2,1)S(1)} %get-tuple-element.279), channel_id=1, source_target_pairs={{0,8},{1,9},{2,10},{3,11},{4,12},{5,13},{6,14},{7,15},{8,0},{9,1},... | collective-permute-start | bytes 393224 | tf_op jit(solution)/shard_map/ppermute | solution.py:89
  425.9 15.2 %collective-permute-start.34 = (bf16[256,256]{1,0:T(8,128)(2,1)}, bf16[256,256]{1,0:T(8,128)(2,1)}, u32[]{:S(2)}, u32[]{:S(2)}) collective-permute-start(bf16[256,256]{1,0:T(8,128)(2,1)} %get-tuple-element.283), channel_id=1, source_target_pairs={{0,1},{1,0},{2,3},{3,2},{4,5},{5,4},{6,7},{7,6},{8,9},{9,8},{10,11... | collective-permute-start | bytes 393224 | tf_op jit(solution)/shard_map/ppermute | solution.py:89
  427.4 23.6 %collective-permute-start.30 = (bf16[256,256]{1,0:T(8,128)(2,1)}, bf16[256,256]{1,0:T(8,128)(2,1)}, u32[]{:S(2)}, u32[]{:S(2)}) collective-permute-start(bf16[256,256]{1,0:T(8,128)(2,1)} %get-tuple-element.287), channel_id=1, source_target_pairs={{0,9},{1,8},{2,11},{3,10},{4,13},{5,12},{6,15},{7,14},{8,1},{9,0},... | collective-permute-start | bytes 393224 | tf_op jit(solution)/shard_map/ppermute | solution.py:89
  427.4 27.8 %collective-permute-start.42 = (bf16[256,256]{1,0:T(8,128)(2,1)}, bf16[256,256]{1,0:T(8,128)(2,1)}, u32[]{:S(2)}, u32[]{:S(2)}) collective-permute-start(bf16[256,256]{1,0:T(8,128)(2,1)} %get-tuple-element.276), channel_id=1, source_target_pairs={{0,2},{1,3},{2,0},{3,1},{4,6},{5,7},{6,4},{7,5},{8,10},{9,11},{10,... | collective-permute-start | bytes 393224 | tf_op jit(solution)/shard_map/ppermute | solution.py:89
  429.2 29.1 %collective-permute-start.51 = (f16[256,256]{1,0:T(8,128)(2,1)}, f16[256,256]{1,0:T(8,128)(2,1)}, u32[]{:S(2)}, u32[]{:S(2)}) collective-permute-start(f16[256,256]{1,0:T(8,128)(2,1)} %convert_element_type.199), channel_id=1, source_target_pairs={{0,11},{1,10},{2,9},{3,8},{4,15},{5,14},{6,13},{7,12},{8,3},{9,2},... | collective-permute-start | bytes 393224 | tf_op jit(solution)/shard_map/ppermute | solution.py:89
  433.9 30.5 %collective-permute-start.50 = (f16[256,256]{1,0:T(8,128)(2,1)}, f16[256,256]{1,0:T(8,128)(2,1)}, u32[]{:S(2)}, u32[]{:S(2)}) collective-permute-start(f16[256,256]{1,0:T(8,128)(2,1)} %convert_element_type.197), channel_id=1, source_target_pairs={{0,3},{1,2},{2,1},{3,0},{4,7},{5,6},{6,5},{7,4},{8,11},{9,10},{10,... | collective-permute-start | bytes 393224 | tf_op jit(solution)/shard_map/ppermute | solution.py:89
  441.1 23.4 %collective-permute-start.49 = (f16[256,256]{1,0:T(8,128)(2,1)}, f16[256,256]{1,0:T(8,128)(2,1)}, u32[]{:S(2)}, u32[]{:S(2)}) collective-permute-start(f16[256,256]{1,0:T(8,128)(2,1)} %convert_element_type.195), channel_id=1, source_target_pairs={{0,10},{1,11},{2,8},{3,9},{4,14},{5,15},{6,12},{7,13},{8,2},{9,3},... | collective-permute-start | bytes 393224 | tf_op jit(solution)/shard_map/ppermute | solution.py:89
  451.0 16.2 %collective-permute-start.52 = (f16[256,256]{1,0:T(8,128)(2,1)}, f16[256,256]{1,0:T(8,128)(2,1)}, u32[]{:S(2)}, u32[]{:S(2)}) collective-permute-start(f16[256,256]{1,0:T(8,128)(2,1)} %convert_element_type.201), channel_id=1, source_target_pairs={{0,4},{1,5},{2,6},{3,7},{4,0},{5,1},{6,2},{7,3},{8,12},{9,13},{10,... | collective-permute-start | bytes 393224 | tf_op jit(solution)/shard_map/ppermute | solution.py:89
  455.3 15.7 %collective-permute-start.39 = (bf16[256,256]{1,0:T(8,128)(2,1)}, bf16[256,256]{1,0:T(8,128)(2,1)}, u32[]{:S(2)}, u32[]{:S(2)}) collective-permute-start(bf16[256,256]{1,0:T(8,128)(2,1)} %get-tuple-element.177), channel_id=1, source_target_pairs={{0,10},{1,11},{2,8},{3,9},{4,14},{5,15},{6,12},{7,13},{8,2},{9,3},... | collective-permute-start | bytes 393224 | tf_op jit(solution)/shard_map/ppermute | solution.py:89
  458.3 21.1 %collective-permute-start.35 = (bf16[256,256]{1,0:T(8,128)(2,1)}, bf16[256,256]{1,0:T(8,128)(2,1)}, u32[]{:S(2)}, u32[]{:S(2)}) collective-permute-start(bf16[256,256]{1,0:T(8,128)(2,1)} %get-tuple-element.173), channel_id=1, source_target_pairs={{0,3},{1,2},{2,1},{3,0},{4,7},{5,6},{6,5},{7,4},{8,11},{9,10},{10,... | collective-permute-start | bytes 393224 | tf_op jit(solution)/shard_map/ppermute | solution.py:89
  464.4 19.3 %collective-permute-start.31 = (bf16[256,256]{1,0:T(8,128)(2,1)}, bf16[256,256]{1,0:T(8,128)(2,1)}, u32[]{:S(2)}, u32[]{:S(2)}) collective-permute-start(bf16[256,256]{1,0:T(8,128)(2,1)} %get-tuple-element.169), channel_id=1, source_target_pairs={{0,11},{1,10},{2,9},{3,8},{4,15},{5,14},{6,13},{7,12},{8,3},{9,2},... | collective-permute-start | bytes 393224 | tf_op jit(solution)/shard_map/ppermute | solution.py:89
  464.5 29.1 %collective-permute-start.43 = (bf16[256,256]{1,0:T(8,128)(2,1)}, bf16[256,256]{1,0:T(8,128)(2,1)}, u32[]{:S(2)}, u32[]{:S(2)}) collective-permute-start(bf16[256,256]{1,0:T(8,128)(2,1)} %get-tuple-element.181), channel_id=1, source_target_pairs={{0,4},{1,5},{2,6},{3,7},{4,0},{5,1},{6,2},{7,3},{8,12},{9,13},{10,... | collective-permute-start | bytes 393224 | tf_op jit(solution)/shard_map/ppermute | solution.py:89
  467.2 31.6 %collective-permute-start.55 = (f16[256,256]{1,0:T(8,128)(2,1)S(1)}, f16[256,256]{1,0:T(8,128)(2,1)}, u32[]{:S(2)}, u32[]{:S(2)}) collective-permute-start(f16[256,256]{1,0:T(8,128)(2,1)S(1)} %convert_element_type.205), channel_id=1, source_target_pairs={{0,13},{1,12},{2,15},{3,14},{4,9},{5,8},{6,11},{7,10},{8,5},{9,4},... | collective-permute-start | bytes 393224 | tf_op jit(solution)/shard_map/ppermute | solution.py:89
  471.0 32.5 %collective-permute-start.54 = (f16[256,256]{1,0:T(8,128)(2,1)S(1)}, f16[256,256]{1,0:T(8,128)(2,1)}, u32[]{:S(2)}, u32[]{:S(2)}) collective-permute-start(f16[256,256]{1,0:T(8,128)(2,1)S(1)} %convert_element_type.204), channel_id=1, source_target_pairs={{0,5},{1,4},{2,7},{3,6},{4,1},{5,0},{6,3},{7,2},{8,13},{9,12},{10,... | collective-permute-start | bytes 393224 | tf_op jit(solution)/shard_map/ppermute | solution.py:89
  479.5 24.0 %collective-permute-start.53 = (f16[256,256]{1,0:T(8,128)(2,1)}, f16[256,256]{1,0:T(8,128)(2,1)}, u32[]{:S(2)}, u32[]{:S(2)}) collective-permute-start(f16[256,256]{1,0:T(8,128)(2,1)} %convert_element_type.203), channel_id=1, source_target_pairs={{0,12},{1,13},{2,14},{3,15},{4,8},{5,9},{6,10},{7,11},{8,4},{9,5},... | collective-permute-start | bytes 393224 | tf_op jit(solution)/shard_map/ppermute | solution.py:89
  483.8 22.7 %collective-permute-start.56 = (f16[256,256]{1,0:T(8,128)(2,1)}, f16[256,256]{1,0:T(8,128)(2,1)}, u32[]{:S(2)}, u32[]{:S(2)}) collective-permute-start(f16[256,256]{1,0:T(8,128)(2,1)} %convert_element_type.206), channel_id=1, source_target_pairs={{0,6},{1,7},{2,4},{3,5},{4,2},{5,3},{6,0},{7,1},{8,14},{9,15},{10,... | collective-permute-start | bytes 393224 | tf_op jit(solution)/shard_map/ppermute | solution.py:89
  493.6 17.1 %collective-permute-start.40 = (bf16[256,256]{1,0:T(8,128)(2,1)}, bf16[256,256]{1,0:T(8,128)(2,1)}, u32[]{:S(2)}, u32[]{:S(2)}) collective-permute-start(bf16[256,256]{1,0:T(8,128)(2,1)} %get-tuple-element.178), channel_id=1, source_target_pairs={{0,12},{1,13},{2,14},{3,15},{4,8},{5,9},{6,10},{7,11},{8,4},{9,5},... | collective-permute-start | bytes 393224 | tf_op jit(solution)/shard_map/ppermute | solution.py:89
  498.7 18.8 %collective-permute-start.36 = (bf16[256,256]{1,0:T(8,128)(2,1)S(1)}, bf16[256,256]{1,0:T(8,128)(2,1)}, u32[]{:S(2)}, u32[]{:S(2)}) collective-permute-start(bf16[256,256]{1,0:T(8,128)(2,1)S(1)} %get-tuple-element.174), channel_id=1, source_target_pairs={{0,5},{1,4},{2,7},{3,6},{4,1},{5,0},{6,3},{7,2},{8,13},{9,12},{10,... | collective-permute-start | bytes 393224 | tf_op jit(solution)/shard_map/ppermute | solution.py:89
  503.5 19.1 %collective-permute-start.32 = (bf16[256,256]{1,0:T(8,128)(2,1)S(1)}, bf16[256,256]{1,0:T(8,128)(2,1)S(1)}, u32[]{:S(2)}, u32[]{:S(2)}) collective-permute-start(bf16[256,256]{1,0:T(8,128)(2,1)S(1)} %get-tuple-element.170), channel_id=1, source_target_pairs={{0,13},{1,12},{2,15},{3,14},{4,9},{5,8},{6,11},{7,10},{8,5},{9,4},... | collective-permute-start | bytes 393224 | tf_op jit(solution)/shard_map/ppermute | solution.py:89
  503.5 30.3 %collective-permute-start.44 = (bf16[256,256]{1,0:T(8,128)(2,1)S(1)}, bf16[256,256]{1,0:T(8,128)(2,1)S(1)}, u32[]{:S(2)}, u32[]{:S(2)}) collective-permute-start(bf16[256,256]{1,0:T(8,128)(2,1)S(1)} %get-tuple-element.182), channel_id=1, source_target_pairs={{0,6},{1,7},{2,4},{3,5},{4,2},{5,3},{6,0},{7,1},{8,14},{9,15},{10,... | collective-permute-start | bytes 393224 | tf_op jit(solution)/shard_map/ppermute | solution.py:89
  506.5 32.2 %collective-permute-start.57 = (f16[256,256]{1,0:T(8,128)(2,1)S(1)}, f16[256,256]{1,0:T(8,128)(2,1)}, u32[]{:S(2)}, u32[]{:S(2)}) collective-permute-start(f16[256,256]{1,0:T(8,128)(2,1)S(1)} %convert_element_type.207), channel_id=1, source_target_pairs={{0,14},{1,15},{2,12},{3,13},{4,10},{5,11},{6,8},{7,9},{8,6},{9,7},... | collective-permute-start | bytes 393224 | tf_op jit(solution)/shard_map/ppermute | solution.py:89
  510.7 34.5 %collective-permute-start.58 = (f16[256,256]{1,0:T(8,128)(2,1)S(1)}, f16[256,256]{1,0:T(8,128)(2,1)}, u32[]{:S(2)}, u32[]{:S(2)}) collective-permute-start(f16[256,256]{1,0:T(8,128)(2,1)S(1)} %convert_element_type.208), channel_id=1, source_target_pairs={{0,7},{1,6},{2,5},{3,4},{4,3},{5,2},{6,1},{7,0},{8,15},{9,14},{10,... | collective-permute-start | bytes 393224 | tf_op jit(solution)/shard_map/ppermute | solution.py:89
  517.5 28.6 %collective-permute-start.59 = (f16[256,256]{1,0:T(8,128)(2,1)S(1)}, f16[256,256]{1,0:T(8,128)(2,1)S(1)}, u32[]{:S(2)}, u32[]{:S(2)}) collective-permute-start(f16[256,256]{1,0:T(8,128)(2,1)S(1)} %convert_element_type.209), channel_id=1, source_target_pairs={{0,15},{1,14},{2,13},{3,12},{4,11},{5,10},{6,9},{7,8},{8,7},{9,6},... | collective-permute-start | bytes 393224 | tf_op jit(solution)/shard_map/ppermute | solution.py:89
  522.6 23.7 %collective-permute-start.41 = (bf16[256,256]{1,0:T(8,128)(2,1)S(1)}, bf16[256,256]{1,0:T(8,128)(2,1)S(1)}, u32[]{:S(2)}, u32[]{:S(2)}) collective-permute-start(bf16[256,256]{1,0:T(8,128)(2,1)S(1)} %get-tuple-element.179), channel_id=1, source_target_pairs={{0,14},{1,15},{2,12},{3,13},{4,10},{5,11},{6,8},{7,9},{8,6},{9,7},... | collective-permute-start | bytes 393224 | tf_op jit(solution)/shard_map/ppermute | solution.py:89
  533.8 20.4 %collective-permute-start.37 = (bf16[256,256]{1,0:T(8,128)(2,1)S(1)}, bf16[256,256]{1,0:T(8,128)(2,1)S(1)}, u32[]{:S(2)}, u32[]{:S(2)}) collective-permute-start(bf16[256,256]{1,0:T(8,128)(2,1)S(1)} %get-tuple-element.175), channel_id=1, source_target_pairs={{0,7},{1,6},{2,5},{3,4},{4,3},{5,2},{6,1},{7,0},{8,15},{9,14},{10,... | collective-permute-start | bytes 393224 | tf_op jit(solution)/shard_map/ppermute | solution.py:89
  538.7 19.5 %collective-permute-start.33 = (bf16[256,256]{1,0:T(8,128)(2,1)S(1)}, bf16[256,256]{1,0:T(8,128)(2,1)S(1)}, u32[]{:S(2)}, u32[]{:S(2)}) collective-permute-start(bf16[256,256]{1,0:T(8,128)(2,1)S(1)} %get-tuple-element.171), channel_id=1, source_target_pairs={{0,15},{1,14},{2,13},{3,12},{4,11},{5,10},{6,9},{7,8},{8,7},{9,6},... | collective-permute-start | bytes 393224 | tf_op jit(solution)/shard_map/ppermute | solution.py:89
  (28 other events, 70.9 us)

commit v2 on v1

v2 whole, which is shorter than its diff:
```python
import math

import jax
import jax.numpy as jnp
from jax import lax
from jax.experimental import pallas as pl
from jax.experimental.pallas import tpu as pltpu
from jax.sharding import PartitionSpec as P

C = 256
TILE = 256
ITERS = 2
WINDOW = 4

sharpness = 1.0
mixing = 0.8

LOG2E = math.log2(math.e)
ANY = pl.BlockSpec(memory_space=pl.ANY)

PEER, MINE, COUNT, START, LIST = 0, 1, 2, 3, 4


def take_kernel(table, src, *rest, slots):
    outs, sem = rest[:-1], rest[-1]
    copies = [
        pltpu.make_async_copy(src.at[table[s, MINE]], out, sem.at[k])
        for k, (s, out) in enumerate(zip(slots, outs))
    ]
    for copy in copies:
        copy.start()
    for copy in copies:
        copy.wait()


def spread_kernel(mine, src, out, sem):
    copies = [
        pltpu.make_async_copy(src.at[mine[k]], out.at[k], sem.at[k]) for k in range(out.shape[0])
    ]
    for copy in copies:
        copy.start()
    for copy in copies:
        copy.wait()


def slot_kernel(table, eloc, erem, bloc, meta, lloc, *rest, slot, scale):
    kout, pout = rest[-2:]
    step = pl.program_id(0)

    @pl.when(step == 0)
    def _():
        pout[...] = jnp.zeros_like(pout)

    @pl.when(step < table[slot, COUNT])
    def _():
        inner = lax.dot_general(
            eloc[0], erem[...], (((1,), (1,)), ((), ())), preferred_element_type=jnp.float32
        )
        k = jnp.exp2(inner * scale + (bloc[0] + meta[0, :1])).astype(jnp.bfloat16)
        kout[0] = k
        pout[0] += lax.dot_general(
            k, lloc[0], (((0,), (0,)), ((), ())), preferred_element_type=jnp.float32
        )


def push_kernel(pairs, kref, lloc, unused, pout):
    step = pl.program_id(0)

    @pl.when((step == 0) | (pairs[0, step] != pairs[0, jnp.maximum(step - 1, 0)]))
    def _():
        pout[...] = jnp.zeros_like(pout)

    pout[0] += lax.dot_general(
        kref[0], lloc[pairs[1, step]], (((0,), (0,)), ((), ())), preferred_element_type=jnp.float32
    )


def gather_kernel(pairs, kref, lrem, gout):
    step = pl.program_id(0)

    @pl.when(step == 0)
    def _():
        gout[...] = jnp.zeros_like(gout)

    gout[pairs[1, step]] += jnp.dot(kref[0], lrem[0], preferred_element_type=jnp.float32)


def update_kernel(mine, gathered, back, old, target, *rest, first):
    if first:
        degree, out, rounded, total = rest
    else:
        degree, out, total = rest
    tile = pl.program_id(0)
    total[...] = gathered[0]
    for k in range(back.shape[0]):

        @pl.when(mine[k] == tile)
        def _():
            total[...] += back[k]

    summed = total[...]
    if first:
        degree[0] = 1.0 + jnp.sum(summed, axis=1, keepdims=True)
    averaged = (old[0] + summed) / degree[0]
    blended = mixing * averaged + (1.0 - mixing) * target[0]
    squared = blended * blended
    labels = squared / jnp.sum(squared, axis=1, keepdims=True)
    out[0] = labels
    if first:
        rounded[0] = labels.astype(jnp.bfloat16)


def body(embed, seed_mask, seed_class, partner, pair_local, pair_peer):
    n = lax.axis_size("shard")
    me = lax.axis_index("shard")
    features = embed.shape[1]
    tiles = embed.reshape(-1, TILE, features)
    tile_count = tiles.shape[0]
    pair_count = pair_local.shape[0]
    mine = partner.reshape(-1)
    half = n // 2
    order = []
    for k in range(half):
        order.append(half + k)
        if k + 1 < half:
            order.append(k + 1)

    tile_ids = jnp.arange(tile_count, dtype=jnp.int32)
    slot_ids = jnp.arange(n, dtype=jnp.int32)
    peers = slot_ids ^ me
    pair_slot = pair_peer ^ me
    mine_x = jnp.sum(jnp.where(peers[:, None] == slot_ids[None, :], mine[None, :], 0), axis=1)
    sends = jnp.stack([peers, mine_x], axis=1)
    active = jnp.any(
        (pair_slot[None, None, :] == slot_ids[:, None, None])
        & (pair_local[None, None, :] == tile_ids[None, :, None]),
        axis=2,
    )
    counts = jnp.sum(active.astype(jnp.int32), axis=1)
    starts = jnp.sum((pair_slot[None, :] < slot_ids[:, None]).astype(jnp.int32), axis=1)
    place = jnp.sum(
        (active[:, None, :] & (tile_ids[None, None, :] < tile_ids[None, :, None])).astype(jnp.int32), axis=2
    )
    wanted = jnp.minimum(tile_ids[None, :], jnp.maximum(counts - 1, 0)[:, None])
    listed = jnp.sum(
        jnp.where(active[:, None, :] & (place[:, None, :] == wanted[:, :, None]), tile_ids[None, None, :], 0),
        axis=2,
    )
    table = jnp.concatenate([sends, counts[:, None], starts[:, None], listed], axis=1).astype(jnp.int32)
    key = pair_slot * tile_count + pair_local
    rank = jnp.sum((key[None, :] < key[:, None]).astype(jnp.int32), axis=1)
    chosen = rank[None, :] == jnp.arange(pair_count, dtype=jnp.int32)[:, None]
    pairs = jnp.stack(
        [
            jnp.sum(jnp.where(chosen, pair_peer[None, :], 0), axis=1),
            jnp.sum(jnp.where(chosen, pair_local[None, :], 0), axis=1),
        ]
    ).astype(jnp.int32)

    def take(slots):
        return pl.pallas_call(
            lambda *refs: take_kernel(*refs, slots=slots),
            grid_spec=pltpu.PrefetchScalarGridSpec(
                num_scalar_prefetch=1,
                grid=(1,),
                in_specs=[ANY],
                out_specs=[ANY] * len(slots),
                scratch_shapes=[pltpu.SemaphoreType.DMA((len(slots),))],
            ),
            out_shape=[jax.ShapeDtypeStruct((TILE, features), embed.dtype)] * len(slots),
            name="take",
        )(sends, tiles)

    outgoing = dict(zip(order[:3], take(order[:3])))
    outgoing.update(zip(order[3:], take(order[3:])))
    received = []
    for k, s in enumerate(order):
        out = outgoing[s]
        if k >= WINDOW:
            out, received[k - WINDOW] = lax.optimization_barrier((out, received[k - WINDOW]))
        received.append(lax.ppermute(out, "shard", [(q, q ^ s) for q in range(n)]))

    norms = jnp.sum(jnp.square(tiles.astype(jnp.float32)), axis=2)
    bias = (1.0 - norms * (1.0 / features)) * (sharpness * LOG2E)
    seeded = seed_mask == 1
    classes = jnp.where(seeded, seed_class, -1).reshape(tile_count, TILE).astype(jnp.float32)
    meta = jnp.stack([bias, classes], axis=1)
    meta_in = lax.all_to_all(meta[mine], "shard", split_axis=0, concat_axis=0, tiled=True)
    class_ids = jnp.arange(C, dtype=jnp.float32)

    def first_labels(ids):
        return jnp.where(ids[..., None] < 0, 1.0 / C, (ids[..., None] == class_ids).astype(jnp.float32))

    labels = first_labels(classes)
    target = jnp.where(seeded.reshape(tile_count, TILE)[..., None], labels, 0.0)
    rounded = labels.astype(jnp.bfloat16)
    rounded_in = first_labels(meta_in[:, 1]).astype(jnp.bfloat16)
    bias_column = bias[:, :, None]

    block = (1, TILE, C)
    square = (1, TILE, TILE)
    sums = jax.ShapeDtypeStruct((n, TILE, C), jnp.float32)
    tile_sums = jax.ShapeDtypeStruct((tile_count, TILE, C), jnp.float32)

    def slot_call(slot, erem, kernels, pushes):
        def listed_tile(g, t):
            return (t[slot, LIST + g], 0, 0)

        def kernel_place(g, t):
            last = jnp.maximum(t[slot, COUNT] - 1, 0)
            here = t[slot, START] + jnp.minimum(g, last)
            return (jnp.where(t[slot, COUNT] > 0, here, pair_count), 0, 0)

        def peer(g, t):
            return (t[slot, PEER], 0, 0)

        begun = [] if kernels is None else [kernels, pushes]
        return pl.pallas_call(
            lambda *refs: slot_kernel(*refs, slot=slot, scale=2.0 * sharpness * LOG2E / features),
            grid_spec=pltpu.PrefetchScalarGridSpec(
                num_scalar_prefetch=1,
                grid=(tile_count,),
                in_specs=[
                    pl.BlockSpec((1, TILE, features), listed_tile),
                    pl.BlockSpec((TILE, features), lambda g, t: (0, 0)),
                    pl.BlockSpec((1, TILE, 1), listed_tile),
                    pl.BlockSpec((1, 2, TILE), peer),
                    pl.BlockSpec(block, listed_tile),
                ]
                + [ANY] * len(begun),
                out_specs=[pl.BlockSpec(square, kernel_place), pl.BlockSpec(block, peer)],
            ),
            out_shape=[jax.ShapeDtypeStruct((pair_count + 1, TILE, TILE), jnp.bfloat16), sums],
            input_output_aliases={6: 0, 7: 1} if begun else {},
            cost_estimate=pl.CostEstimate(flops=int(2e9), bytes_accessed=int(8e6), transcendentals=0),
            name="slot",
        )(table, tiles, erem, bias_column, meta_in, rounded, *begun)

    def push_call(kernels, own):
        return pl.pallas_call(
            push_kernel,
            grid_spec=pltpu.PrefetchScalarGridSpec(
                num_scalar_prefetch=1,
                grid=(pair_count,),
                in_specs=[
                    pl.BlockSpec(square, lambda g, p: (g, 0, 0)),
                    pl.BlockSpec(own.shape, lambda g, p: (0, 0, 0)),
                    ANY,
                ],
                out_specs=pl.BlockSpec(block, lambda g, p: (p[0, g], 0, 0)),
            ),
            out_shape=sums,
            input_output_aliases={3: 0},
            cost_estimate=pl.CostEstimate(flops=int(2e10), bytes_accessed=int(6e7), transcendentals=0),
            name="push",
        )(pairs, kernels, own, jnp.zeros(sums.shape, sums.dtype))

    def gather_call(kernels, incoming):
        return pl.pallas_call(
            gather_kernel,
            grid_spec=pltpu.PrefetchScalarGridSpec(
                num_scalar_prefetch=1,
                grid=(pair_count,),
                in_specs=[
                    pl.BlockSpec(square, lambda g, p: (g, 0, 0)),
                    pl.BlockSpec(block, lambda g, p: (p[0, g], 0, 0)),
                ],
                out_specs=pl.BlockSpec(tile_sums.shape, lambda g, p: (0, 0, 0)),
            ),
            out_shape=tile_sums,
            cost_estimate=pl.CostEstimate(flops=int(2e10), bytes_accessed=int(6e7), transcendentals=0),
            name="gather",
        )(pairs, kernels, incoming)

    def update_call(gathered, back, old, degree):
        first = degree is None
        by_tile = pl.BlockSpec(block, lambda g, m: (g, 0, 0))
        column = pl.BlockSpec((1, TILE, 1), lambda g, m: (g, 0, 0))
        column_shape = jax.ShapeDtypeStruct((tile_count, TILE, 1), jnp.float32)
        return pl.pallas_call(
            lambda *refs: update_kernel(*refs, first=first),
            grid_spec=pltpu.PrefetchScalarGridSpec(
                num_scalar_prefetch=1,
                grid=(tile_count,),
                in_specs=[by_tile, pl.BlockSpec(back.shape, lambda g, m: (0, 0, 0)), by_tile, by_tile]
                + ([] if first else [column]),
                out_specs=[column, by_tile, by_tile] if first else by_tile,
                scratch_shapes=[pltpu.VMEM((TILE, C), jnp.float32)],
            ),
            out_shape=[column_shape, tile_sums, jax.ShapeDtypeStruct(tile_sums.shape, jnp.bfloat16)]
            if first
            else tile_sums,
            name="update",
        )(owners, gathered, back, old, target, *([] if first else [degree]))

    def spread(array):
        return pl.pallas_call(
            spread_kernel,
            grid_spec=pltpu.PrefetchScalarGridSpec(
                num_scalar_prefetch=1,
                grid=(1,),
                in_specs=[ANY],
                out_specs=ANY,
                scratch_shapes=[pltpu.SemaphoreType.DMA((n,))],
            ),
            out_shape=jax.ShapeDtypeStruct((n,) + array.shape[1:], array.dtype),
            name="spread",
        )(mine, array)

    def exchange(array):
        return lax.all_to_all(array, "shard", split_axis=0, concat_axis=0, tiled=True)

    owners = jnp.where(slot_ids == me, -1, mine)
    kernels = pushes = None
    for k, s in enumerate(order):
        kernels, pushes = slot_call(s, received[k], kernels, pushes)
    back = exchange(pushes.astype(jnp.float16)).astype(jnp.float32)
    gathered = gather_call(kernels, rounded_in)
    degree, labels, rounded = update_call(gathered, back, labels, None)
    for _ in range(1, ITERS):
        incoming = exchange(spread(rounded))
        pushes = push_call(kernels, rounded)
        back = exchange(pushes.astype(jnp.float16)).astype(jnp.float32)
        gathered = gather_call(kernels, incoming)
        labels = update_call(gathered, back, labels, degree)
    return labels.reshape(embed.shape[0], C)


def solution(mesh):
    in_specs = (
        P(("groups", "shard"), None),
        P(("groups", "shard")),
        P(("groups", "shard")),
        P(("groups", "shard"), None),
        P(("groups", "shard")),
        P(("groups", "shard")),
    )
    out_specs = P(("groups", "shard"), None)
    return jax.shard_map(body, mesh=mesh, in_specs=in_specs, out_specs=out_specs, check_vma=False)
```

time: 591 us -> 630 us (1.066)
  Pallas kernels: 249 us -> 485 us
  starting transfers between devices: 139 us -> 43.5 us
  other arithmetic: 79.1 us -> 22.8 us
  between operations: 29.3 us -> 0.33 us
  local copies, waits for them, and re-layouts: 25.2 us -> 10.4 us
    pallas_call x15 -> x20, Pallas kernels: 106 us -> 367 us  [the longest x2 183 us: take(): pl.pallas_call(lambda *refs: take_kernel(*refs, slots=slots), grid_spec=p...]
    ppermute x60 -> x15, starting transfers between devices: 134 us -> 22 us  [body(): received.append(lax.ppermute(out, 'shard', [(q, q ^ s) for q in range(n)]))]
    all_to_all x0 -> x3, waiting for transfers between devices: none -> 49.5 us  [exchange(): lax.all_to_all(array, 'shard', split_axis=0, concat_axis=0, tiled=True)]
    ppermute x60 -> x15, waiting for transfers between devices: 49.9 us -> 12.6 us  [body(): received.append(lax.ppermute(out, 'shard', [(q, q ^ s) for q in range(n)]))]
    pallas_call x15 -> x1, Pallas kernels: 68.7 us -> 40.8 us  [push_call(): pl.pallas_call(push_kernel, grid_spec=pltpu.PrefetchScalarGridSpec(num_sc...]
    convert_element_type x33 -> x5, other arithmetic: 37.2 us -> 12.5 us  [the longest x4 12.5 us: body(): back = exchange(pushes.astype(jnp.float16)).astype(jnp.float32)]
    dynamic_update_slice x30 -> x0, other arithmetic: 17.7 us -> none  [add_push(): lax.dynamic_update_slice(total, old + arrived.astype(jnp.float32)[None],...]
    all_to_all x0 -> x3, starting transfers between devices: none -> 16.7 us  [exchange(): lax.all_to_all(array, 'shard', split_axis=0, concat_axis=0, tiled=True)]
  transfers between devices with their start and end apart: 61 -> 19, of which waited for: 6 -> 6; matrix products, arithmetic and copies ran while one was open for 11% -> 2% of each run, Pallas kernels for 38% -> 54%
where the time goes in v2:
time: 630 us; the launch traced here: 624 us
  Pallas kernels  485 us (77%)
  waiting for transfers between devices  62.1 us (10%)
  starting transfers between devices  43.5 us (7%)
  other arithmetic  22.8 us (4%)
  local copies, waits for them, and re-layouts  10.4 us (2%)
    pallas_call x2, Pallas kernels, take(): pl.pallas_call(lambda *refs: take_kernel(*refs, slots=slots), grid_spec=p...  183 us
    pallas_call x15, Pallas kernels, slot_call(): pl.pallas_call(lambda *refs: slot_kernel(*refs, slot=slot, scale=2.0 * sh...  97.7 us
    pallas_call x2, Pallas kernels, gather_call(): pl.pallas_call(gather_kernel, grid_spec=pltpu.PrefetchScalarGridSpec(num_...  77.6 us
    pallas_call x1, Pallas kernels, spread(): pl.pallas_call(spread_kernel, grid_spec=pltpu.PrefetchScalarGridSpec(num_...  65.4 us
    all_to_all x3, waiting for transfers between devices, exchange(): lax.all_to_all(array, 'shard', split_axis=0, concat_axis=0, tiled=True)  49.5 us
    pallas_call x1, Pallas kernels, push_call(): pl.pallas_call(push_kernel, grid_spec=pltpu.PrefetchScalarGridSpec(num_sc...  40.8 us
    ppermute x15, starting transfers between devices, body(): received.append(lax.ppermute(out, 'shard', [(q, q ^ s) for q in range(n)]))  22 us
    pallas_call x2, Pallas kernels, update_call(): pl.pallas_call(lambda *refs: update_kernel(*refs, first=first), grid_spec...  20.8 us
  transfers between devices with their start and end apart: 19, of which 6 were waited for; matrix products, arithmetic and copies ran while one was open for 2% of the time, Pallas kernels for 54%

profile of v2, /device:TPU:13, one launch (start us, length us, event | category | flops | bytes accessed | tf_op | source)
XLA Modules:
  0.0 624.1 jit_solution(5551665834422284421)
XLA Ops:
  0.0 1.0 select_reduce_fusion.3
  1.1 0.7 pad_add_fusion.refs_0_
  1.8 37.7 %take.3 = (bf16[256,768]{1,0:T(8,128)(2,1)}, bf16[256,768]{1,0:T(8,128)(2,1)}, bf16[256,768]{1,0:T(8,128)(2,1)}) custom-call(s32[16,2]{1,0:T(8,128)} %pad_add_fusion.refs_0_, bf16[8,256,768]{2,1,0:T(8,128)(2,1)} %bitcast.20), custom_call_target="tpu_custom_call" | custom-call | tf_op jit(solution)/shard_map/take/pallas_call | solution.py:161
  39.5 2.4 collective-permute-start.8
  41.9 0.7 multiply_reduce_fusion
  42.7 1.2 gather_fusion
  43.9 4.8 all-to-all-start
  48.7 0.4 collective-permute-start.4
  49.0 2.1 collective-permute-start
  51.2 144.9 %take.2 = (bf16[256,768]{1,0:T(8,128)(2,1)}, bf16[256,768]{1,0:T(8,128)(2,1)}, bf16[256,768]{1,0:T(8,128)(2,1)}, bf16[256,768]{1,0:T(8,128)(2,1)}, bf16[256,768]...) custom-call(s32[16,2]{1,0:T(8,128)} %pad_add_fusion.refs_0_, ...), custom_call_target="tpu_custom_call" | custom-call | tf_op jit(solution)/shard_map/take/pallas_call | solution.py:161
  196.5 1.9 mul.62.refs_3_
  198.4 0.4 and_reduce_fusion
  199.2 3.1 fusion
  202.5 0.7 concatenate.4.refs_0_
  203.2 3.5 collective-permute-done.12.refs_2_
  207.0 2.5 collective-permute-start.5
  209.5 1.8 collective-permute-start.1
  211.6 0.6 copy-done.1
  212.2 7.2 %slot.15 = (bf16[65,256,256]{2,1,0:T(8,128)(2,1)}, f32[16,256,256]{2,1,0:T(8,128)}) custom-call(s32[16,12]{1,0:T(8,128)} %concatenate.4.refs_0_, bf16[8,256,768]{2,1,0:T(8,128)(2,1)} %bitcast.22, bf16[256,768]{1,0:T(8,128)(2,1)} %collective-permute-done.8.refs_2_, f32[8,256,1]{2,1,0:T(8,128)} %mul.62.refs_3_, f32[16,2,256]{2,1,0:T(2,128)} %copy-done.1, ...), custom_call_target="tpu_custom_call" | custom-call | flops 2000000000 | bytes 8000000 | tf_op jit(solution)/shard_map/slot/pallas_call | solution.py:218
  219.4 4.7 slot.16
  224.1 4.7 slot.17
  228.9 5.7 slot.18
  234.5 2.0 collective-permute-done.5.refs_2_
  236.5 4.9 collective-permute-done.1.refs_2_
  241.7 5.5 collective-permute-start.6
  247.2 0.7 collective-permute-start.2
  247.9 0.6 collective-permute-start.14
  248.5 7.7 %slot.19 = (bf16[65,256,256]{2,1,0:T(8,128)(2,1)}, f32[16,256,256]{2,1,0:T(8,128)}) custom-call(s32[16,12]{1,0:T(8,128)} %concatenate.4.refs_0_, bf16[8,256,768]{2,1,0:T(8,128)(2,1)} %bitcast.26, bf16[256,768]{1,0:T(8,128)(2,1)} %copy-done.10, f32[8,256,1]{2,1,0:T(8,128)} %mul.62.refs_3_, ...), custom_call_target="tpu_custom_call", output_to_operand_aliasing={{0}: (6, {}), {1}: (7, {})} | custom-call | flops 2000000000 | bytes 8000000 | tf_op jit(solution)/shard_map/slot/pallas_call | solution.py:218
  256.2 4.7 slot.20
  260.9 8.7 %slot.21 = (bf16[65,256,256]{2,1,0:T(8,128)(2,1)}, f32[16,256,256]{2,1,0:T(8,128)}) custom-call(s32[16,12]{1,0:T(8,128)} %concatenate.4.refs_0_, bf16[8,256,768]{2,1,0:T(8,128)(2,1)} %bitcast.28, bf16[256,768]{1,0:T(8,128)(2,1)} %copy-done.7, f32[8,256,1]{2,1,0:T(8,128)} %mul.62.refs_3_, ...), custom_call_target="tpu_custom_call", output_to_operand_aliasing={{0}: (6, {}), {1}: (7, {})} | custom-call | flops 2000000000 | bytes 8000000 | tf_op jit(solution)/shard_map/slot/pallas_call | solution.py:218
  269.6 6.4 %slot.22 = (bf16[65,256,256]{2,1,0:T(8,128)(2,1)}, f32[16,256,256]{2,1,0:T(8,128)}) custom-call(s32[16,12]{1,0:T(8,128)} %concatenate.4.refs_0_, bf16[8,256,768]{2,1,0:T(8,128)(2,1)} %bitcast.29, bf16[256,768]{1,0:T(8,128)(2,1)} %copy-done.6, f32[8,256,1]{2,1,0:T(8,128)} %mul.62.refs_3_, ...), custom_call_target="tpu_custom_call", output_to_operand_aliasing={{0}: (6, {}), {1}: (7, {})} | custom-call | flops 2000000000 | bytes 8000000 | tf_op jit(solution)/shard_map/slot/pallas_call | solution.py:218
  276.0 2.1 collective-permute-done.2.refs_2_
  278.1 1.1 collective-permute-start.11
  279.2 3.8 collective-permute-start.3
  283.0 7.2 %slot.23 = (bf16[65,256,256]{2,1,0:T(8,128)(2,1)}, f32[16,256,256]{2,1,0:T(8,128)}) custom-call(s32[16,12]{1,0:T(8,128)} %concatenate.4.refs_0_, bf16[8,256,768]{2,1,0:T(8,128)(2,1)} %bitcast.30, bf16[256,768]{1,0:T(8,128)(2,1)} %copy-done.13, f32[8,256,1]{2,1,0:T(8,128)} %mul.62.refs_3_, ...), custom_call_target="tpu_custom_call", output_to_operand_aliasing={{0}: (6, {}), {1}: (7, {})} | custom-call | flops 2000000000 | bytes 8000000 | tf_op jit(solution)/shard_map/slot/pallas_call | solution.py:218
  290.2 4.7 slot.24
  294.8 8.7 %slot.25 = (bf16[65,256,256]{2,1,0:T(8,128)(2,1)}, f32[16,256,256]{2,1,0:T(8,128)}) custom-call(s32[16,12]{1,0:T(8,128)} %concatenate.4.refs_0_, bf16[8,256,768]{2,1,0:T(8,128)(2,1)} %bitcast.32, bf16[256,768]{1,0:T(8,128)(2,1)} %copy-done.11, f32[8,256,1]{2,1,0:T(8,128)} %mul.62.refs_3_, ...), custom_call_target="tpu_custom_call", output_to_operand_aliasing={{0}: (6, {}), {1}: (7, {})} | custom-call | flops 2000000000 | bytes 8000000 | tf_op jit(solution)/shard_map/slot/pallas_call | solution.py:218
  303.5 0.7 copy-done.8
  304.3 4.1 slot.26
  308.4 0.8 copy-done.16
  309.1 9.3 %slot.27 = (bf16[65,256,256]{2,1,0:T(8,128)(2,1)}, f32[16,256,256]{2,1,0:T(8,128)}) custom-call(s32[16,12]{1,0:T(8,128)} %concatenate.4.refs_0_, bf16[8,256,768]{2,1,0:T(8,128)(2,1)} %bitcast.34, bf16[256,768]{1,0:T(8,128)(2,1)} %copy-done.16, f32[8,256,1]{2,1,0:T(8,128)} %mul.62.refs_3_, ...), custom_call_target="tpu_custom_call", output_to_operand_aliasing={{0}: (6, {}), {1}: (7, {})} | custom-call | flops 2000000000 | bytes 8000000 | tf_op jit(solution)/shard_map/slot/pallas_call | solution.py:218
  318.5 0.8 copy-done.15
  319.2 4.7 slot.28
  323.9 0.8 copy-done.14
  324.7 9.3 %slot.29 = (bf16[65,256,256]{2,1,0:T(8,128)(2,1)}, f32[16,256,256]{2,1,0:T(8,128)}) custom-call(s32[16,12]{1,0:T(8,128)} %concatenate.4.refs_0_, bf16[8,256,768]{2,1,0:T(8,128)(2,1)} %bitcast.36, bf16[256,768]{1,0:T(8,128)(2,1)} %copy-done.14, f32[8,256,1]{2,1,0:T(8,128)} %mul.62.refs_3_, ...), custom_call_target="tpu_custom_call", output_to_operand_aliasing={{0}: (6, {}), {1}: (7, {})} | custom-call | flops 2000000000 | bytes 8000000 | tf_op jit(solution)/shard_map/slot/pallas_call | solution.py:218
  334.0 3.8 convert_element_type.75
  337.8 5.7 all-to-all-start.1
  343.8 0.6 pad_add_fusion.1.pairs
  344.4 0.5 compare_select_fusion.1.refs_0_
  345.0 2.7 select_convert_fusion.lrem
  347.7 38.8 %gather.8.refs_1_ = f32[8,256,256]{2,1,0:T(8,128)} custom-call(s32[2,64]{1,0:T(2,128)} %pad_add_fusion.1.pairs, bf16[65,256,256]{2,1,0:T(8,128)(2,1)} %get-tuple-element.140.kref, bf16[16,256,256]{2,1,0:T(8,128)(2,1)} %select_convert_fusion.lrem), custom_call_target="tpu_custom_call" | custom-call | flops 20000000000 | bytes 60000000 | tf_op jit(solution)/shard_map/gather/pallas_call | solution.py:259
  386.5 4.4 all-to-all-done.1
  390.9 2.4 convert_element_type.76.refs_2_
  393.3 10.7 %update.2 = (f32[8,256,1]{2,1,0:T(8,128)}, f32[8,256,256]{2,1,0:T(8,128)}, bf16[8,256,256]{2,1,0:T(8,128)(2,1)}) custom-call(s32[16]{0:T(128)} %compare_select_fusion.1.refs_0_, f32[8,256,256]{2,1,0:T(8,128)} %gather.8.refs_1_, f32[16,256,256]{2,1,0:T(8,128)} %convert_element_type.76.refs_2_, f32[8,256,256]{2,1,0:T(8,128)} %get-tuple-element.153.refs_3_, ...), custom_call_target="tpu_custom_call" | custom-call | tf_op jit(solution)/shard_map/update/pallas_call | solution.py:280
  404.0 2.5 broadcast_in_dim.144.unused
  406.5 40.8 %push.1 = f32[16,256,256]{2,1,0:T(8,128)} custom-call(s32[2,64]{1,0:T(2,128)} %pad_add_fusion.1.pairs, bf16[65,256,256]{2,1,0:T(8,128)(2,1)} %get-tuple-element.140.kref, bf16[8,256,256]{2,1,0:T(8,128)(2,1)} %get-tuple-element.142.src.lloc, f32[16,256,256]{2,1,0:T(8,128)} %broadcast_in_dim.144.unused), custom_call_target="tpu_custom_call", output_to_operand_aliasing={{}: (3, {})} | custom-call | flops 20000000000 | bytes 60000000 | tf_op jit(solution)/shard_map/push/pallas_call | solution.py:240
  447.2 3.9 convert_element_type.77
  451.1 5.0 all-to-all-start.3
  456.1 65.4 %spread.1 = bf16[16,256,256]{2,1,0:T(8,128)(2,1)} custom-call(s32[16]{0:T(128)} %bitcast.46, bf16[8,256,256]{2,1,0:T(8,128)(2,1)} %get-tuple-element.142.src.lloc), custom_call_target="tpu_custom_call" | custom-call | tf_op jit(solution)/shard_map/spread/pallas_call | solution.py:297
  521.6 6.0 all-to-all-start.2
  527.6 2.4 convert_element_type.78.refs_2_
  530.0 45.1 %all-to-all-done.2.lrem = bf16[16,256,256]{2,1,0:T(8,128)(2,1)} async-done(((bf16[16,256,256]{2,1,0:T(8,128)(2,1)}), bf16[16,256,256]{2,1,0:T(8,128)(2,1)}, u32[]{:S(2)}, u32[]{:S(2)}) %all-to-all-start.2) | async-done | bytes 2097184 | tf_op jit(solution)/shard_map/all_to_all | solution.py:311
  575.1 38.8 %gather.9.refs_1_ = f32[8,256,256]{2,1,0:T(8,128)} custom-call(s32[2,64]{1,0:T(2,128)} %pad_add_fusion.1.pairs, bf16[65,256,256]{2,1,0:T(8,128)(2,1)} %get-tuple-element.140.kref, bf16[16,256,256]{2,1,0:T(8,128)(2,1)} %all-to-all-done.2.lrem), custom_call_target="tpu_custom_call" | custom-call | flops 20000000000 | bytes 60000000 | tf_op jit(solution)/shard_map/gather/pallas_call | solution.py:259
  614.0 10.2 %update.3 = f32[8,256,256]{2,1,0:T(8,128)} custom-call(s32[16]{0:T(128)} %compare_select_fusion.1.refs_0_, f32[8,256,256]{2,1,0:T(8,128)} %gather.9.refs_1_, f32[16,256,256]{2,1,0:T(8,128)} %convert_element_type.78.refs_2_, f32[8,256,256]{2,1,0:T(8,128)} %get-tuple-element.143.refs_3_, f32[8,256,256]{2,1,0:T(8,128)} %get-tuple-element.151.refs_4_, ...), custom_call_target="tpu_custom_call" | custom-call | tf_op jit(solution)/shard_map/update/pallas_call | solution.py:280
  (89 shorter events, 2.3 us)
Async XLA Ops:
  0.0 42.6 %copy-start.21 = (s32[1,16]{1,0:T(1,128)S(1)}, s32[1,16]{1,0:T(1,128)}, u32[]{:S(2)}) copy-start(s32[1,16]{1,0:T(1,128)} %param.9) | copy-start | bytes 196
  0.0 41.9 %copy-start = (bf16[2048,768]{1,0:T(8,128)(2,1)S(1)}, bf16[2048,768]{1,0:T(8,128)(2,1)}, u32[]{:S(2)}) copy-start(bf16[2048,768]{1,0:T(8,128)(2,1)} %param.6) | copy-start | bytes 9437188
  0.0 42.6 %copy-start.18 = (s32[2048]{0:T(1024)S(1)}, s32[2048]{0:T(1024)}, u32[]{:S(2)}) copy-start(s32[2048]{0:T(1024)} %param.7) | copy-start | bytes 24580
  0.0 42.6 %copy-start.17 = (s32[2048]{0:T(1024)S(1)}, s32[2048]{0:T(1024)}, u32[]{:S(2)}) copy-start(s32[2048]{0:T(1024)} %param.8) | copy-start | bytes 24580
  39.5 158.9 %copy-start.20 = (s32[64]{0:T(128)S(1)}, s32[64]{0:T(128)}, u32[]{:S(2)}) copy-start(s32[64]{0:T(128)} %param.10) | copy-start | bytes 772
  39.5 158.9 %copy-start.19 = (s32[64]{0:T(128)S(1)}, s32[64]{0:T(128)}, u32[]{:S(2)}) copy-start(s32[64]{0:T(128)} %param.11) | copy-start | bytes 772
  39.5 163.7 %collective-permute-start.8 = (bf16[256,768]{1,0:T(8,128)(2,1)}, bf16[256,768]{1,0:T(8,128)(2,1)}, u32[]{:S(2)}, u32[]{:S(2)}) collective-permute-start(bf16[256,768]{1,0:T(8,128)(2,1)} %get-tuple-element.92), channel_id=1, source_target_pairs={{0,8},{1,9},{2,10},{3,11},{4,12},{5,13},{6,14},{7,15},{8,0},{9,1},... | collective-permute-start | bytes 1179656 | tf_op jit(solution)/shard_map/ppermute | solution.py:181
  43.9 167.8 %all-to-all-start = ((f32[16,2,256]{2,1,0:T(2,128)}), f32[16,2,256]{2,1,0:T(2,128)S(1)}, u32[]{:S(2)}, u32[]{:S(2)}) async-start(f32[16,2,256]{2,1,0:T(2,128)} %gather_fusion), calls=%async_computation | async-start | bytes 65536 | tf_op jit(solution)/shard_map/all_to_all | solution.py:188
  48.7 154.5 %collective-permute-start.4 = (bf16[256,768]{1,0:T(8,128)(2,1)}, bf16[256,768]{1,0:T(8,128)(2,1)S(1)}, u32[]{:S(2)}, u32[]{:S(2)}) collective-permute-start(bf16[256,768]{1,0:T(8,128)(2,1)} %get-tuple-element.85), channel_id=1, source_target_pairs={{0,1},{1,0},{2,3},{3,2},{4,5},{5,4},{6,7},{7,6},{8,9},{9,8},{10,11... | collective-permute-start | bytes 1179656 | tf_op jit(solution)/shard_map/ppermute | solution.py:181
  49.0 154.1 %collective-permute-start = (bf16[256,768]{1,0:T(8,128)(2,1)}, bf16[256,768]{1,0:T(8,128)(2,1)S(1)}, u32[]{:S(2)}, u32[]{:S(2)}) collective-permute-start(bf16[256,768]{1,0:T(8,128)(2,1)} %get-tuple-element.78), channel_id=1, source_target_pairs={{0,9},{1,8},{2,11},{3,10},{4,13},{5,12},{6,15},{7,14},{8,1},{9,0},... | collective-permute-start | bytes 1179656 | tf_op jit(solution)/shard_map/ppermute | solution.py:181
  196.1 10.6 %collective-permute-start.12 = (bf16[256,768]{1,0:T(8,128)(2,1)}, bf16[256,768]{1,0:T(8,128)(2,1)S(1)}, u32[]{:S(2)}, u32[]{:S(2)}) collective-permute-start(bf16[256,768]{1,0:T(8,128)(2,1)} %get-tuple-element.98), channel_id=1, source_target_pairs={{0,2},{1,3},{2,0},{3,1},{4,6},{5,7},{6,4},{7,5},{8,10},{9,11},{10,... | collective-permute-start | bytes 1179656 | tf_op jit(solution)/shard_map/ppermute | solution.py:181
  203.2 16.2 %copy-start.4 = (bf16[256,768]{1,0:T(8,128)(2,1)}, bf16[256,768]{1,0:T(8,128)(2,1)S(1)}, u32[]{:S(2)}) copy-start(bf16[256,768]{1,0:T(8,128)(2,1)S(1)} %collective-permute-done.4.refs_2_) | copy-start | bytes 1179652
  203.2 20.9 %copy-start.3 = (bf16[256,768]{1,0:T(8,128)(2,1)}, bf16[256,768]{1,0:T(8,128)(2,1)S(1)}, u32[]{:S(2)}) copy-start(bf16[256,768]{1,0:T(8,128)(2,1)S(1)} %collective-permute-done.refs_2_) | copy-start | bytes 1179652
  206.7 17.4 %copy-start.5 = (bf16[256,768]{1,0:T(8,128)(2,1)}, bf16[256,768]{1,0:T(8,128)(2,1)S(1)}, u32[]{:S(2)}) copy-start(bf16[256,768]{1,0:T(8,128)(2,1)S(1)} %collective-permute-done.12.refs_2_) | copy-start | bytes 1179652
  206.7 27.8 %collective-permute-start.9 = (bf16[256,768]{1,0:T(8,128)(2,1)}, bf16[256,768]{1,0:T(8,128)(2,1)S(1)}, u32[]{:S(2)}, u32[]{:S(2)}) collective-permute-start(bf16[256,768]{1,0:T(8,128)(2,1)} %get-tuple-element.93), channel_id=1, source_target_pairs={{0,10},{1,11},{2,8},{3,9},{4,14},{5,15},{6,12},{7,13},{8,2},{9,3},... | collective-permute-start | bytes 1179656 | tf_op jit(solution)/shard_map/ppermute | solution.py:181
  207.0 29.5 %collective-permute-start.5 = (bf16[256,768]{1,0:T(8,128)(2,1)}, bf16[256,768]{1,0:T(8,128)(2,1)S(1)}, u32[]{:S(2)}, u32[]{:S(2)}) collective-permute-start(bf16[256,768]{1,0:T(8,128)(2,1)} %get-tuple-element.86), channel_id=1, source_target_pairs={{0,3},{1,2},{2,1},{3,0},{4,7},{5,6},{6,5},{7,4},{8,11},{9,10},{10,... | collective-permute-start | bytes 1179656 | tf_op jit(solution)/shard_map/ppermute | solution.py:181
  209.5 31.9 %collective-permute-start.1 = (bf16[256,768]{1,0:T(8,128)(2,1)}, bf16[256,768]{1,0:T(8,128)(2,1)S(1)}, u32[]{:S(2)}, u32[]{:S(2)}) collective-permute-start(bf16[256,768]{1,0:T(8,128)(2,1)} %get-tuple-element.79), channel_id=1, source_target_pairs={{0,11},{1,10},{2,9},{3,8},{4,15},{5,14},{6,13},{7,12},{8,3},{9,2},... | collective-permute-start | bytes 1179656 | tf_op jit(solution)/shard_map/ppermute | solution.py:181
  211.4 30.1 %collective-permute-start.13 = (bf16[256,768]{1,0:T(8,128)(2,1)}, bf16[256,768]{1,0:T(8,128)(2,1)S(1)}, u32[]{:S(2)}, u32[]{:S(2)}) collective-permute-start(bf16[256,768]{1,0:T(8,128)(2,1)} %get-tuple-element.99), channel_id=1, source_target_pairs={{0,4},{1,5},{2,6},{3,7},{4,0},{5,1},{6,2},{7,3},{8,12},{9,13},{10,... | collective-permute-start | bytes 1179656 | tf_op jit(solution)/shard_map/ppermute | solution.py:181
  211.6 0.6 copy-start.1
  234.5 13.9 %copy-start.10 = (bf16[256,768]{1,0:T(8,128)(2,1)}, bf16[256,768]{1,0:T(8,128)(2,1)S(1)}, u32[]{:S(2)}) copy-start(bf16[256,768]{1,0:T(8,128)(2,1)S(1)} %collective-permute-done.9.refs_2_) | copy-start | bytes 1179652
  236.5 19.7 %copy-start.9 = (bf16[256,768]{1,0:T(8,128)(2,1)}, bf16[256,768]{1,0:T(8,128)(2,1)S(1)}, u32[]{:S(2)}) copy-start(bf16[256,768]{1,0:T(8,128)(2,1)S(1)} %collective-permute-done.5.refs_2_) | copy-start | bytes 1179652
  241.4 14.8 %copy-start.7 = (bf16[256,768]{1,0:T(8,128)(2,1)}, bf16[256,768]{1,0:T(8,128)(2,1)S(1)}, u32[]{:S(2)}) copy-start(bf16[256,768]{1,0:T(8,128)(2,1)S(1)} %collective-permute-done.1.refs_2_) | copy-start | bytes 1179652
  241.5 14.8 %copy-start.6 = (bf16[256,768]{1,0:T(8,128)(2,1)}, bf16[256,768]{1,0:T(8,128)(2,1)S(1)}, u32[]{:S(2)}) copy-start(bf16[256,768]{1,0:T(8,128)(2,1)S(1)} %collective-permute-done.13.refs_2_) | copy-start | bytes 1179652
  241.5 34.5 %collective-permute-start.10 = (bf16[256,768]{1,0:T(8,128)(2,1)}, bf16[256,768]{1,0:T(8,128)(2,1)S(1)}, u32[]{:S(2)}, u32[]{:S(2)}) collective-permute-start(bf16[256,768]{1,0:T(8,128)(2,1)} %get-tuple-element.94), channel_id=1, source_target_pairs={{0,12},{1,13},{2,14},{3,15},{4,8},{5,9},{6,10},{7,11},{8,4},{9,5},... | collective-permute-start | bytes 1179656 | tf_op jit(solution)/shard_map/ppermute | solution.py:181
  241.7 34.3 %collective-permute-start.6 = (bf16[256,768]{1,0:T(8,128)(2,1)}, bf16[256,768]{1,0:T(8,128)(2,1)S(1)}, u32[]{:S(2)}, u32[]{:S(2)}) collective-permute-start(bf16[256,768]{1,0:T(8,128)(2,1)} %get-tuple-element.87), channel_id=1, source_target_pairs={{0,5},{1,4},{2,7},{3,6},{4,1},{5,0},{6,3},{7,2},{8,13},{9,12},{10,... | collective-permute-start | bytes 1179656 | tf_op jit(solution)/shard_map/ppermute | solution.py:181
  247.2 30.9 %collective-permute-start.2 = (bf16[256,768]{1,0:T(8,128)(2,1)}, bf16[256,768]{1,0:T(8,128)(2,1)S(1)}, u32[]{:S(2)}, u32[]{:S(2)}) collective-permute-start(bf16[256,768]{1,0:T(8,128)(2,1)} %get-tuple-element.80), channel_id=1, source_target_pairs={{0,13},{1,12},{2,15},{3,14},{4,9},{5,8},{6,11},{7,10},{8,5},{9,4},... | collective-permute-start | bytes 1179656 | tf_op jit(solution)/shard_map/ppermute | solution.py:181
  247.9 55.7 %collective-permute-start.14 = (bf16[256,768]{1,0:T(8,128)(2,1)}, bf16[256,768]{1,0:T(8,128)(2,1)S(1)}, u32[]{:S(2)}, u32[]{:S(2)}) collective-permute-start(bf16[256,768]{1,0:T(8,128)(2,1)} %get-tuple-element.100), channel_id=1, source_target_pairs={{0,6},{1,7},{2,4},{3,5},{4,2},{5,3},{6,0},{7,1},{8,14},{9,15},{10,... | collective-permute-start | bytes 1179656 | tf_op jit(solution)/shard_map/ppermute | solution.py:181
  269.6 9.6 %copy-start.22 = (bf16[256,768]{1,0:T(8,128)(2,1)S(1)}, bf16[256,768]{1,0:T(8,128)(2,1)}, u32[]{:S(2)}) copy-start(bf16[256,768]{1,0:T(8,128)(2,1)} %get-tuple-element.81) | copy-start | bytes 1179652
  276.0 7.0 %copy-start.13 = (bf16[256,768]{1,0:T(8,128)(2,1)}, bf16[256,768]{1,0:T(8,128)(2,1)S(1)}, u32[]{:S(2)}) copy-start(bf16[256,768]{1,0:T(8,128)(2,1)S(1)} %collective-permute-done.10.refs_2_) | copy-start | bytes 1179652
  276.0 14.2 %copy-start.12 = (bf16[256,768]{1,0:T(8,128)(2,1)}, bf16[256,768]{1,0:T(8,128)(2,1)S(1)}, u32[]{:S(2)}) copy-start(bf16[256,768]{1,0:T(8,128)(2,1)S(1)} %collective-permute-done.6.refs_2_) | copy-start | bytes 1179652
  278.1 12.1 %copy-start.11 = (bf16[256,768]{1,0:T(8,128)(2,1)}, bf16[256,768]{1,0:T(8,128)(2,1)S(1)}, u32[]{:S(2)}) copy-start(bf16[256,768]{1,0:T(8,128)(2,1)S(1)} %collective-permute-done.2.refs_2_) | copy-start | bytes 1179652
  278.1 30.3 %collective-permute-start.11 = (bf16[256,768]{1,0:T(8,128)(2,1)}, bf16[256,768]{1,0:T(8,128)(2,1)S(1)}, u32[]{:S(2)}, u32[]{:S(2)}) collective-permute-start(bf16[256,768]{1,0:T(8,128)(2,1)} %get-tuple-element.95), channel_id=1, source_target_pairs={{0,14},{1,15},{2,12},{3,13},{4,10},{5,11},{6,8},{7,9},{8,6},{9,7},... | collective-permute-start | bytes 1179656 | tf_op jit(solution)/shard_map/ppermute | solution.py:181
  279.2 39.3 %collective-permute-start.7 = (bf16[256,768]{1,0:T(8,128)(2,1)}, bf16[256,768]{1,0:T(8,128)(2,1)S(1)}, u32[]{:S(2)}, u32[]{:S(2)}) collective-permute-start(bf16[256,768]{1,0:T(8,128)(2,1)} %get-tuple-element.88), channel_id=1, source_target_pairs={{0,7},{1,6},{2,5},{3,4},{4,3},{5,2},{6,1},{7,0},{8,15},{9,14},{10,... | collective-permute-start | bytes 1179656 | tf_op jit(solution)/shard_map/ppermute | solution.py:181
  279.2 44.7 %collective-permute-start.3 = (bf16[256,768]{1,0:T(8,128)(2,1)S(1)}, bf16[256,768]{1,0:T(8,128)(2,1)S(1)}, u32[]{:S(2)}, u32[]{:S(2)}) collective-permute-start(bf16[256,768]{1,0:T(8,128)(2,1)S(1)} %copy-done.22), channel_id=1, source_target_pairs={{0,15},{1,14},{2,13},{3,12},{4,11},{5,10},{6,9},{7,8},{8,7},{9,6},... | collective-permute-start | bytes 1179656 | tf_op jit(solution)/shard_map/ppermute | solution.py:181
  303.5 0.8 copy-start.8
  308.4 0.8 copy-start.16
  318.5 0.8 copy-start.15
  323.9 0.8 copy-start.14
  334.0 10.9 %copy-start.2 = (f32[16,2,256]{2,1,0:T(2,128)S(1)}, f32[16,2,256]{2,1,0:T(2,128)}, u32[]{:S(2)}) copy-start(f32[16,2,256]{2,1,0:T(2,128)} %copy-done.1) | copy-start | bytes 98308
  337.8 53.1 %all-to-all-start.1 = ((f16[16,256,256]{2,1,0:T(8,128)(2,1)}), f16[16,256,256]{2,1,0:T(8,128)(2,1)S(1)}, u32[]{:S(2)}, u32[]{:S(2)}) async-start(f16[16,256,256]{2,1,0:T(8,128)(2,1)} %convert_element_type.75), calls=%async_computation.1 | async-start | bytes 4194304 | tf_op jit(solution)/shard_map/all_to_all | solution.py:311
  451.1 70.5 %all-to-all-start.3 = ((f16[16,256,256]{2,1,0:T(8,128)(2,1)}), f16[16,256,256]{2,1,0:T(8,128)(2,1)S(1)}, u32[]{:S(2)}, u32[]{:S(2)}) async-start(f16[16,256,256]{2,1,0:T(8,128)(2,1)} %convert_element_type.77), calls=%async_computation.3 | async-start | bytes 4194304 | tf_op jit(solution)/shard_map/all_to_all | solution.py:311
  521.6 53.6 %all-to-all-start.2 = ((bf16[16,256,256]{2,1,0:T(8,128)(2,1)}), bf16[16,256,256]{2,1,0:T(8,128)(2,1)}, u32[]{:S(2)}, u32[]{:S(2)}) async-start(bf16[16,256,256]{2,1,0:T(8,128)(2,1)} %spread.1), calls=%async_computation.2 | async-start | bytes 4194304 | tf_op jit(solution)/shard_map/all_to_all | solution.py:311

commit v3 on v2

v3 whole, which is shorter than its diff:
```python
import math

import jax
import jax.numpy as jnp
from jax import lax
from jax.experimental import pallas as pl
from jax.experimental.pallas import tpu as pltpu
from jax.sharding import PartitionSpec as P

C = 256
TILE = 256
ITERS = 2
WINDOW = 4
FLIGHT = 5
BATCH = 4
VMEM = 40 * 1024 * 1024

sharpness = 1.0
mixing = 0.8

LOG2E = math.log2(math.e)
ANY = pl.BlockSpec(memory_space=pl.ANY)

PEER, MINE, COUNT, LIST = 0, 1, 2, 3


def take_kernel(table, src, *rest, first):
    outs, sem = rest[:-1], rest[-1]
    for k, out in enumerate(outs):

        @pl.when(pl.program_id(0) == k)
        def _():
            copy = pltpu.make_async_copy(src.at[0], out, sem)
            copy.start()
            copy.wait()


def batch_kernel(table, tiles, bias, meta, own, gin, *rest, slots, begin, scale):
    size = len(slots)
    erem, lrem = rest[:size], rest[size : 2 * size]
    kout, gout, pouts = rest[-2 - size], rest[-1 - size], rest[-size:]
    gout[...] = gin[...]
    for k, slot in enumerate(slots):
        pouts[k][...] = jnp.zeros_like(pouts[k])
        row = meta[table[slot, PEER]][:1]

        def pair(g, carry, k=k, slot=slot, row=row):
            tile = table[slot, LIST + g]
            inner = lax.dot_general(
                tiles[tile], erem[k][...], (((1,), (1,)), ((), ())), preferred_element_type=jnp.float32
            )
            kernel = jnp.exp2(inner * scale + (bias[tile] + row)).astype(jnp.bfloat16)
            kout[k * tiles.shape[0] + g] = kernel
            gout[tile] += jnp.dot(kernel, lrem[k][0], preferred_element_type=jnp.float32)
            pouts[k][...] += lax.dot_general(
                kernel, own[tile], (((0,), (0,)), ((), ())), preferred_element_type=jnp.float32
            )
            return carry

        lax.fori_loop(0, table[slot, COUNT], pair, 0)


def push_kernel(table, kref, own, pout):
    slot = pl.program_id(0)
    pout[...] = jnp.zeros_like(pout)

    def pair(g, carry):
        pout[0] += lax.dot_general(
            kref[g],
            own[table[slot, LIST + g]],
            (((0,), (0,)), ((), ())),
            preferred_element_type=jnp.float32,
        )
        return carry

    lax.fori_loop(0, table[slot, COUNT], pair, 0)


def gather_kernel(table, kref, lrem, gout):
    slot = pl.program_id(0)

    @pl.when(slot == 0)
    def _():
        gout[...] = jnp.zeros_like(gout)

    def pair(g, carry):
        gout[table[slot, LIST + g]] += jnp.dot(kref[g], lrem[0], preferred_element_type=jnp.float32)
        return carry

    lax.fori_loop(0, table[slot, COUNT], pair, 0)


def update_kernel(owners, mine, gathered, classes, *rest, count, first):
    tile = pl.program_id(0)
    backs, rest = rest[:count], rest[count:]
    if first:
        degree, out, send, total, rounded, sem = rest
    else:
        old, degree, out, total = rest
    total[...] = gathered[0]
    for k in range(owners.shape[0]):

        @pl.when(owners[k] == tile)
        def _():
            total[...] += backs[k][...] if first else backs[0][k]

    summed = total[...]
    ids = classes[0]
    target = (ids == lax.broadcasted_iota(jnp.int32, (TILE, C), 1).astype(jnp.float32)).astype(jnp.float32)
    if first:
        degree[0] = 1.0 + jnp.sum(summed, axis=1, keepdims=True)
        labels = jnp.where(ids < 0, 1.0 / C, target)
    else:
        labels = old[0]
    blended = (labels + summed) * (mixing / degree[0]) + (1.0 - mixing) * target
    squared = blended * blended
    labels = squared * (1.0 / jnp.sum(squared, axis=1, keepdims=True))
    out[0] = labels
    if first:
        rounded[tile] = labels.astype(jnp.bfloat16)

        @pl.when(tile == pl.num_programs(0) - 1)
        def _():
            copies = [
                pltpu.make_async_copy(rounded.at[mine[k]], send.at[k], sem.at[k])
                for k in range(send.shape[0])
            ]
            for copy in copies:
                copy.start()
            for copy in copies:
                copy.wait()


def body(embed, seed_mask, seed_class, partner, pair_local, pair_peer):
    n = lax.axis_size("shard")
    me = lax.axis_index("shard")
    features = embed.shape[1]
    tiles = embed.reshape(-1, TILE, features)
    tile_count = tiles.shape[0]
    mine = partner.reshape(-1)
    half = n // 2
    order = []
    for k in range(half):
        order.append(half + k)
        if k + 1 < half:
            order.append(k + 1)
    slot_count = len(order)
    batches = [list(range(b, min(b + BATCH, slot_count))) for b in range(0, slot_count, BATCH)]

    tile_ids = jnp.arange(tile_count, dtype=jnp.int32)
    shard_ids = jnp.arange(n, dtype=jnp.int32)
    peers = jnp.array(order, jnp.int32) ^ me
    mine_x = jnp.sum(jnp.where(peers[:, None] == shard_ids[None, :], mine[None, :], 0), axis=1)
    sends = jnp.stack([peers, mine_x], axis=1).astype(jnp.int32)
    active = jnp.any(
        (pair_peer[None, None, :] == peers[:, None, None])
        & (pair_local[None, None, :] == tile_ids[None, :, None]),
        axis=2,
    )
    counts = jnp.sum(active.astype(jnp.int32), axis=1)
    place = jnp.sum(
        (active[:, None, :] & (tile_ids[None, None, :] < tile_ids[None, :, None])).astype(jnp.int32), axis=2
    )
    listed = jnp.sum(
        jnp.where(
            active[:, None, :] & (place[:, None, :] == tile_ids[None, :, None]), tile_ids[None, None, :], 0
        ),
        axis=2,
    )
    table = jnp.concatenate([sends, counts[:, None], listed], axis=1).astype(jnp.int32)

    def swap(value, k):
        return lax.ppermute(value, "shard", [(q, q ^ order[k]) for q in range(n)])

    def take(slots):
        first, size = slots[0], len(slots)
        return pl.pallas_call(
            lambda *refs: take_kernel(*refs, first=first),
            grid_spec=pltpu.PrefetchScalarGridSpec(
                num_scalar_prefetch=1,
                grid=(size,),
                in_specs=[pl.BlockSpec((1, TILE, features), lambda g, t: (t[first + g, MINE], 0, 0))],
                out_specs=[ANY] * size,
                scratch_shapes=[pltpu.SemaphoreType.DMA],
            ),
            out_shape=[jax.ShapeDtypeStruct((TILE, features), embed.dtype)] * size,
            name="take",
        )(sends, tiles)

    outgoing = list(take(list(range(WINDOW)))) + list(take(list(range(WINDOW, slot_count))))
    flying = []
    for k in range(slot_count):
        out = outgoing[k]
        if k >= WINDOW:
            out, flying[k - WINDOW] = lax.optimization_barrier((out, flying[k - WINDOW]))
        flying.append(swap(out, k))

    norms = jnp.sum(jnp.square(tiles.astype(jnp.float32)), axis=2)
    bias = (1.0 - norms * (1.0 / features)) * (sharpness * LOG2E)
    classes = jnp.where(seed_mask == 1, seed_class, -1).reshape(tile_count, TILE).astype(jnp.float32)
    meta = jnp.stack([bias, classes], axis=1)
    meta_in = lax.all_to_all(meta[mine], "shard", split_axis=0, concat_axis=0, tiled=True)
    class_ids = jnp.arange(C, dtype=jnp.float32)

    def first_labels(ids):
        hot = (ids[..., None] == class_ids).astype(jnp.float32)
        return jnp.where(ids[..., None] < 0, 1.0 / C, hot).astype(jnp.bfloat16)

    own = first_labels(classes)
    own_in = first_labels(meta_in[:, 1])
    bias_column = bias[:, :, None]
    class_column = classes[:, :, None]

    block = (1, TILE, C)
    store = (tile_count, TILE, TILE)
    sums = jax.ShapeDtypeStruct((TILE, C), jnp.float32)
    all_sums = jax.ShapeDtypeStruct((n, TILE, C), jnp.float32)
    tile_sums = jax.ShapeDtypeStruct((tile_count, TILE, C), jnp.float32)
    kernel_store = jax.ShapeDtypeStruct((len(batches) * BATCH * tile_count, TILE, TILE), jnp.bfloat16)

    def full(array):
        return pl.BlockSpec(array.shape, lambda g, t: (0,) * len(array.shape))

    def by_peer(slot):
        return pl.BlockSpec(block, lambda g, t: (t[slot, PEER], 0, 0))

    def batch_call(index, erem, kernels, gathered):
        slots = batches[index]
        size = len(slots)
        begun = [] if kernels is None else [kernels]
        args = [tiles, bias_column, meta_in, own, gathered] + erem + [own_in] * size
        in_specs = [full(a) for a in args[: 5 + size]] + [by_peer(s) for s in slots]
        return pl.pallas_call(
            lambda *refs: batch_kernel(
                *refs, slots=slots, begin=slots[0], scale=2.0 * sharpness * LOG2E / features
            ),
            grid_spec=pltpu.PrefetchScalarGridSpec(
                num_scalar_prefetch=1,
                grid=(1,),
                in_specs=in_specs + [ANY] * len(begun),
                out_specs=[
                    pl.BlockSpec((BATCH * tile_count, TILE, TILE), lambda g, t: (index, 0, 0)),
                    full(tile_sums),
                ]
                + [full(sums)] * size,
            ),
            out_shape=[kernel_store, tile_sums] + [sums] * size,
            input_output_aliases={6 + 2 * size: 0} if begun else {},
            compiler_params=pltpu.CompilerParams(vmem_limit_bytes=VMEM),
            cost_estimate=pl.CostEstimate(flops=int(1e10), bytes_accessed=int(3e7), transcendentals=0),
            name="batch",
        )(table, *args, *begun)

    def push_call(kernels, own):
        return pl.pallas_call(
            push_kernel,
            grid_spec=pltpu.PrefetchScalarGridSpec(
                num_scalar_prefetch=1,
                grid=(slot_count,),
                in_specs=[pl.BlockSpec(store, lambda g, t: (g, 0, 0)), full(own)],
                out_specs=pl.BlockSpec(block, lambda g, t: (t[g, PEER], 0, 0)),
            ),
            out_shape=all_sums,
            compiler_params=pltpu.CompilerParams(vmem_limit_bytes=VMEM),
            cost_estimate=pl.CostEstimate(flops=int(2e10), bytes_accessed=int(6e7), transcendentals=0),
            name="push",
        )(table, kernels, own)

    def gather_call(kernels, incoming):
        return pl.pallas_call(
            gather_kernel,
            grid_spec=pltpu.PrefetchScalarGridSpec(
                num_scalar_prefetch=1,
                grid=(slot_count,),
                in_specs=[
                    pl.BlockSpec(store, lambda g, t: (g, 0, 0)),
                    pl.BlockSpec(block, lambda g, t: (t[g, PEER], 0, 0)),
                ],
                out_specs=full(tile_sums),
            ),
            out_shape=tile_sums,
            compiler_params=pltpu.CompilerParams(vmem_limit_bytes=VMEM),
            cost_estimate=pl.CostEstimate(flops=int(2e10), bytes_accessed=int(6e7), transcendentals=0),
            name="gather",
        )(table, kernels, incoming)

    def update_call(owners, gathered, backs, state):
        first = state is None
        by_tile = pl.BlockSpec(block, lambda g, o, m: (g, 0, 0))
        column = pl.BlockSpec((1, TILE, 1), lambda g, o, m: (g, 0, 0))
        column_shape = jax.ShapeDtypeStruct((tile_count, TILE, 1), jnp.float32)
        back_specs = [pl.BlockSpec(b.shape, lambda g, o, m, d=len(b.shape): (0,) * d) for b in backs]
        out_shape, out_specs = [tile_sums], [by_tile]
        scratch = [pltpu.VMEM((TILE, C), jnp.float32)]
        if first:
            send = jax.ShapeDtypeStruct((n, TILE, C), jnp.bfloat16)
            out_shape, out_specs = [column_shape, tile_sums, send], [column, by_tile, ANY]
            scratch += [
                pltpu.VMEM((tile_count, TILE, C), jnp.bfloat16),
                pltpu.SemaphoreType.DMA((n,)),
            ]
        return pl.pallas_call(
            lambda *refs: update_kernel(*refs, count=len(backs), first=first),
            grid_spec=pltpu.PrefetchScalarGridSpec(
                num_scalar_prefetch=2,
                grid=(tile_count,),
                in_specs=[by_tile, column] + back_specs + ([] if first else [by_tile, column]),
                out_specs=out_specs,
                scratch_shapes=scratch,
            ),
            out_shape=out_shape,
            compiler_params=pltpu.CompilerParams(vmem_limit_bytes=VMEM),
            name="update",
        )(owners, mine, gathered, class_column, *backs, *([] if first else state))

    def exchange(array):
        return lax.all_to_all(array, "shard", split_axis=0, concat_axis=0, tiled=True)

    kernels, gathered = None, jnp.zeros(tile_sums.shape, tile_sums.dtype)
    pushes = []
    for b, slots in enumerate(batches):
        kernels, gathered, *done = batch_call(b, [flying[k] for k in slots], kernels, gathered)
        pushes += done
    for k in range(slot_count):
        out = pushes[k].astype(jnp.float16)
        ahead = slot_count + k - FLIGHT
        out, flying[ahead] = lax.optimization_barrier((out, flying[ahead]))
        flying.append(swap(out, k))
    backs = [back.astype(jnp.float32) for back in flying[slot_count:]]
    degree, labels, send = update_call(mine_x, gathered, backs, None)

    incoming = exchange(send)
    rounded = labels.astype(jnp.bfloat16)
    pushes = push_call(kernels, rounded)
    back = exchange(pushes.astype(jnp.float16)).astype(jnp.float32)
    gathered = gather_call(kernels, incoming)
    owners = jnp.where(shard_ids == me, -1, mine)
    (labels,) = update_call(owners, gathered, [back], [labels, degree])
    return labels.reshape(embed.shape[0], C)


def solution(mesh):
    in_specs = (
        P(("groups", "shard"), None),
        P(("groups", "shard")),
        P(("groups", "shard")),
        P(("groups", "shard"), None),
        P(("groups", "shard")),
        P(("groups", "shard")),
    )
    out_specs = P(("groups", "shard"), None)
    return jax.shard_map(body, mesh=mesh, in_specs=in_specs, out_specs=out_specs, check_vma=False)
```

time: 630 us -> 388 us (0.62)
  Pallas kernels: 485 us -> 122 us
  waiting for transfers between devices: 62.1 us -> 142 us
  blocking collectives: 0 us -> 51.3 us
  other arithmetic: 22.8 us -> 14.8 us
    pallas_call x20 -> x8, Pallas kernels: 367 us -> 80.9 us  [the longest x4 50.8 us: batch_call(): pl.pallas_call(lambda *refs: batch_kernel(*refs, slots=slots, begin=slots...]
    ppermute x15 -> x30, waiting for transfers between devices: 12.6 us -> 88.3 us  [swap(): return lax.ppermute(value, 'shard', [(q, q ^ order[k]) for q in range(n)])]
    pallas_call x2 -> x1, Pallas kernels: 77.6 us -> 20 us  [gather_call(): pl.pallas_call(gather_kernel, grid_spec=pltpu.PrefetchScalarGridSpec(num_...]
    all_to_all x0 -> x1, blocking collectives: none -> 51.3 us  [exchange(): lax.all_to_all(array, 'shard', split_axis=0, concat_axis=0, tiled=True)]
    pallas_call x1, Pallas kernels: 40.8 us -> 21.3 us  [push_call(): pl.pallas_call(push_kernel, grid_spec=pltpu.PrefetchScalarGridSpec(num_sc...]
    ppermute x15 -> x30, starting transfers between devices: 22 us -> 36.4 us  [swap(): return lax.ppermute(value, 'shard', [(q, q ^ order[k]) for q in range(n)])]
    all_to_all x3 -> x1, starting transfers between devices: 16.7 us -> 5.12 us  [exchange(): lax.all_to_all(array, 'shard', split_axis=0, concat_axis=0, tiled=True)]
    all_to_all x1, waiting for transfers between devices: 0.01 us -> 10.6 us  [body(): lax.all_to_all(meta[mine], 'shard', split_axis=0, concat_axis=0, tiled=True)]
  transfers between devices with their start and end apart: 19 -> 32, of which waited for: 6 -> 11; matrix products, arithmetic and copies ran while one was open for 2% -> 4% of each run, Pallas kernels for 54% -> 16%
where the time goes in v3:
time: 388 us; the launch traced here: 387 us
  waiting for transfers between devices  142 us (37%)
  Pallas kernels  122 us (31%)
  blocking collectives  51.3 us (13%)
  starting transfers between devices  47.3 us (12%)
  other arithmetic  14.8 us (4%)
  local copies, waits for them, and re-layouts  7.88 us (2%)
    ppermute x30, waiting for transfers between devices, swap(): return lax.ppermute(value, 'shard', [(q, q ^ order[k]) for q in range(n)])  88.3 us
    all_to_all x1, blocking collectives, exchange(): lax.all_to_all(array, 'shard', split_axis=0, concat_axis=0, tiled=True)  51.3 us
    pallas_call x4, Pallas kernels, batch_call(): pl.pallas_call(lambda *refs: batch_kernel(*refs, slots=slots, begin=slots...  50.8 us
    all_to_all x1, waiting for transfers between devices, exchange(): lax.all_to_all(array, 'shard', split_axis=0, concat_axis=0, tiled=True)  43.6 us
    ppermute x30, starting transfers between devices, swap(): return lax.ppermute(value, 'shard', [(q, q ^ order[k]) for q in range(n)])  36.4 us
    pallas_call x1, Pallas kernels, push_call(): pl.pallas_call(push_kernel, grid_spec=pltpu.PrefetchScalarGridSpec(num_sc...  21.3 us
    pallas_call x1, Pallas kernels, gather_call(): pl.pallas_call(gather_kernel, grid_spec=pltpu.PrefetchScalarGridSpec(num_...  20 us
    pallas_call x2, Pallas kernels, take(): pl.pallas_call(lambda *refs: take_kernel(*refs, first=first), grid_spec=p...  16.8 us
  transfers between devices with their start and end apart: 32, of which 11 were waited for; matrix products, arithmetic and copies ran while one was open for 4% of the time, Pallas kernels for 16%

profile of v3, /device:TPU:13, one launch (start us, length us, event | category | flops | bytes accessed | tf_op | source)
XLA Modules:
  0.0 386.7 jit_solution(4445252107253700200)
XLA Ops:
  0.0 0.8 fusion.2
  0.8 1.0 select_reduce_fusion.1.refs_0_
  1.8 0.7 copy.58.refs_0_
  2.5 5.2 %take.3 = (bf16[256,768]{1,0:T(8,128)(2,1)}, bf16[256,768]{1,0:T(8,128)(2,1)}, bf16[256,768]{1,0:T(8,128)(2,1)}, bf16[256,768]{1,0:T(8,128)(2,1)}) custom-call(s32[15,2]{1,0:T(8,128)} %copy.58.refs_0_, bf16[8,256,768]{2,1,0:T(8,128)(2,1)} %bitcast.19), custom_call_target="tpu_custom_call" | custom-call | tf_op jit(solution)/shard_map/take/pallas_call | solution.py:177
  7.8 2.9 collective-permute-start.2
  10.7 0.2 collective-permute-start.3
  11.0 0.7 collective-permute-start.1
  11.7 0.7 multiply_reduce_fusion
  12.5 1.2 gather_fusion
  13.7 5.8 %all-to-all-start = ((f32[16,2,256]{2,1,0:T(2,128)}), f32[16,2,256]{2,1,0:T(2,128)S(1)}, u32[]{:S(2)}, u32[]{:S(2)}) async-start(f32[16,2,256]{2,1,0:T(2,128)} %gather_fusion), calls=%async_computation | async-start | bytes 65536 | tf_op jit(solution)/shard_map/all_to_all | solution.py:202
  19.5 0.7 broadcast_compare_fusion.2
  20.2 0.7 iota_compare_fusion.5
  20.9 0.4 and_reduce_fusion
  21.5 11.6 %take.2 = (bf16[256,768]{1,0:T(8,128)(2,1)}, bf16[256,768]{1,0:T(8,128)(2,1)}, bf16[256,768]{1,0:T(8,128)(2,1)}, bf16[256,768]{1,0:T(8,128)(2,1)}, bf16[256,768]...) custom-call(s32[15,2]{1,0:T(8,128)} %copy.58.refs_0_, ...), custom_call_target="tpu_custom_call" | custom-call | tf_op jit(solution)/shard_map/take/pallas_call | solution.py:177
  33.3 0.9 mul.54.refs_2_
  34.4 0.7 select_convert_fusion.1.refs_4_
  35.1 10.6 %all-to-all-done.refs_3_ = f32[16,2,256]{2,1,0:T(2,128)S(1)} async-done(((f32[16,2,256]{2,1,0:T(2,128)}), f32[16,2,256]{2,1,0:T(2,128)S(1)}, u32[]{:S(2)}, u32[]{:S(2)}) %all-to-all-start) | async-done | bytes 32800 | tf_op jit(solution)/shard_map/all_to_all | solution.py:202
  45.8 4.0 %collective-permute-start.4 = (bf16[256,768]{1,0:T(8,128)(2,1)}, bf16[256,768]{1,0:T(8,128)(2,1)S(1)}, u32[]{:S(2)}, u32[]{:S(2)}) collective-permute-start(bf16[256,768]{1,0:T(8,128)(2,1)} %get-tuple-element.107), channel_id=1, source_target_pairs={{0,10},{1,11},{2,8},{3,9},{4,14},{5,15},{6,12},{7,13},{8,2},{9,3},... | collective-permute-start | bytes 1179656 | tf_op jit(solution)/shard_map/ppermute | solution.py:173
  49.7 0.9 collective-permute-start.5
  50.6 0.8 collective-permute-start.7
  51.5 1.4 select_convert_fusion.refs_10_.refs_11_.refs_12_.refs_13_.refs_9_
  52.9 22.7 %collective-permute-done.4.refs_6_ = bf16[256,768]{1,0:T(8,128)(2,1)S(1)} collective-permute-done((bf16[256,768]{1,0:T(8,128)(2,1)}, bf16[256,768]{1,0:T(8,128)(2,1)S(1)}, u32[]{:S(2)}, u32[]{:S(2)}) %collective-permute-start.4) | collective-permute-done | bytes 393248 | tf_op jit(solution)/shard_map/ppermute | solution.py:173
  75.7 0.9 collective-permute-done.5.refs_7_
  76.6 7.5 %collective-permute-done.6.refs_8_ = bf16[256,768]{1,0:T(8,128)(2,1)S(1)} collective-permute-done((bf16[256,768]{1,0:T(8,128)(2,1)}, bf16[256,768]{1,0:T(8,128)(2,1)S(1)}, u32[]{:S(2)}, u32[]{:S(2)}) %collective-permute-start.6) | collective-permute-done | bytes 393248 | tf_op jit(solution)/shard_map/ppermute | solution.py:173
  84.1 1.9 collective-permute-start.8
  86.0 2.9 collective-permute-start.9
  88.9 0.6 collective-permute-start.11
  89.7 10.6 %batch.4 = (bf16[128,256,256]{2,1,0:T(8,128)(2,1)}, f32[8,256,256]{2,1,0:T(8,128)S(1)}, f32[256,256]{1,0:T(8,128)S(1)}, f32[256,256]{1,0:T(8,128)S(1)}, f32[256,256]{1,0:T(8,128)S(1)}, /*index=5*/f32[256,256]{1,0:T(8,128)S(1)}) custom-call(s32[15,11]{1,0:T(8,128)S(1)} %pad_add_fusion.refs_0_.table, bf16[8,256,768]{2,1,0:T(8,128)(2,1)S(1)} %bitcast.21, ...), custom_call_target="tpu_custom_call" | custom-call | flops 10000000000 | bytes 30000000 | tf_op jit(solution)/shard_map/batch/pallas_call | solution.py:233
  100.5 12.4 %collective-permute-done.10.refs_8_ = bf16[256,768]{1,0:T(8,128)(2,1)S(1)} collective-permute-done((bf16[256,768]{1,0:T(8,128)(2,1)}, bf16[256,768]{1,0:T(8,128)(2,1)S(1)}, u32[]{:S(2)}, u32[]{:S(2)}) %collective-permute-start.10) | collective-permute-done | bytes 393248 | tf_op jit(solution)/shard_map/ppermute | solution.py:173
  112.9 8.2 %collective-permute-done.8.refs_6_ = bf16[256,768]{1,0:T(8,128)(2,1)S(1)} collective-permute-done((bf16[256,768]{1,0:T(8,128)(2,1)}, bf16[256,768]{1,0:T(8,128)(2,1)S(1)}, u32[]{:S(2)}, u32[]{:S(2)}) %collective-permute-start.8) | collective-permute-done | bytes 393248 | tf_op jit(solution)/shard_map/ppermute | solution.py:173
  121.1 2.7 collective-permute-start.12
  123.8 0.5 collective-permute-done.11.refs_9_
  124.4 1.0 collective-permute-start.16
  125.4 2.1 collective-permute-start.15
  127.5 11.8 %batch.5 = (bf16[128,256,256]{2,1,0:T(8,128)(2,1)}, f32[8,256,256]{2,1,0:T(8,128)S(1)}, f32[256,256]{1,0:T(8,128)S(1)}, f32[256,256]{1,0:T(8,128)S(1)}, f32[256,256]{1,0:T(8,128)S(1)}, /*index=5*/f32[256,256]{1,0:T(8,128)S(1)}) custom-call(s32[15,11]{1,0:T(8,128)S(1)} %pad_add_fusion.refs_0_.table, ...), custom_call_target="tpu_custom_call", output_to_operand_aliasing={{0}: (14, {})} | custom-call | flops 10000000000 | bytes 30000000 | tf_op jit(solution)/shard_map/batch/pallas_call | solution.py:233
  139.5 29.6 %collective-permute-done.15 = f16[256,256]{1,0:T(8,128)(2,1)S(1)} collective-permute-done((f16[256,256]{1,0:T(8,128)(2,1)S(1)}, f16[256,256]{1,0:T(8,128)(2,1)S(1)}, u32[]{:S(2)}, u32[]{:S(2)}) %collective-permute-start.15) | collective-permute-done | bytes 131104 | tf_op jit(solution)/shard_map/ppermute | solution.py:173
  169.1 2.3 collective-permute-start.20
  171.4 3.5 collective-permute-start.19
  174.9 0.8 collective-permute-start.18
  175.7 14.8 %batch.6 = (bf16[128,256,256]{2,1,0:T(8,128)(2,1)}, f32[8,256,256]{2,1,0:T(8,128)S(1)}, f32[256,256]{1,0:T(8,128)S(1)}, f32[256,256]{1,0:T(8,128)S(1)}, f32[256,256]{1,0:T(8,128)S(1)}, /*index=5*/f32[256,256]{1,0:T(8,128)S(1)}) custom-call(s32[15,11]{1,0:T(8,128)S(1)} %pad_add_fusion.refs_0_.table, ...), custom_call_target="tpu_custom_call", output_to_operand_aliasing={{0}: (14, {})} | custom-call | flops 10000000000 | bytes 30000000 | tf_op jit(solution)/shard_map/batch/pallas_call | solution.py:233
  190.5 0.7 convert_element_type.179
  191.2 0.7 convert_element_type.177
  191.9 1.2 collective-permute-start.25
  193.1 3.7 collective-permute-start.24
  197.0 13.7 %batch.7 = (bf16[128,256,256]{2,1,0:T(8,128)(2,1)}, f32[8,256,256]{2,1,0:T(8,128)S(1)}, f32[256,256]{1,0:T(8,128)S(1)}, f32[256,256]{1,0:T(8,128)S(1)}, f32[256,256]{1,0:T(8,128)S(1)}) custom-call(s32[15,11]{1,0:T(8,128)S(1)} %pad_add_fusion.refs_0_.table, bf16[8,256,768]{2,1,0:T(8,128)(2,1)S(1)} %bitcast.24, ...), custom_call_target="tpu_custom_call", output_to_operand_aliasing={{0}: (12, {})} | custom-call | flops 10000000000 | bytes 30000000 | tf_op jit(solution)/shard_map/batch/pallas_call | solution.py:233
  210.7 1.3 copy-done.4
  212.2 3.7 collective-permute-start.28
  215.9 0.6 copy-done.19
  216.5 0.9 convert_element_type.195.refs_3_
  217.6 1.1 convert_element_type.188.refs_15_
  218.7 0.9 convert_element_type.187.refs_14_
  219.8 3.6 collective-permute-done.29
  223.4 2.7 collective-permute-done.27
  226.2 7.7 %update.2 = (f32[8,256,1]{2,1,0:T(8,128)S(1)}, f32[8,256,256]{2,1,0:T(8,128)S(1)}, bf16[16,256,256]{2,1,0:T(8,128)(2,1)S(1)}) custom-call(s32[15]{0:T(128)S(1)} %select_reduce_fusion.1.refs_0_, s32[16]{0:T(128)S(1)} %bitcast.28, f32[8,256,256]{2,1,0:T(8,128)S(1)} %copy-done.5, f32[8,256,1]{2,1,0:T(8,128)S(1)} %convert_element_type.195.refs_3_, ...), custom_call_target="tpu_custom_call" | custom-call | tf_op jit(solution)/shard_map/update/pallas_call | solution.py:302
  234.1 1.2 copy-done.3
  235.3 0.3 copy-done.6
  235.6 21.3 %push.1 = f32[16,256,256]{2,1,0:T(8,128)S(1)} custom-call(s32[15,11]{1,0:T(8,128)S(1)} %pad_add_fusion.refs_0_.table, bf16[128,256,256]{2,1,0:T(8,128)(2,1)} %get-tuple-element.136.kref, bf16[8,256,256]{2,1,0:T(8,128)(2,1)S(1)} %convert_element_type.192.own), custom_call_target="tpu_custom_call" | custom-call | flops 20000000000 | bytes 60000000 | tf_op jit(solution)/shard_map/push/pallas_call | solution.py:255
  256.9 0.3 convert_element_type.193
  257.3 51.3 %all_to_all.15 = f16[16,256,256]{2,1,0:T(8,128)(2,1)} all-to-all(f16[16,256,256]{2,1,0:T(8,128)(2,1)S(1)} %convert_element_type.193), channel_id=1, replica_groups=mesh['groups'=2,'shard'=16] {'shard'}, dimensions={0} | all-to-all | bytes 4194304 | tf_op jit(solution)/shard_map/all_to_all | solution.py:317
  308.5 5.1 %all-to-all-start.1 = ((bf16[16,256,256]{2,1,0:T(8,128)(2,1)}), bf16[16,256,256]{2,1,0:T(8,128)(2,1)}, u32[]{:S(2)}, u32[]{:S(2)}) async-start(bf16[16,256,256]{2,1,0:T(8,128)(2,1)} %copy-done.3), calls=%async_computation.1 | async-start | bytes 4194304 | tf_op jit(solution)/shard_map/all_to_all | solution.py:317
  313.7 4.0 %convert_element_type.194.refs_4_ = f32[16,256,256]{2,1,0:T(8,128)} convert(f16[16,256,256]{2,1,0:T(8,128)(2,1)} %all_to_all.15) | non-fusion elementwise | flops 1048576 | bytes 6291456 | tf_op jit(solution)/shard_map/convert_element_type | solution.py:335
  317.6 43.6 %all-to-all-done.1.lrem = bf16[16,256,256]{2,1,0:T(8,128)(2,1)} async-done(((bf16[16,256,256]{2,1,0:T(8,128)(2,1)}), bf16[16,256,256]{2,1,0:T(8,128)(2,1)}, u32[]{:S(2)}, u32[]{:S(2)}) %all-to-all-start.1) | async-done | bytes 2097184 | tf_op jit(solution)/shard_map/all_to_all | solution.py:317
  361.2 20.0 %gather.7.refs_2_ = f32[8,256,256]{2,1,0:T(8,128)S(1)} custom-call(s32[15,11]{1,0:T(8,128)S(1)} %pad_add_fusion.refs_0_.table, bf16[128,256,256]{2,1,0:T(8,128)(2,1)} %get-tuple-element.136.kref, bf16[16,256,256]{2,1,0:T(8,128)(2,1)} %all-to-all-done.1.lrem), custom_call_target="tpu_custom_call" | custom-call | flops 20000000000 | bytes 60000000 | tf_op jit(solution)/shard_map/gather/pallas_call | solution.py:270
  381.2 5.5 %update.3 = f32[8,256,256]{2,1,0:T(8,128)} custom-call(s32[16]{0:T(128)S(1)} %compare_select_fusion.1.refs_0_, s32[16]{0:T(128)S(1)} %bitcast.29, f32[8,256,256]{2,1,0:T(8,128)S(1)} %gather.7.refs_2_, f32[8,256,1]{2,1,0:T(8,128)S(1)} %convert_element_type.195.refs_3_, f32[16,256,256]{2,1,0:T(8,128)S(1)} %copy-done.2, ...), custom_call_target="tpu_custom_call" | custom-call | tf_op jit(solution)/shard_map/update/pallas_call | solution.py:302
  (139 shorter events, 2.0 us)
Async XLA Ops:
  0.0 11.7 %copy-start = (bf16[2048,768]{1,0:T(8,128)(2,1)S(1)}, bf16[2048,768]{1,0:T(8,128)(2,1)}, u32[]{:S(2)}) copy-start(bf16[2048,768]{1,0:T(8,128)(2,1)} %param.7) | copy-start | bytes 9437188
  0.8 1.0 copy-start.25
  0.8 10.2 %copy-start.23 = (s32[15,1]{0,1:T(1,128)}, s32[15,1]{0,1:T(1,128)S(1)}, u32[]{:S(2)}) copy-start(s32[15,1]{0,1:T(1,128)S(1)} %get-tuple-element.181) | copy-start | bytes 184
  7.7 4.7 %copy-start.8 = (s32[1,16]{1,0:T(1,128)S(1)}, s32[1,16]{1,0:T(1,128)}, u32[]{:S(2)}) copy-start(s32[1,16]{1,0:T(1,128)} %param.10) | copy-start | bytes 196
  7.7 4.7 %copy-start.21 = (s32[2048]{0:T(1024)S(1)}, s32[2048]{0:T(1024)}, u32[]{:S(2)}) copy-start(s32[2048]{0:T(1024)} %param.9) | copy-start | bytes 24580
  7.7 4.7 %copy-start.22 = (s32[2048]{0:T(1024)S(1)}, s32[2048]{0:T(1024)}, u32[]{:S(2)}) copy-start(s32[2048]{0:T(1024)} %param.8) | copy-start | bytes 24580
  7.8 38.0 %collective-permute-start.2 = (bf16[256,768]{1,0:T(8,128)(2,1)}, bf16[256,768]{1,0:T(8,128)(2,1)S(1)}, u32[]{:S(2)}, u32[]{:S(2)}) collective-permute-start(bf16[256,768]{1,0:T(8,128)(2,1)} %get-tuple-element.100), channel_id=1, source_target_pairs={{0,9},{1,8},{2,11},{3,10},{4,13},{5,12},{6,15},{7,14},{8,1},{9,0},... | collective-permute-start | bytes 1179656 | tf_op jit(solution)/shard_map/ppermute | solution.py:173
  10.7 35.1 %collective-permute-start.3 = (bf16[256,768]{1,0:T(8,128)(2,1)}, bf16[256,768]{1,0:T(8,128)(2,1)}, u32[]{:S(2)}, u32[]{:S(2)}) collective-permute-start(bf16[256,768]{1,0:T(8,128)(2,1)} %get-tuple-element.103), channel_id=1, source_target_pairs={{0,2},{1,3},{2,0},{3,1},{4,6},{5,7},{6,4},{7,5},{8,10},{9,11},{10,... | collective-permute-start | bytes 1179656 | tf_op jit(solution)/shard_map/ppermute | solution.py:173
  10.9 34.8 %collective-permute-start = (bf16[256,768]{1,0:T(8,128)(2,1)}, bf16[256,768]{1,0:T(8,128)(2,1)}, u32[]{:S(2)}, u32[]{:S(2)}) collective-permute-start(bf16[256,768]{1,0:T(8,128)(2,1)} %get-tuple-element.94), channel_id=1, source_target_pairs={{0,8},{1,9},{2,10},{3,11},{4,12},{5,13},{6,14},{7,15},{8,0},{9,1},... | collective-permute-start | bytes 1179656 | tf_op jit(solution)/shard_map/ppermute | solution.py:173
  11.0 34.8 %collective-permute-start.1 = (bf16[256,768]{1,0:T(8,128)(2,1)}, bf16[256,768]{1,0:T(8,128)(2,1)}, u32[]{:S(2)}, u32[]{:S(2)}) collective-permute-start(bf16[256,768]{1,0:T(8,128)(2,1)} %get-tuple-element.97), channel_id=1, source_target_pairs={{0,1},{1,0},{2,3},{3,2},{4,5},{5,4},{6,7},{7,6},{8,9},{9,8},{10,11... | collective-permute-start | bytes 1179656 | tf_op jit(solution)/shard_map/ppermute | solution.py:173
  12.4 20.8 %copy-start.24 = (s32[15,1]{0,1:T(1,128)S(1)}, s32[15,1]{0,1:T(1,128)}, u32[]{:S(2)}) copy-start(s32[15,1]{0,1:T(1,128)} %copy-done.23) | copy-start | bytes 184
  13.7 32.0 %all-to-all-start = ((f32[16,2,256]{2,1,0:T(2,128)}), f32[16,2,256]{2,1,0:T(2,128)S(1)}, u32[]{:S(2)}, u32[]{:S(2)}) async-start(f32[16,2,256]{2,1,0:T(2,128)} %gather_fusion), calls=%async_computation | async-start | bytes 65536 | tf_op jit(solution)/shard_map/all_to_all | solution.py:202
  33.3 52.7 %copy-start.29 = (bf16[256,768]{1,0:T(8,128)(2,1)S(1)}, bf16[256,768]{1,0:T(8,128)(2,1)}, u32[]{:S(2)}) copy-start(bf16[256,768]{1,0:T(8,128)(2,1)} %get-tuple-element.124) | copy-start | bytes 1179652
  45.8 29.9 %collective-permute-start.4 = (bf16[256,768]{1,0:T(8,128)(2,1)}, bf16[256,768]{1,0:T(8,128)(2,1)S(1)}, u32[]{:S(2)}, u32[]{:S(2)}) collective-permute-start(bf16[256,768]{1,0:T(8,128)(2,1)} %get-tuple-element.107), channel_id=1, source_target_pairs={{0,10},{1,11},{2,8},{3,9},{4,14},{5,15},{6,12},{7,13},{8,2},{9,3},... | collective-permute-start | bytes 1179656 | tf_op jit(solution)/shard_map/ppermute | solution.py:173
  49.7 26.8 %collective-permute-start.5 = (bf16[256,768]{1,0:T(8,128)(2,1)}, bf16[256,768]{1,0:T(8,128)(2,1)S(1)}, u32[]{:S(2)}, u32[]{:S(2)}) collective-permute-start(bf16[256,768]{1,0:T(8,128)(2,1)} %get-tuple-element.110), channel_id=1, source_target_pairs={{0,3},{1,2},{2,1},{3,0},{4,7},{5,6},{6,5},{7,4},{8,11},{9,10},{10,... | collective-permute-start | bytes 1179656 | tf_op jit(solution)/shard_map/ppermute | solution.py:173
  50.6 33.4 %collective-permute-start.6 = (bf16[256,768]{1,0:T(8,128)(2,1)}, bf16[256,768]{1,0:T(8,128)(2,1)S(1)}, u32[]{:S(2)}, u32[]{:S(2)}) collective-permute-start(bf16[256,768]{1,0:T(8,128)(2,1)} %get-tuple-element.113), channel_id=1, source_target_pairs={{0,11},{1,10},{2,9},{3,8},{4,15},{5,14},{6,13},{7,12},{8,3},{9,2},... | collective-permute-start | bytes 1179656 | tf_op jit(solution)/shard_map/ppermute | solution.py:173
  50.6 33.4 %collective-permute-start.7 = (bf16[256,768]{1,0:T(8,128)(2,1)}, bf16[256,768]{1,0:T(8,128)(2,1)S(1)}, u32[]{:S(2)}, u32[]{:S(2)}) collective-permute-start(bf16[256,768]{1,0:T(8,128)(2,1)} %get-tuple-element.116), channel_id=1, source_target_pairs={{0,4},{1,5},{2,6},{3,7},{4,0},{5,1},{6,2},{7,3},{8,12},{9,13},{10,... | collective-permute-start | bytes 1179656 | tf_op jit(solution)/shard_map/ppermute | solution.py:173
  51.5 38.2 %copy-start.1 = (bf16[2048,768]{1,0:T(8,128)(2,1)S(1)}, bf16[2048,768]{1,0:T(8,128)(2,1)}, u32[]{:S(2)}) copy-start(bf16[2048,768]{1,0:T(8,128)(2,1)} %param.7) | copy-start | bytes 9437188
  84.1 28.8 %collective-permute-start.10 = (bf16[256,768]{1,0:T(8,128)(2,1)}, bf16[256,768]{1,0:T(8,128)(2,1)S(1)}, u32[]{:S(2)}, u32[]{:S(2)}) collective-permute-start(bf16[256,768]{1,0:T(8,128)(2,1)} %get-tuple-element.127), channel_id=1, source_target_pairs={{0,13},{1,12},{2,15},{3,14},{4,9},{5,8},{6,11},{7,10},{8,5},{9,4},... | collective-permute-start | bytes 1179656 | tf_op jit(solution)/shard_map/ppermute | solution.py:173
  84.1 37.0 %collective-permute-start.8 = (bf16[256,768]{1,0:T(8,128)(2,1)}, bf16[256,768]{1,0:T(8,128)(2,1)S(1)}, u32[]{:S(2)}, u32[]{:S(2)}) collective-permute-start(bf16[256,768]{1,0:T(8,128)(2,1)} %get-tuple-element.121), channel_id=1, source_target_pairs={{0,12},{1,13},{2,14},{3,15},{4,8},{5,9},{6,10},{7,11},{8,4},{9,5},... | collective-permute-start | bytes 1179656 | tf_op jit(solution)/shard_map/ppermute | solution.py:173
  86.0 35.1 %collective-permute-start.9 = (bf16[256,768]{1,0:T(8,128)(2,1)S(1)}, bf16[256,768]{1,0:T(8,128)(2,1)S(1)}, u32[]{:S(2)}, u32[]{:S(2)}) collective-permute-start(bf16[256,768]{1,0:T(8,128)(2,1)S(1)} %copy-done.29), channel_id=1, source_target_pairs={{0,5},{1,4},{2,7},{3,6},{4,1},{5,0},{6,3},{7,2},{8,13},{9,12},{10,... | collective-permute-start | bytes 1179656 | tf_op jit(solution)/shard_map/ppermute | solution.py:173
  88.9 35.5 %collective-permute-start.11 = (bf16[256,768]{1,0:T(8,128)(2,1)}, bf16[256,768]{1,0:T(8,128)(2,1)S(1)}, u32[]{:S(2)}, u32[]{:S(2)}) collective-permute-start(bf16[256,768]{1,0:T(8,128)(2,1)} %get-tuple-element.129), channel_id=1, source_target_pairs={{0,6},{1,7},{2,4},{3,5},{4,2},{5,3},{6,0},{7,1},{8,14},{9,15},{10,... | collective-permute-start | bytes 1179656 | tf_op jit(solution)/shard_map/ppermute | solution.py:173
  89.7 31.4 %copy-start.28 = (bf16[256,768]{1,0:T(8,128)(2,1)S(1)}, bf16[256,768]{1,0:T(8,128)(2,1)}, u32[]{:S(2)}) copy-start(bf16[256,768]{1,0:T(8,128)(2,1)} %get-tuple-element.134) | copy-start | bytes 1179652
  89.7 31.4 %copy-start.26 = (bf16[256,768]{1,0:T(8,128)(2,1)S(1)}, bf16[256,768]{1,0:T(8,128)(2,1)}, u32[]{:S(2)}) copy-start(bf16[256,768]{1,0:T(8,128)(2,1)} %get-tuple-element.132) | copy-start | bytes 1179652
  89.7 34.1 %copy-start.27 = (bf16[256,768]{1,0:T(8,128)(2,1)S(1)}, bf16[256,768]{1,0:T(8,128)(2,1)}, u32[]{:S(2)}) copy-start(bf16[256,768]{1,0:T(8,128)(2,1)} %get-tuple-element.133) | copy-start | bytes 1179652
  121.1 50.3 %collective-permute-start.14 = (bf16[256,768]{1,0:T(8,128)(2,1)S(1)}, bf16[256,768]{1,0:T(8,128)(2,1)S(1)}, u32[]{:S(2)}, u32[]{:S(2)}) collective-permute-start(bf16[256,768]{1,0:T(8,128)(2,1)S(1)} %copy-done.28), channel_id=1, source_target_pairs={{0,15},{1,14},{2,13},{3,12},{4,11},{5,10},{6,9},{7,8},{8,7},{9,6},... | collective-permute-start | bytes 1179656 | tf_op jit(solution)/shard_map/ppermute | solution.py:173
  121.1 54.6 %collective-permute-start.12 = (bf16[256,768]{1,0:T(8,128)(2,1)S(1)}, bf16[256,768]{1,0:T(8,128)(2,1)S(1)}, u32[]{:S(2)}, u32[]{:S(2)}) collective-permute-start(bf16[256,768]{1,0:T(8,128)(2,1)S(1)} %copy-done.26), channel_id=1, source_target_pairs={{0,14},{1,15},{2,12},{3,13},{4,10},{5,11},{6,8},{7,9},{8,6},{9,7},... | collective-permute-start | bytes 1179656 | tf_op jit(solution)/shard_map/ppermute | solution.py:173
  123.8 51.1 %collective-permute-start.13 = (bf16[256,768]{1,0:T(8,128)(2,1)S(1)}, bf16[256,768]{1,0:T(8,128)(2,1)S(1)}, u32[]{:S(2)}, u32[]{:S(2)}) collective-permute-start(bf16[256,768]{1,0:T(8,128)(2,1)S(1)} %copy-done.27), channel_id=1, source_target_pairs={{0,7},{1,6},{2,5},{3,4},{4,3},{5,2},{6,1},{7,0},{8,15},{9,14},{10,... | collective-permute-start | bytes 1179656 | tf_op jit(solution)/shard_map/ppermute | solution.py:173
  124.4 15.0 %collective-permute-start.16 = (f16[256,256]{1,0:T(8,128)(2,1)S(1)}, f16[256,256]{1,0:T(8,128)(2,1)S(1)}, u32[]{:S(2)}, u32[]{:S(2)}) collective-permute-start(f16[256,256]{1,0:T(8,128)(2,1)S(1)} %convert_element_type.166), channel_id=1, source_target_pairs={{0,1},{1,0},{2,3},{3,2},{4,5},{5,4},{6,7},{7,6},{8,9},{9,8},{10,11... | collective-permute-start | bytes 393224 | tf_op jit(solution)/shard_map/ppermute | solution.py:173
  125.4 43.7 %collective-permute-start.15 = (f16[256,256]{1,0:T(8,128)(2,1)S(1)}, f16[256,256]{1,0:T(8,128)(2,1)S(1)}, u32[]{:S(2)}, u32[]{:S(2)}) collective-permute-start(f16[256,256]{1,0:T(8,128)(2,1)S(1)} %convert_element_type.163), channel_id=1, source_target_pairs={{0,8},{1,9},{2,10},{3,11},{4,12},{5,13},{6,14},{7,15},{8,0},{9,1},... | collective-permute-start | bytes 393224 | tf_op jit(solution)/shard_map/ppermute | solution.py:173
  139.4 52.5 %collective-permute-start.21 = (f16[256,256]{1,0:T(8,128)(2,1)S(1)}, f16[256,256]{1,0:T(8,128)(2,1)S(1)}, u32[]{:S(2)}, u32[]{:S(2)}) collective-permute-start(f16[256,256]{1,0:T(8,128)(2,1)S(1)} %convert_element_type.165), channel_id=1, source_target_pairs={{0,11},{1,10},{2,9},{3,8},{4,15},{5,14},{6,13},{7,12},{8,3},{9,2},... | collective-permute-start | bytes 393224 | tf_op jit(solution)/shard_map/ppermute | solution.py:173
  169.1 22.8 %collective-permute-start.20 = (f16[256,256]{1,0:T(8,128)(2,1)S(1)}, f16[256,256]{1,0:T(8,128)(2,1)S(1)}, u32[]{:S(2)}, u32[]{:S(2)}) collective-permute-start(f16[256,256]{1,0:T(8,128)(2,1)S(1)} %convert_element_type.162), channel_id=1, source_target_pairs={{0,3},{1,2},{2,1},{3,0},{4,7},{5,6},{6,5},{7,4},{8,11},{9,10},{10,... | collective-permute-start | bytes 393224 | tf_op jit(solution)/shard_map/ppermute | solution.py:173
  171.4 21.7 %collective-permute-start.19 = (f16[256,256]{1,0:T(8,128)(2,1)S(1)}, f16[256,256]{1,0:T(8,128)(2,1)S(1)}, u32[]{:S(2)}, u32[]{:S(2)}) collective-permute-start(f16[256,256]{1,0:T(8,128)(2,1)S(1)} %convert_element_type.175), channel_id=1, source_target_pairs={{0,10},{1,11},{2,8},{3,9},{4,14},{5,15},{6,12},{7,13},{8,2},{9,3},... | collective-permute-start | bytes 393224 | tf_op jit(solution)/shard_map/ppermute | solution.py:173
  174.9 22.0 %collective-permute-start.18 = (f16[256,256]{1,0:T(8,128)(2,1)S(1)}, f16[256,256]{1,0:T(8,128)(2,1)S(1)}, u32[]{:S(2)}, u32[]{:S(2)}) collective-permute-start(f16[256,256]{1,0:T(8,128)(2,1)S(1)} %convert_element_type.172), channel_id=1, source_target_pairs={{0,2},{1,3},{2,0},{3,1},{4,6},{5,7},{6,4},{7,5},{8,10},{9,11},{10,... | collective-permute-start | bytes 393224 | tf_op jit(solution)/shard_map/ppermute | solution.py:173
  175.7 21.2 %collective-permute-start.17 = (f16[256,256]{1,0:T(8,128)(2,1)S(1)}, f16[256,256]{1,0:T(8,128)(2,1)S(1)}, u32[]{:S(2)}, u32[]{:S(2)}) collective-permute-start(f16[256,256]{1,0:T(8,128)(2,1)S(1)} %convert_element_type.169), channel_id=1, source_target_pairs={{0,9},{1,8},{2,11},{3,10},{4,13},{5,12},{6,15},{7,14},{8,1},{9,0},... | collective-permute-start | bytes 393224 | tf_op jit(solution)/shard_map/ppermute | solution.py:173
  191.9 25.7 %collective-permute-start.26 = (f16[256,256]{1,0:T(8,128)(2,1)}, f16[256,256]{1,0:T(8,128)(2,1)}, u32[]{:S(2)}, u32[]{:S(2)}) collective-permute-start(f16[256,256]{1,0:T(8,128)(2,1)} %convert_element_type.179), channel_id=1, source_target_pairs={{0,6},{1,7},{2,4},{3,5},{4,2},{5,3},{6,0},{7,1},{8,14},{9,15},{10,... | collective-permute-start | bytes 393224 | tf_op jit(solution)/shard_map/ppermute | solution.py:173
  191.9 5.1 %copy-start.9 = (f16[256,256]{1,0:T(8,128)(2,1)}, f16[256,256]{1,0:T(8,128)(2,1)S(1)}, u32[]{:S(2)}) copy-start(f16[256,256]{1,0:T(8,128)(2,1)S(1)} %collective-permute-done.20) | copy-start | bytes 393220
  191.9 26.8 %collective-permute-start.25 = (f16[256,256]{1,0:T(8,128)(2,1)}, f16[256,256]{1,0:T(8,128)(2,1)}, u32[]{:S(2)}, u32[]{:S(2)}) collective-permute-start(f16[256,256]{1,0:T(8,128)(2,1)} %convert_element_type.177), channel_id=1, source_target_pairs={{0,13},{1,12},{2,15},{3,14},{4,9},{5,8},{6,11},{7,10},{8,5},{9,4},... | collective-permute-start | bytes 393224 | tf_op jit(solution)/shard_map/ppermute | solution.py:173
  193.1 18.9 %collective-permute-start.24 = (f16[256,256]{1,0:T(8,128)(2,1)S(1)}, f16[256,256]{1,0:T(8,128)(2,1)S(1)}, u32[]{:S(2)}, u32[]{:S(2)}) collective-permute-start(f16[256,256]{1,0:T(8,128)(2,1)S(1)} %convert_element_type.174), channel_id=1, source_target_pairs={{0,5},{1,4},{2,7},{3,6},{4,1},{5,0},{6,3},{7,2},{8,13},{9,12},{10,... | collective-permute-start | bytes 393224 | tf_op jit(solution)/shard_map/ppermute | solution.py:173
  196.9 13.8 %copy-start.11 = (f16[256,256]{1,0:T(8,128)(2,1)}, f16[256,256]{1,0:T(8,128)(2,1)S(1)}, u32[]{:S(2)}) copy-start(f16[256,256]{1,0:T(8,128)(2,1)S(1)} %collective-permute-done.18) | copy-start | bytes 393220
  196.9 15.3 %collective-permute-start.23 = (f16[256,256]{1,0:T(8,128)(2,1)S(1)}, f16[256,256]{1,0:T(8,128)(2,1)S(1)}, u32[]{:S(2)}, u32[]{:S(2)}) collective-permute-start(f16[256,256]{1,0:T(8,128)(2,1)S(1)} %convert_element_type.171), channel_id=1, source_target_pairs={{0,12},{1,13},{2,14},{3,15},{4,8},{5,9},{6,10},{7,11},{8,4},{9,5},... | collective-permute-start | bytes 393224 | tf_op jit(solution)/shard_map/ppermute | solution.py:173
  196.9 13.8 %copy-start.13 = (f16[256,256]{1,0:T(8,128)(2,1)}, f16[256,256]{1,0:T(8,128)(2,1)S(1)}, u32[]{:S(2)}) copy-start(f16[256,256]{1,0:T(8,128)(2,1)S(1)} %collective-permute-done.17) | copy-start | bytes 393220
  196.9 19.0 %collective-permute-start.22 = (f16[256,256]{1,0:T(8,128)(2,1)S(1)}, f16[256,256]{1,0:T(8,128)(2,1)S(1)}, u32[]{:S(2)}, u32[]{:S(2)}) collective-permute-start(f16[256,256]{1,0:T(8,128)(2,1)S(1)} %convert_element_type.168), channel_id=1, source_target_pairs={{0,4},{1,5},{2,6},{3,7},{4,0},{5,1},{6,2},{7,3},{8,12},{9,13},{10,... | collective-permute-start | bytes 393224 | tf_op jit(solution)/shard_map/ppermute | solution.py:173
  210.7 1.3 copy-start.4
  212.0 5.5 %copy-start.10 = (f16[256,256]{1,0:T(8,128)(2,1)S(1)}, f16[256,256]{1,0:T(8,128)(2,1)}, u32[]{:S(2)}) copy-start(f16[256,256]{1,0:T(8,128)(2,1)} %copy-done.9) | copy-start | bytes 393220
  212.0 7.6 %copy-start.12 = (f16[256,256]{1,0:T(8,128)(2,1)S(1)}, f16[256,256]{1,0:T(8,128)(2,1)}, u32[]{:S(2)}) copy-start(f16[256,256]{1,0:T(8,128)(2,1)} %copy-done.11) | copy-start | bytes 393220
  212.1 7.6 %copy-start.14 = (f16[256,256]{1,0:T(8,128)(2,1)S(1)}, f16[256,256]{1,0:T(8,128)(2,1)}, u32[]{:S(2)}) copy-start(f16[256,256]{1,0:T(8,128)(2,1)} %copy-done.13) | copy-start | bytes 393220
  212.1 3.8 copy-start.15
  212.1 11.3 %collective-permute-start.29 = (f16[256,256]{1,0:T(8,128)(2,1)S(1)}, f16[256,256]{1,0:T(8,128)(2,1)S(1)}, u32[]{:S(2)}, u32[]{:S(2)}) collective-permute-start(f16[256,256]{1,0:T(8,128)(2,1)S(1)} %convert_element_type.185), channel_id=1, source_target_pairs={{0,15},{1,14},{2,13},{3,12},{4,11},{5,10},{6,9},{7,8},{8,7},{9,6},... | collective-permute-start | bytes 393224 | tf_op jit(solution)/shard_map/ppermute | solution.py:173
  212.2 3.7 copy-start.17
  212.2 11.2 %collective-permute-start.28 = (f16[256,256]{1,0:T(8,128)(2,1)S(1)}, f16[256,256]{1,0:T(8,128)(2,1)S(1)}, u32[]{:S(2)}, u32[]{:S(2)}) collective-permute-start(f16[256,256]{1,0:T(8,128)(2,1)S(1)} %convert_element_type.183), channel_id=1, source_target_pairs={{0,7},{1,6},{2,5},{3,4},{4,3},{5,2},{6,1},{7,0},{8,15},{9,14},{10,... | collective-permute-start | bytes 393224 | tf_op jit(solution)/shard_map/ppermute | solution.py:173
  215.9 0.7 copy-start.19
  216.5 9.6 %collective-permute-start.27 = (f16[256,256]{1,0:T(8,128)(2,1)S(1)}, f16[256,256]{1,0:T(8,128)(2,1)S(1)}, u32[]{:S(2)}, u32[]{:S(2)}) collective-permute-start(f16[256,256]{1,0:T(8,128)(2,1)S(1)} %convert_element_type.181), channel_id=1, source_target_pairs={{0,14},{1,15},{2,12},{3,13},{4,10},{5,11},{6,8},{7,9},{8,6},{9,7},... | collective-permute-start | bytes 393224 | tf_op jit(solution)/shard_map/ppermute | solution.py:173
  216.5 3.2 copy-start.16
  217.4 2.3 copy-start.18
  217.4 2.3 copy-start.20
  217.6 8.6 %copy-start.5 = (f32[8,256,256]{2,1,0:T(8,128)S(1)}, f32[8,256,256]{2,1,0:T(8,128)}, u32[]{:S(2)}) copy-start(f32[8,256,256]{2,1,0:T(8,128)} %copy-done.4) | copy-start | bytes 6291460
  233.9 1.3 copy-start.3
  233.9 1.6 copy-start.6
  308.5 52.6 %all-to-all-start.1 = ((bf16[16,256,256]{2,1,0:T(8,128)(2,1)}), bf16[16,256,256]{2,1,0:T(8,128)(2,1)}, u32[]{:S(2)}, u32[]{:S(2)}) async-start(bf16[16,256,256]{2,1,0:T(8,128)(2,1)} %copy-done.3), calls=%async_computation.1 | async-start | bytes 4194304 | tf_op jit(solution)/shard_map/all_to_all | solution.py:317
  361.2 20.0 %copy-start.2 = (f32[16,256,256]{2,1,0:T(8,128)S(1)}, f32[16,256,256]{2,1,0:T(8,128)}, u32[]{:S(2)}) copy-start(f32[16,256,256]{2,1,0:T(8,128)} %convert_element_type.194.refs_4_) | copy-start | bytes 12582916
  361.2 20.0 %copy-start.7 = (f32[8,256,1]{2,1,0:T(8,128)S(1)}, f32[8,256,1]{2,1,0:T(8,128)}, u32[]{:S(2)}) copy-start(f32[8,256,1]{2,1,0:T(8,128)} %copy-done.6) | copy-start | bytes 24580

commit v4 on v3

--- a/solution.py
+++ b/solution.py
@@ -10,8 +10,8 @@
 C = 256
 TILE = 256
 ITERS = 2
-WINDOW = 4
-FLIGHT = 5
+WINDOW = 8
+FLIGHT = 8
 BATCH = 4
 VMEM = 40 * 1024 * 1024
 
@@ -24,15 +24,21 @@
 PEER, MINE, COUNT, LIST = 0, 1, 2, 3
 
 
-def take_kernel(table, src, *rest, first):
-    outs, sem = rest[:-1], rest[-1]
-    for k, out in enumerate(outs):
-
-        @pl.when(pl.program_id(0) == k)
-        def _():
-            copy = pltpu.make_async_copy(src.at[0], out, sem)
-            copy.start()
-            copy.wait()
+def take_kernel(mine, me, src, *rest, peers):
+    size = len(peers)
+    outs, stage, arrive, leave = rest[:size], rest[size], rest[size + 1], rest[size + 2]
+    loads = [
+        pltpu.make_async_copy(src.at[mine[me[0] ^ peer]], stage.at[k], arrive.at[k])
+        for k, peer in enumerate(peers)
+    ]
+    stores = [pltpu.make_async_copy(stage.at[k], out, leave.at[k]) for k, out in enumerate(outs)]
+    for load in loads:
+        load.start()
+    for load, store in zip(loads, stores):
+        load.wait()
+        store.start()
+    for store in stores:
+        store.wait()
 
 
 def batch_kernel(table, tiles, bias, meta, own, gin, *rest, slots, begin, scale):
@@ -173,19 +179,23 @@
         return lax.ppermute(value, "shard", [(q, q ^ order[k]) for q in range(n)])
 
     def take(slots):
-        first, size = slots[0], len(slots)
-        return pl.pallas_call(
-            lambda *refs: take_kernel(*refs, first=first),
-            grid_spec=pltpu.PrefetchScalarGridSpec(
-                num_scalar_prefetch=1,
-                grid=(size,),
-                in_specs=[pl.BlockSpec((1, TILE, features), lambda g, t: (t[first + g, MINE], 0, 0))],
+        size = len(slots)
+        return pl.pallas_call(
+            lambda *refs: take_kernel(*refs, peers=[order[k] for k in slots]),
+            grid_spec=pltpu.PrefetchScalarGridSpec(
+                num_scalar_prefetch=2,
+                grid=(1,),
+                in_specs=[ANY],
                 out_specs=[ANY] * size,
-                scratch_shapes=[pltpu.SemaphoreType.DMA],
+                scratch_shapes=[
+                    pltpu.VMEM((size, TILE, features), embed.dtype),
+                    pltpu.SemaphoreType.DMA((size,)),
+                    pltpu.SemaphoreType.DMA((size,)),
+                ],
             ),
             out_shape=[jax.ShapeDtypeStruct((TILE, features), embed.dtype)] * size,
             name="take",
-        )(sends, tiles)
+        )(mine, me.reshape(1), tiles)
 
     outgoing = list(take(list(range(WINDOW)))) + list(take(list(range(WINDOW, slot_count))))
     flying = []
@@ -332,7 +342,8 @@
     incoming = exchange(send)
     rounded = labels.astype(jnp.bfloat16)
     pushes = push_call(kernels, rounded)
-    back = exchange(pushes.astype(jnp.float16)).astype(jnp.float32)
+    pushes, incoming = lax.optimization_barrier((pushes.astype(jnp.float16), incoming))
+    back = exchange(pushes).astype(jnp.float32)
     gathered = gather_call(kernels, incoming)
     owners = jnp.where(shard_ids == me, -1, mine)
     (labels,) = update_call(owners, gathered, [back], [labels, degree])

time: 388 us -> 331 us (0.85)
  blocking collectives: 51.3 us -> 0 us
  starting transfers between devices: 47.3 us -> 58.6 us
  Pallas kernels: 122 us -> 114 us
  waiting for transfers between devices: 142 us -> 136 us
    all_to_all x1 -> x0, blocking collectives: 51.3 us -> none  [exchange(): lax.all_to_all(array, 'shard', split_axis=0, concat_axis=0, tiled=True)]
    ppermute x30, waiting for transfers between devices: 88.3 us -> 70.3 us  [swap(): return lax.ppermute(value, 'shard', [(q, q ^ order[k]) for q in range(n)])]
    pallas_call x2, Pallas kernels: 16.8 us -> 8.3 us  [take(): pl.pallas_call(lambda *refs: take_kernel(*refs, peers=[order[k] for k in...]
    all_to_all x1 -> x2, waiting for transfers between devices: 43.6 us -> 50.4 us  [exchange(): lax.all_to_all(array, 'shard', split_axis=0, concat_axis=0, tiled=True)]
    ppermute x30, starting transfers between devices: 36.4 us -> 42.5 us  [swap(): return lax.ppermute(value, 'shard', [(q, q ^ order[k]) for q in range(n)])]
    all_to_all x1, waiting for transfers between devices: 10.6 us -> 15.4 us  [body(): lax.all_to_all(meta[mine], 'shard', split_axis=0, concat_axis=0, tiled=True)]
    all_to_all x1 -> x2, starting transfers between devices: 5.12 us -> 9.25 us  [exchange(): lax.all_to_all(array, 'shard', split_axis=0, concat_axis=0, tiled=True)]
  transfers between devices with their start and end apart: 32 -> 33, of which waited for: 11 -> 12; matrix products, arithmetic and copies ran while one was open for 4% -> 4% of each run, Pallas kernels for 16% -> 29%
where the time goes in v4:
time: 331 us; the launch traced here: 329 us
  waiting for transfers between devices  136 us (41%)
  Pallas kernels  114 us (34%)
  starting transfers between devices  58.6 us (18%)
  other arithmetic  11.9 us (4%)
  local copies, waits for them, and re-layouts  7.61 us (2%)
    ppermute x30, waiting for transfers between devices, swap(): return lax.ppermute(value, 'shard', [(q, q ^ order[k]) for q in range(n)])  70.3 us
    pallas_call x4, Pallas kernels, batch_call(): pl.pallas_call(lambda *refs: batch_kernel(*refs, slots=slots, begin=slots...  50.8 us
    all_to_all x2, waiting for transfers between devices, exchange(): lax.all_to_all(array, 'shard', split_axis=0, concat_axis=0, tiled=True)  50.4 us
    ppermute x30, starting transfers between devices, swap(): return lax.ppermute(value, 'shard', [(q, q ^ order[k]) for q in range(n)])  42.5 us
    pallas_call x1, Pallas kernels, push_call(): pl.pallas_call(push_kernel, grid_spec=pltpu.PrefetchScalarGridSpec(num_sc...  21.6 us
    pallas_call x1, Pallas kernels, gather_call(): pl.pallas_call(gather_kernel, grid_spec=pltpu.PrefetchScalarGridSpec(num_...  19.8 us
    all_to_all x1, waiting for transfers between devices, body(): lax.all_to_all(meta[mine], 'shard', split_axis=0, concat_axis=0, tiled=True)  15.4 us
    pallas_call x2, Pallas kernels, update_call(): pl.pallas_call(lambda *refs: update_kernel(*refs, count=len(backs), first...  13.2 us
  transfers between devices with their start and end apart: 33, of which 12 were waited for; matrix products, arithmetic and copies ran while one was open for 4% of the time, Pallas kernels for 29%

profile of v4, /device:TPU:13, one launch (start us, length us, event | category | flops | bytes accessed | tf_op | source)
XLA Modules:
  0.0 328.8 jit_solution(16734872324192787574)
XLA Ops:
  0.0 4.4 %take.3 = (bf16[256,768]{1,0:T(8,128)(2,1)}, bf16[256,768]{1,0:T(8,128)(2,1)}, bf16[256,768]{1,0:T(8,128)(2,1)}, bf16[256,768]{1,0:T(8,128)(2,1)}, bf16[256,768]...) custom-call(s32[16]{0:T(128)} %bitcast.26, s32[1]{0:T(128)} %bitcast.9.refs_1_, ...), custom_call_target="tpu_custom_call" | custom-call | tf_op jit(solution)/shard_map/take/pallas_call | solution.py:183
  4.4 2.1 collective-permute-start
  6.5 1.4 collective-permute-start.1
  7.9 0.7 multiply_reduce_fusion
  8.7 1.2 gather_fusion
  9.9 6.9 %all-to-all-start = ((f32[16,2,256]{2,1,0:T(2,128)}), f32[16,2,256]{2,1,0:T(2,128)S(1)}, u32[]{:S(2)}, u32[]{:S(2)}) async-start(f32[16,2,256]{2,1,0:T(2,128)} %gather_fusion), calls=%async_computation | async-start | bytes 65536 | tf_op jit(solution)/shard_map/all_to_all | solution.py:212
  16.8 0.5 collective-permute-start.5
  17.3 0.7 fusion.2
  18.0 0.2 select_reduce_fusion.1.refs_0_
  18.2 0.7 broadcast_compare_fusion.2
  18.9 0.7 iota_compare_fusion.5
  19.6 0.4 and_reduce_fusion
  20.2 3.9 %take.2 = (bf16[256,768]{1,0:T(8,128)(2,1)}, bf16[256,768]{1,0:T(8,128)(2,1)}, bf16[256,768]{1,0:T(8,128)(2,1)}, bf16[256,768]{1,0:T(8,128)(2,1)}, bf16[256,768]...) custom-call(s32[16]{0:T(128)} %bitcast.27, s32[1]{0:T(128)} %bitcast.9.refs_1_, ...), custom_call_target="tpu_custom_call" | custom-call | tf_op jit(solution)/shard_map/take/pallas_call | solution.py:183
  24.1 0.9 mul.54.refs_2_
  25.4 0.7 select_convert_fusion.1.refs_4_
  26.2 15.4 %all-to-all-done.refs_3_ = f32[16,2,256]{2,1,0:T(2,128)S(1)} async-done(((f32[16,2,256]{2,1,0:T(2,128)}), f32[16,2,256]{2,1,0:T(2,128)S(1)}, u32[]{:S(2)}, u32[]{:S(2)}) %all-to-all-start) | async-done | bytes 32800 | tf_op jit(solution)/shard_map/all_to_all | solution.py:212
  41.6 4.0 %collective-permute-start.4 = (bf16[256,768]{1,0:T(8,128)(2,1)}, bf16[256,768]{1,0:T(8,128)(2,1)S(1)}, u32[]{:S(2)}, u32[]{:S(2)}) collective-permute-start(bf16[256,768]{1,0:T(8,128)(2,1)} %get-tuple-element.98), channel_id=1, source_target_pairs={{0,10},{1,11},{2,8},{3,9},{4,14},{5,15},{6,12},{7,13},{8,2},{9,3},... | collective-permute-start | bytes 1179656 | tf_op jit(solution)/shard_map/ppermute | solution.py:179
  45.6 1.4 select_convert_fusion.refs_10_.refs_11_.refs_12_.refs_13_.refs_9_
  47.1 0.4 collective-permute-start.6
  47.5 0.7 collective-permute-start.7
  48.2 23.2 %collective-permute-done.4.refs_6_ = bf16[256,768]{1,0:T(8,128)(2,1)S(1)} collective-permute-done((bf16[256,768]{1,0:T(8,128)(2,1)}, bf16[256,768]{1,0:T(8,128)(2,1)S(1)}, u32[]{:S(2)}, u32[]{:S(2)}) %collective-permute-start.4) | collective-permute-done | bytes 393248 | tf_op jit(solution)/shard_map/ppermute | solution.py:179
  71.4 5.5 %collective-permute-start.11 = (bf16[256,768]{1,0:T(8,128)(2,1)S(1)}, bf16[256,768]{1,0:T(8,128)(2,1)S(1)}, u32[]{:S(2)}, u32[]{:S(2)}) collective-permute-start(bf16[256,768]{1,0:T(8,128)(2,1)S(1)} %copy-done.19), channel_id=1, source_target_pairs={{0,6},{1,7},{2,4},{3,5},{4,2},{5,3},{6,0},{7,1},{8,14},{9,15},{10,... | collective-permute-start | bytes 1179656 | tf_op jit(solution)/shard_map/ppermute | solution.py:179
  76.9 0.2 broadcast_in_dim.91.refs_5_
  77.2 13.0 %batch.4 = (bf16[128,256,256]{2,1,0:T(8,128)(2,1)}, f32[8,256,256]{2,1,0:T(8,128)S(1)}, f32[256,256]{1,0:T(8,128)S(1)}, f32[256,256]{1,0:T(8,128)S(1)}, f32[256,256]{1,0:T(8,128)S(1)}, /*index=5*/f32[256,256]{1,0:T(8,128)S(1)}) custom-call(s32[15,11]{1,0:T(8,128)S(1)} %pad_add_fusion.refs_0_.table, bf16[8,256,768]{2,1,0:T(8,128)(2,1)S(1)} %bitcast.22, ...), custom_call_target="tpu_custom_call" | custom-call | flops 10000000000 | bytes 30000000 | tf_op jit(solution)/shard_map/batch/pallas_call | solution.py:243
  90.2 4.9 %collective-permute-start.9 = (bf16[256,768]{1,0:T(8,128)(2,1)S(1)}, bf16[256,768]{1,0:T(8,128)(2,1)S(1)}, u32[]{:S(2)}, u32[]{:S(2)}) collective-permute-start(bf16[256,768]{1,0:T(8,128)(2,1)S(1)} %copy-done.16), channel_id=1, source_target_pairs={{0,5},{1,4},{2,7},{3,6},{4,1},{5,0},{6,3},{7,2},{8,13},{9,12},{10,... | collective-permute-start | bytes 1179656 | tf_op jit(solution)/shard_map/ppermute | solution.py:179
  95.1 17.7 %collective-permute-done.13.refs_7_ = bf16[256,768]{1,0:T(8,128)(2,1)S(1)} collective-permute-done((bf16[256,768]{1,0:T(8,128)(2,1)}, bf16[256,768]{1,0:T(8,128)(2,1)S(1)}, u32[]{:S(2)}, u32[]{:S(2)}) %collective-permute-start.13) | collective-permute-done | bytes 393248 | tf_op jit(solution)/shard_map/ppermute | solution.py:179
  112.8 2.2 collective-permute-start.12
  115.1 10.6 %batch.5 = (bf16[128,256,256]{2,1,0:T(8,128)(2,1)}, f32[8,256,256]{2,1,0:T(8,128)S(1)}, f32[256,256]{1,0:T(8,128)S(1)}, f32[256,256]{1,0:T(8,128)S(1)}, f32[256,256]{1,0:T(8,128)S(1)}, /*index=5*/f32[256,256]{1,0:T(8,128)S(1)}) custom-call(s32[15,11]{1,0:T(8,128)S(1)} %pad_add_fusion.refs_0_.table, ...), custom_call_target="tpu_custom_call", output_to_operand_aliasing={{0}: (14, {})} | custom-call | flops 10000000000 | bytes 30000000 | tf_op jit(solution)/shard_map/batch/pallas_call | solution.py:243
  125.9 6.5 %collective-permute-done.12.refs_6_ = bf16[256,768]{1,0:T(8,128)(2,1)S(1)} collective-permute-done((bf16[256,768]{1,0:T(8,128)(2,1)S(1)}, bf16[256,768]{1,0:T(8,128)(2,1)S(1)}, u32[]{:S(2)}, u32[]{:S(2)}) %collective-permute-start.12) | collective-permute-done | bytes 393248 | tf_op jit(solution)/shard_map/ppermute | solution.py:179
  132.4 3.4 %collective-permute-start.14 = (bf16[256,768]{1,0:T(8,128)(2,1)S(1)}, bf16[256,768]{1,0:T(8,128)(2,1)S(1)}, u32[]{:S(2)}, u32[]{:S(2)}) collective-permute-start(bf16[256,768]{1,0:T(8,128)(2,1)S(1)} %copy-done.15), channel_id=1, source_target_pairs={{0,15},{1,14},{2,13},{3,12},{4,11},{5,10},{6,9},{7,8},{8,7},{9,6},... | collective-permute-start | bytes 1179656 | tf_op jit(solution)/shard_map/ppermute | solution.py:179
  135.8 2.4 collective-permute-start.21
  138.2 1.4 collective-permute-start.20
  139.6 3.3 %collective-permute-start.19 = (f16[256,256]{1,0:T(8,128)(2,1)S(1)}, f16[256,256]{1,0:T(8,128)(2,1)S(1)}, u32[]{:S(2)}, u32[]{:S(2)}) collective-permute-start(f16[256,256]{1,0:T(8,128)(2,1)S(1)} %convert_element_type.175), channel_id=1, source_target_pairs={{0,10},{1,11},{2,8},{3,9},{4,14},{5,15},{6,12},{7,13},{8,2},{9,3},... | collective-permute-start | bytes 393224 | tf_op jit(solution)/shard_map/ppermute | solution.py:179
  143.0 15.4 %batch.6 = (bf16[128,256,256]{2,1,0:T(8,128)(2,1)}, f32[8,256,256]{2,1,0:T(8,128)S(1)}, f32[256,256]{1,0:T(8,128)S(1)}, f32[256,256]{1,0:T(8,128)S(1)}, f32[256,256]{1,0:T(8,128)S(1)}, /*index=5*/f32[256,256]{1,0:T(8,128)S(1)}) custom-call(s32[15,11]{1,0:T(8,128)S(1)} %pad_add_fusion.refs_0_.table, ...), custom_call_target="tpu_custom_call", output_to_operand_aliasing={{0}: (14, {})} | custom-call | flops 10000000000 | bytes 30000000 | tf_op jit(solution)/shard_map/batch/pallas_call | solution.py:243
  158.3 4.0 %collective-permute-done.14.refs_8_ = bf16[256,768]{1,0:T(8,128)(2,1)S(1)} collective-permute-done((bf16[256,768]{1,0:T(8,128)(2,1)S(1)}, bf16[256,768]{1,0:T(8,128)(2,1)S(1)}, u32[]{:S(2)}, u32[]{:S(2)}) %collective-permute-start.14) | collective-permute-done | bytes 393248 | tf_op jit(solution)/shard_map/ppermute | solution.py:179
  162.3 0.8 collective-permute-start.18
  163.1 11.9 %batch.7 = (bf16[128,256,256]{2,1,0:T(8,128)(2,1)}, f32[8,256,256]{2,1,0:T(8,128)S(1)}, f32[256,256]{1,0:T(8,128)S(1)}, f32[256,256]{1,0:T(8,128)S(1)}, f32[256,256]{1,0:T(8,128)S(1)}) custom-call(s32[15,11]{1,0:T(8,128)S(1)} %pad_add_fusion.refs_0_.table, bf16[8,256,768]{2,1,0:T(8,128)(2,1)S(1)} %bitcast.25, ...), custom_call_target="tpu_custom_call", output_to_operand_aliasing={{0}: (12, {})} | custom-call | flops 10000000000 | bytes 30000000 | tf_op jit(solution)/shard_map/batch/pallas_call | solution.py:243
  175.1 1.9 collective-permute-start.16
  177.1 3.4 %collective-permute-start.22 = (f16[256,256]{1,0:T(8,128)(2,1)S(1)}, f16[256,256]{1,0:T(8,128)(2,1)S(1)}, u32[]{:S(2)}, u32[]{:S(2)}) collective-permute-start(f16[256,256]{1,0:T(8,128)(2,1)S(1)} %convert_element_type.183), channel_id=1, source_target_pairs={{0,4},{1,5},{2,6},{3,7},{4,0},{5,1},{6,2},{7,3},{8,12},{9,13},{10,... | collective-permute-start | bytes 393224 | tf_op jit(solution)/shard_map/ppermute | solution.py:179
  180.6 0.3 collective-permute-done.17
  180.9 1.4 collective-permute-start.28
  182.3 1.7 collective-permute-start.27
  184.0 4.5 %collective-permute-done.23 = f16[256,256]{1,0:T(8,128)(2,1)S(1)} collective-permute-done((f16[256,256]{1,0:T(8,128)(2,1)S(1)}, f16[256,256]{1,0:T(8,128)(2,1)S(1)}, u32[]{:S(2)}, u32[]{:S(2)}) %collective-permute-start.23) | collective-permute-done | bytes 131104 | tf_op jit(solution)/shard_map/ppermute | solution.py:179
  188.5 0.8 collective-permute-start.25
  189.3 5.5 %collective-permute-done.29 = f16[256,256]{1,0:T(8,128)(2,1)S(1)} collective-permute-done((f16[256,256]{1,0:T(8,128)(2,1)S(1)}, f16[256,256]{1,0:T(8,128)(2,1)S(1)}, u32[]{:S(2)}, u32[]{:S(2)}) %collective-permute-start.29) | collective-permute-done | bytes 131104 | tf_op jit(solution)/shard_map/ppermute | solution.py:179
  194.9 0.9 convert_element_type.195.refs_3_
  196.1 5.4 %collective-permute-done.27 = f16[256,256]{1,0:T(8,128)(2,1)S(1)} collective-permute-done((f16[256,256]{1,0:T(8,128)(2,1)S(1)}, f16[256,256]{1,0:T(8,128)(2,1)S(1)}, u32[]{:S(2)}, u32[]{:S(2)}) %collective-permute-start.27) | collective-permute-done | bytes 131104 | tf_op jit(solution)/shard_map/ppermute | solution.py:179
  201.6 3.1 collective-permute-done.25
  204.7 0.9 convert_element_type.187.refs_14_
  205.6 0.9 convert_element_type.186.refs_13_
  206.6 7.7 %update.2 = (f32[8,256,1]{2,1,0:T(8,128)S(1)}, f32[8,256,256]{2,1,0:T(8,128)S(1)}, bf16[16,256,256]{2,1,0:T(8,128)(2,1)S(1)}) custom-call(s32[15]{0:T(128)S(1)} %select_reduce_fusion.1.refs_0_, s32[16]{0:T(128)S(1)} %bitcast.29, f32[8,256,256]{2,1,0:T(8,128)S(1)} %copy-done.6, f32[8,256,1]{2,1,0:T(8,128)S(1)} %convert_element_type.195.refs_3_, ...), custom_call_target="tpu_custom_call" | custom-call | tf_op jit(solution)/shard_map/update/pallas_call | solution.py:312
  214.3 1.3 copy-done.4
  215.6 1.0 copy-done.7
  216.6 4.3 %all-to-all-start.1 = ((bf16[16,256,256]{2,1,0:T(8,128)(2,1)}), bf16[16,256,256]{2,1,0:T(8,128)(2,1)}, u32[]{:S(2)}, u32[]{:S(2)}) async-start(bf16[16,256,256]{2,1,0:T(8,128)(2,1)} %copy-done.4), calls=%async_computation.1 | async-start | bytes 4194304 | tf_op jit(solution)/shard_map/all_to_all | solution.py:327
  221.0 21.6 %push.1 = f32[16,256,256]{2,1,0:T(8,128)S(1)} custom-call(s32[15,11]{1,0:T(8,128)S(1)} %pad_add_fusion.refs_0_.table, bf16[128,256,256]{2,1,0:T(8,128)(2,1)} %get-tuple-element.119.kref, bf16[8,256,256]{2,1,0:T(8,128)(2,1)S(1)} %convert_element_type.192.own), custom_call_target="tpu_custom_call" | custom-call | flops 20000000000 | bytes 60000000 | tf_op jit(solution)/shard_map/push/pallas_call | solution.py:265
  242.6 1.7 convert_element_type.193
  244.3 24.0 %all-to-all-done.1.lrem = bf16[16,256,256]{2,1,0:T(8,128)(2,1)} async-done(((bf16[16,256,256]{2,1,0:T(8,128)(2,1)}), bf16[16,256,256]{2,1,0:T(8,128)(2,1)}, u32[]{:S(2)}, u32[]{:S(2)}) %all-to-all-start.1) | async-done | bytes 2097184 | tf_op jit(solution)/shard_map/all_to_all | solution.py:327
  268.3 4.9 %all-to-all-start.2 = ((f16[16,256,256]{2,1,0:T(8,128)(2,1)}), f16[16,256,256]{2,1,0:T(8,128)(2,1)}, u32[]{:S(2)}, u32[]{:S(2)}) async-start(f16[16,256,256]{2,1,0:T(8,128)(2,1)} %convert_element_type.193), calls=%async_computation.2 | async-start | bytes 4194304 | tf_op jit(solution)/shard_map/all_to_all | solution.py:327
  273.3 19.8 %gather.7.refs_2_ = f32[8,256,256]{2,1,0:T(8,128)S(1)} custom-call(s32[15,11]{1,0:T(8,128)S(1)} %pad_add_fusion.refs_0_.table, bf16[128,256,256]{2,1,0:T(8,128)(2,1)} %get-tuple-element.119.kref, bf16[16,256,256]{2,1,0:T(8,128)(2,1)} %all-to-all-done.1.lrem), custom_call_target="tpu_custom_call" | custom-call | flops 20000000000 | bytes 60000000 | tf_op jit(solution)/shard_map/gather/pallas_call | solution.py:280
  293.1 1.3 copy-done.2
  294.4 26.4 %all-to-all-done.2 = f16[16,256,256]{2,1,0:T(8,128)(2,1)} async-done(((f16[16,256,256]{2,1,0:T(8,128)(2,1)}), f16[16,256,256]{2,1,0:T(8,128)(2,1)}, u32[]{:S(2)}, u32[]{:S(2)}) %all-to-all-start.2) | async-done | bytes 2097184 | tf_op jit(solution)/shard_map/all_to_all | solution.py:327
  320.8 2.1 convert_element_type.194.refs_4_
  323.0 0.3 copy-done.8
  323.3 5.5 %update.3 = f32[8,256,256]{2,1,0:T(8,128)} custom-call(s32[16]{0:T(128)S(1)} %compare_select_fusion.1.refs_0_, s32[16]{0:T(128)S(1)} %bitcast.30, f32[8,256,256]{2,1,0:T(8,128)S(1)} %copy-done.3, f32[8,256,1]{2,1,0:T(8,128)S(1)} %convert_element_type.195.refs_3_, f32[16,256,256]{2,1,0:T(8,128)S(1)} %convert_element_type.194.refs_4_, ...), custom_call_target="tpu_custom_call" | custom-call | tf_op jit(solution)/shard_map/update/pallas_call | solution.py:312
  (120 shorter events, 1.7 us)
Async XLA Ops:
  0.0 7.9 %copy-start = (bf16[2048,768]{1,0:T(8,128)(2,1)S(1)}, bf16[2048,768]{1,0:T(8,128)(2,1)}, u32[]{:S(2)}) copy-start(bf16[2048,768]{1,0:T(8,128)(2,1)} %param.7) | copy-start | bytes 9437188
  4.4 4.2 %copy-start.9 = (s32[1,16]{1,0:T(1,128)S(1)}, s32[1,16]{1,0:T(1,128)}, u32[]{:S(2)}) copy-start(s32[1,16]{1,0:T(1,128)} %param.10) | copy-start | bytes 196
  4.4 4.3 %copy-start.13 = (s32[2048]{0:T(1024)S(1)}, s32[2048]{0:T(1024)}, u32[]{:S(2)}) copy-start(s32[2048]{0:T(1024)} %param.9) | copy-start | bytes 24580
  4.4 4.3 %copy-start.14 = (s32[2048]{0:T(1024)S(1)}, s32[2048]{0:T(1024)}, u32[]{:S(2)}) copy-start(s32[2048]{0:T(1024)} %param.8) | copy-start | bytes 24580
  4.4 37.2 %collective-permute-start = (bf16[256,768]{1,0:T(8,128)(2,1)}, bf16[256,768]{1,0:T(8,128)(2,1)S(1)}, u32[]{:S(2)}, u32[]{:S(2)}) collective-permute-start(bf16[256,768]{1,0:T(8,128)(2,1)} %get-tuple-element.85), channel_id=1, source_target_pairs={{0,8},{1,9},{2,10},{3,11},{4,12},{5,13},{6,14},{7,15},{8,0},{9,1},... | collective-permute-start | bytes 1179656 | tf_op jit(solution)/shard_map/ppermute | solution.py:179
  6.5 40.5 %collective-permute-start.1 = (bf16[256,768]{1,0:T(8,128)(2,1)}, bf16[256,768]{1,0:T(8,128)(2,1)}, u32[]{:S(2)}, u32[]{:S(2)}) collective-permute-start(bf16[256,768]{1,0:T(8,128)(2,1)} %get-tuple-element.88), channel_id=1, source_target_pairs={{0,1},{1,0},{2,3},{3,2},{4,5},{5,4},{6,7},{7,6},{8,9},{9,8},{10,11... | collective-permute-start | bytes 1179656 | tf_op jit(solution)/shard_map/ppermute | solution.py:179
  7.9 39.5 %collective-permute-start.2 = (bf16[256,768]{1,0:T(8,128)(2,1)}, bf16[256,768]{1,0:T(8,128)(2,1)}, u32[]{:S(2)}, u32[]{:S(2)}) collective-permute-start(bf16[256,768]{1,0:T(8,128)(2,1)} %get-tuple-element.91), channel_id=1, source_target_pairs={{0,9},{1,8},{2,11},{3,10},{4,13},{5,12},{6,15},{7,14},{8,1},{9,0},... | collective-permute-start | bytes 1179656 | tf_op jit(solution)/shard_map/ppermute | solution.py:179
  7.9 40.3 %collective-permute-start.3 = (bf16[256,768]{1,0:T(8,128)(2,1)}, bf16[256,768]{1,0:T(8,128)(2,1)}, u32[]{:S(2)}, u32[]{:S(2)}) collective-permute-start(bf16[256,768]{1,0:T(8,128)(2,1)} %get-tuple-element.94), channel_id=1, source_target_pairs={{0,2},{1,3},{2,0},{3,1},{4,6},{5,7},{6,4},{7,5},{8,10},{9,11},{10,... | collective-permute-start | bytes 1179656 | tf_op jit(solution)/shard_map/ppermute | solution.py:179
  9.9 31.7 %all-to-all-start = ((f32[16,2,256]{2,1,0:T(2,128)}), f32[16,2,256]{2,1,0:T(2,128)S(1)}, u32[]{:S(2)}, u32[]{:S(2)}) async-start(f32[16,2,256]{2,1,0:T(2,128)} %gather_fusion), calls=%async_computation | async-start | bytes 65536 | tf_op jit(solution)/shard_map/all_to_all | solution.py:212
  16.8 31.4 %collective-permute-start.5 = (bf16[256,768]{1,0:T(8,128)(2,1)}, bf16[256,768]{1,0:T(8,128)(2,1)S(1)}, u32[]{:S(2)}, u32[]{:S(2)}) collective-permute-start(bf16[256,768]{1,0:T(8,128)(2,1)} %get-tuple-element.101), channel_id=1, source_target_pairs={{0,3},{1,2},{2,1},{3,0},{4,7},{5,6},{6,5},{7,4},{8,11},{9,10},{10,... | collective-permute-start | bytes 1179656 | tf_op jit(solution)/shard_map/ppermute | solution.py:179
  41.6 29.8 %copy-start.18 = (bf16[256,768]{1,0:T(8,128)(2,1)S(1)}, bf16[256,768]{1,0:T(8,128)(2,1)}, u32[]{:S(2)}) copy-start(bf16[256,768]{1,0:T(8,128)(2,1)} %get-tuple-element.111) | copy-start | bytes 1179652
  41.6 29.8 %copy-start.19 = (bf16[256,768]{1,0:T(8,128)(2,1)S(1)}, bf16[256,768]{1,0:T(8,128)(2,1)}, u32[]{:S(2)}) copy-start(bf16[256,768]{1,0:T(8,128)(2,1)} %get-tuple-element.112) | copy-start | bytes 1179652
  41.6 29.8 %collective-permute-start.4 = (bf16[256,768]{1,0:T(8,128)(2,1)}, bf16[256,768]{1,0:T(8,128)(2,1)S(1)}, u32[]{:S(2)}, u32[]{:S(2)}) collective-permute-start(bf16[256,768]{1,0:T(8,128)(2,1)} %get-tuple-element.98), channel_id=1, source_target_pairs={{0,10},{1,11},{2,8},{3,9},{4,14},{5,15},{6,12},{7,13},{8,2},{9,3},... | collective-permute-start | bytes 1179656 | tf_op jit(solution)/shard_map/ppermute | solution.py:179
  45.6 31.5 %copy-start.1 = (bf16[2048,768]{1,0:T(8,128)(2,1)S(1)}, bf16[2048,768]{1,0:T(8,128)(2,1)}, u32[]{:S(2)}) copy-start(bf16[2048,768]{1,0:T(8,128)(2,1)} %param.7) | copy-start | bytes 9437188
  47.1 43.1 %collective-permute-start.6 = (bf16[256,768]{1,0:T(8,128)(2,1)}, bf16[256,768]{1,0:T(8,128)(2,1)S(1)}, u32[]{:S(2)}, u32[]{:S(2)}) collective-permute-start(bf16[256,768]{1,0:T(8,128)(2,1)} %get-tuple-element.104), channel_id=1, source_target_pairs={{0,11},{1,10},{2,9},{3,8},{4,15},{5,14},{6,13},{7,12},{8,3},{9,2},... | collective-permute-start | bytes 1179656 | tf_op jit(solution)/shard_map/ppermute | solution.py:179
  47.5 42.7 %collective-permute-start.7 = (bf16[256,768]{1,0:T(8,128)(2,1)}, bf16[256,768]{1,0:T(8,128)(2,1)S(1)}, u32[]{:S(2)}, u32[]{:S(2)}) collective-permute-start(bf16[256,768]{1,0:T(8,128)(2,1)} %get-tuple-element.106), channel_id=1, source_target_pairs={{0,4},{1,5},{2,6},{3,7},{4,0},{5,1},{6,2},{7,3},{8,12},{9,13},{10,... | collective-permute-start | bytes 1179656 | tf_op jit(solution)/shard_map/ppermute | solution.py:179
  71.4 64.4 %collective-permute-start.10 = (bf16[256,768]{1,0:T(8,128)(2,1)S(1)}, bf16[256,768]{1,0:T(8,128)(2,1)S(1)}, u32[]{:S(2)}, u32[]{:S(2)}) collective-permute-start(bf16[256,768]{1,0:T(8,128)(2,1)S(1)} %copy-done.18), channel_id=1, source_target_pairs={{0,13},{1,12},{2,15},{3,14},{4,9},{5,8},{6,11},{7,10},{8,5},{9,4},... | collective-permute-start | bytes 1179656 | tf_op jit(solution)/shard_map/ppermute | solution.py:179
  71.4 64.4 %collective-permute-start.11 = (bf16[256,768]{1,0:T(8,128)(2,1)S(1)}, bf16[256,768]{1,0:T(8,128)(2,1)S(1)}, u32[]{:S(2)}, u32[]{:S(2)}) collective-permute-start(bf16[256,768]{1,0:T(8,128)(2,1)S(1)} %copy-done.19), channel_id=1, source_target_pairs={{0,6},{1,7},{2,4},{3,5},{4,2},{5,3},{6,0},{7,1},{8,14},{9,15},{10,... | collective-permute-start | bytes 1179656 | tf_op jit(solution)/shard_map/ppermute | solution.py:179
  76.9 35.9 %collective-permute-start.13 = (bf16[256,768]{1,0:T(8,128)(2,1)}, bf16[256,768]{1,0:T(8,128)(2,1)S(1)}, u32[]{:S(2)}, u32[]{:S(2)}) collective-permute-start(bf16[256,768]{1,0:T(8,128)(2,1)} %get-tuple-element.116), channel_id=1, source_target_pairs={{0,7},{1,6},{2,5},{3,4},{4,3},{5,2},{6,1},{7,0},{8,15},{9,14},{10,... | collective-permute-start | bytes 1179656 | tf_op jit(solution)/shard_map/ppermute | solution.py:179
  77.1 13.0 %copy-start.17 = (bf16[256,768]{1,0:T(8,128)(2,1)S(1)}, bf16[256,768]{1,0:T(8,128)(2,1)}, u32[]{:S(2)}) copy-start(bf16[256,768]{1,0:T(8,128)(2,1)} %get-tuple-element.109) | copy-start | bytes 1179652
  77.1 13.0 %copy-start.16 = (bf16[256,768]{1,0:T(8,128)(2,1)S(1)}, bf16[256,768]{1,0:T(8,128)(2,1)}, u32[]{:S(2)}) copy-start(bf16[256,768]{1,0:T(8,128)(2,1)} %get-tuple-element.110) | copy-start | bytes 1179652
  77.1 35.7 %copy-start.20 = (bf16[256,768]{1,0:T(8,128)(2,1)S(1)}, bf16[256,768]{1,0:T(8,128)(2,1)}, u32[]{:S(2)}) copy-start(bf16[256,768]{1,0:T(8,128)(2,1)} %get-tuple-element.115) | copy-start | bytes 1179652
  90.1 48.1 %collective-permute-start.8 = (bf16[256,768]{1,0:T(8,128)(2,1)S(1)}, bf16[256,768]{1,0:T(8,128)(2,1)S(1)}, u32[]{:S(2)}, u32[]{:S(2)}) collective-permute-start(bf16[256,768]{1,0:T(8,128)(2,1)S(1)} %copy-done.17), channel_id=1, source_target_pairs={{0,12},{1,13},{2,14},{3,15},{4,8},{5,9},{6,10},{7,11},{8,4},{9,5},... | collective-permute-start | bytes 1179656 | tf_op jit(solution)/shard_map/ppermute | solution.py:179
  90.2 49.5 %collective-permute-start.9 = (bf16[256,768]{1,0:T(8,128)(2,1)S(1)}, bf16[256,768]{1,0:T(8,128)(2,1)S(1)}, u32[]{:S(2)}, u32[]{:S(2)}) collective-permute-start(bf16[256,768]{1,0:T(8,128)(2,1)S(1)} %copy-done.16), channel_id=1, source_target_pairs={{0,5},{1,4},{2,7},{3,6},{4,1},{5,0},{6,3},{7,2},{8,13},{9,12},{10,... | collective-permute-start | bytes 1179656 | tf_op jit(solution)/shard_map/ppermute | solution.py:179
  112.8 19.5 %collective-permute-start.12 = (bf16[256,768]{1,0:T(8,128)(2,1)S(1)}, bf16[256,768]{1,0:T(8,128)(2,1)S(1)}, u32[]{:S(2)}, u32[]{:S(2)}) collective-permute-start(bf16[256,768]{1,0:T(8,128)(2,1)S(1)} %copy-done.20), channel_id=1, source_target_pairs={{0,14},{1,15},{2,12},{3,13},{4,10},{5,11},{6,8},{7,9},{8,6},{9,7},... | collective-permute-start | bytes 1179656 | tf_op jit(solution)/shard_map/ppermute | solution.py:179
  125.7 6.7 %copy-start.15 = (bf16[256,768]{1,0:T(8,128)(2,1)S(1)}, bf16[256,768]{1,0:T(8,128)(2,1)}, u32[]{:S(2)}) copy-start(bf16[256,768]{1,0:T(8,128)(2,1)} %get-tuple-element.117) | copy-start | bytes 1179652
  132.4 30.0 %collective-permute-start.14 = (bf16[256,768]{1,0:T(8,128)(2,1)S(1)}, bf16[256,768]{1,0:T(8,128)(2,1)S(1)}, u32[]{:S(2)}, u32[]{:S(2)}) collective-permute-start(bf16[256,768]{1,0:T(8,128)(2,1)S(1)} %copy-done.15), channel_id=1, source_target_pairs={{0,15},{1,14},{2,13},{3,12},{4,11},{5,10},{6,9},{7,8},{8,7},{9,6},... | collective-permute-start | bytes 1179656 | tf_op jit(solution)/shard_map/ppermute | solution.py:179
  135.8 39.2 %collective-permute-start.15 = (f16[256,256]{1,0:T(8,128)(2,1)S(1)}, f16[256,256]{1,0:T(8,128)(2,1)S(1)}, u32[]{:S(2)}, u32[]{:S(2)}) collective-permute-start(f16[256,256]{1,0:T(8,128)(2,1)S(1)} %convert_element_type.163), channel_id=1, source_target_pairs={{0,8},{1,9},{2,10},{3,11},{4,12},{5,13},{6,14},{7,15},{8,0},{9,1},... | collective-permute-start | bytes 393224 | tf_op jit(solution)/shard_map/ppermute | solution.py:179
  135.8 39.3 %collective-permute-start.21 = (f16[256,256]{1,0:T(8,128)(2,1)S(1)}, f16[256,256]{1,0:T(8,128)(2,1)S(1)}, u32[]{:S(2)}, u32[]{:S(2)}) collective-permute-start(f16[256,256]{1,0:T(8,128)(2,1)S(1)} %convert_element_type.181), channel_id=1, source_target_pairs={{0,11},{1,10},{2,9},{3,8},{4,15},{5,14},{6,13},{7,12},{8,3},{9,2},... | collective-permute-start | bytes 393224 | tf_op jit(solution)/shard_map/ppermute | solution.py:179
  138.2 38.9 %collective-permute-start.20 = (f16[256,256]{1,0:T(8,128)(2,1)S(1)}, f16[256,256]{1,0:T(8,128)(2,1)S(1)}, u32[]{:S(2)}, u32[]{:S(2)}) collective-permute-start(f16[256,256]{1,0:T(8,128)(2,1)S(1)} %convert_element_type.178), channel_id=1, source_target_pairs={{0,3},{1,2},{2,1},{3,0},{4,7},{5,6},{6,5},{7,4},{8,11},{9,10},{10,... | collective-permute-start | bytes 393224 | tf_op jit(solution)/shard_map/ppermute | solution.py:179
  139.6 37.4 %collective-permute-start.19 = (f16[256,256]{1,0:T(8,128)(2,1)S(1)}, f16[256,256]{1,0:T(8,128)(2,1)S(1)}, u32[]{:S(2)}, u32[]{:S(2)}) collective-permute-start(f16[256,256]{1,0:T(8,128)(2,1)S(1)} %convert_element_type.175), channel_id=1, source_target_pairs={{0,10},{1,11},{2,8},{3,9},{4,14},{5,15},{6,12},{7,13},{8,2},{9,3},... | collective-permute-start | bytes 393224 | tf_op jit(solution)/shard_map/ppermute | solution.py:179
  162.3 18.2 %collective-permute-start.18 = (f16[256,256]{1,0:T(8,128)(2,1)S(1)}, f16[256,256]{1,0:T(8,128)(2,1)S(1)}, u32[]{:S(2)}, u32[]{:S(2)}) collective-permute-start(f16[256,256]{1,0:T(8,128)(2,1)S(1)} %convert_element_type.172), channel_id=1, source_target_pairs={{0,2},{1,3},{2,0},{3,1},{4,6},{5,7},{6,4},{7,5},{8,10},{9,11},{10,... | collective-permute-start | bytes 393224 | tf_op jit(solution)/shard_map/ppermute | solution.py:179
  175.0 19.9 %copy-start.5 = (f32[8,256,256]{2,1,0:T(8,128)}, f32[8,256,256]{2,1,0:T(8,128)S(1)}, u32[]{:S(2)}) copy-start(f32[8,256,256]{2,1,0:T(8,128)S(1)} %get-tuple-element.120.refs_2_) | copy-start | bytes 6291460
  175.0 5.9 %collective-permute-start.17 = (f16[256,256]{1,0:T(8,128)(2,1)S(1)}, f16[256,256]{1,0:T(8,128)(2,1)S(1)}, u32[]{:S(2)}, u32[]{:S(2)}) collective-permute-start(f16[256,256]{1,0:T(8,128)(2,1)S(1)} %convert_element_type.169), channel_id=1, source_target_pairs={{0,9},{1,8},{2,11},{3,10},{4,13},{5,12},{6,15},{7,14},{8,1},{9,0},... | collective-permute-start | bytes 393224 | tf_op jit(solution)/shard_map/ppermute | solution.py:179
  175.1 7.2 %collective-permute-start.16 = (f16[256,256]{1,0:T(8,128)(2,1)S(1)}, f16[256,256]{1,0:T(8,128)(2,1)S(1)}, u32[]{:S(2)}, u32[]{:S(2)}) collective-permute-start(f16[256,256]{1,0:T(8,128)(2,1)S(1)} %convert_element_type.166), channel_id=1, source_target_pairs={{0,1},{1,0},{2,3},{3,2},{4,5},{5,4},{6,7},{7,6},{8,9},{9,8},{10,11... | collective-permute-start | bytes 393224 | tf_op jit(solution)/shard_map/ppermute | solution.py:179
  177.1 11.5 %collective-permute-start.23 = (f16[256,256]{1,0:T(8,128)(2,1)S(1)}, f16[256,256]{1,0:T(8,128)(2,1)S(1)}, u32[]{:S(2)}, u32[]{:S(2)}) collective-permute-start(f16[256,256]{1,0:T(8,128)(2,1)S(1)} %convert_element_type.162), channel_id=1, source_target_pairs={{0,12},{1,13},{2,14},{3,15},{4,8},{5,9},{6,10},{7,11},{8,4},{9,5},... | collective-permute-start | bytes 393224 | tf_op jit(solution)/shard_map/ppermute | solution.py:179
  177.1 11.5 %collective-permute-start.22 = (f16[256,256]{1,0:T(8,128)(2,1)S(1)}, f16[256,256]{1,0:T(8,128)(2,1)S(1)}, u32[]{:S(2)}, u32[]{:S(2)}) collective-permute-start(f16[256,256]{1,0:T(8,128)(2,1)S(1)} %convert_element_type.183), channel_id=1, source_target_pairs={{0,4},{1,5},{2,6},{3,7},{4,0},{5,1},{6,2},{7,3},{8,12},{9,13},{10,... | collective-permute-start | bytes 393224 | tf_op jit(solution)/shard_map/ppermute | solution.py:179
  180.5 14.4 %copy-start.11 = (f16[256,256]{1,0:T(8,128)(2,1)}, f16[256,256]{1,0:T(8,128)(2,1)S(1)}, u32[]{:S(2)}) copy-start(f16[256,256]{1,0:T(8,128)(2,1)S(1)} %collective-permute-done.18) | copy-start | bytes 393220
  180.5 14.4 %collective-permute-start.29 = (f16[256,256]{1,0:T(8,128)(2,1)S(1)}, f16[256,256]{1,0:T(8,128)(2,1)S(1)}, u32[]{:S(2)}, u32[]{:S(2)}) collective-permute-start(f16[256,256]{1,0:T(8,128)(2,1)S(1)} %convert_element_type.180), channel_id=1, source_target_pairs={{0,15},{1,14},{2,13},{3,12},{4,11},{5,10},{6,9},{7,8},{8,7},{9,6},... | collective-permute-start | bytes 393224 | tf_op jit(solution)/shard_map/ppermute | solution.py:179
  180.9 15.2 %collective-permute-start.28 = (f16[256,256]{1,0:T(8,128)(2,1)S(1)}, f16[256,256]{1,0:T(8,128)(2,1)S(1)}, u32[]{:S(2)}, u32[]{:S(2)}) collective-permute-start(f16[256,256]{1,0:T(8,128)(2,1)S(1)} %convert_element_type.177), channel_id=1, source_target_pairs={{0,7},{1,6},{2,5},{3,4},{4,3},{5,2},{6,1},{7,0},{8,15},{9,14},{10,... | collective-permute-start | bytes 393224 | tf_op jit(solution)/shard_map/ppermute | solution.py:179
  182.3 19.2 %collective-permute-start.27 = (f16[256,256]{1,0:T(8,128)(2,1)S(1)}, f16[256,256]{1,0:T(8,128)(2,1)S(1)}, u32[]{:S(2)}, u32[]{:S(2)}) collective-permute-start(f16[256,256]{1,0:T(8,128)(2,1)S(1)} %convert_element_type.174), channel_id=1, source_target_pairs={{0,14},{1,15},{2,12},{3,13},{4,10},{5,11},{6,8},{7,9},{8,6},{9,7},... | collective-permute-start | bytes 393224 | tf_op jit(solution)/shard_map/ppermute | solution.py:179
  188.5 13.0 %collective-permute-start.26 = (f16[256,256]{1,0:T(8,128)(2,1)S(1)}, f16[256,256]{1,0:T(8,128)(2,1)S(1)}, u32[]{:S(2)}, u32[]{:S(2)}) collective-permute-start(f16[256,256]{1,0:T(8,128)(2,1)S(1)} %convert_element_type.171), channel_id=1, source_target_pairs={{0,6},{1,7},{2,4},{3,5},{4,2},{5,3},{6,0},{7,1},{8,14},{9,15},{10,... | collective-permute-start | bytes 393224 | tf_op jit(solution)/shard_map/ppermute | solution.py:179
  188.5 16.1 %collective-permute-start.25 = (f16[256,256]{1,0:T(8,128)(2,1)S(1)}, f16[256,256]{1,0:T(8,128)(2,1)}, u32[]{:S(2)}, u32[]{:S(2)}) collective-permute-start(f16[256,256]{1,0:T(8,128)(2,1)S(1)} %convert_element_type.168), channel_id=1, source_target_pairs={{0,13},{1,12},{2,15},{3,14},{4,9},{5,8},{6,11},{7,10},{8,5},{9,4},... | collective-permute-start | bytes 393224 | tf_op jit(solution)/shard_map/ppermute | solution.py:179
  194.9 10.8 %collective-permute-start.24 = (f16[256,256]{1,0:T(8,128)(2,1)S(1)}, f16[256,256]{1,0:T(8,128)(2,1)}, u32[]{:S(2)}, u32[]{:S(2)}) collective-permute-start(f16[256,256]{1,0:T(8,128)(2,1)S(1)} %convert_element_type.165), channel_id=1, source_target_pairs={{0,5},{1,4},{2,7},{3,6},{4,1},{5,0},{6,3},{7,2},{8,13},{9,12},{10,... | collective-permute-start | bytes 393224 | tf_op jit(solution)/shard_map/ppermute | solution.py:179
  194.9 1.0 copy-start.12
  195.9 10.7 %copy-start.6 = (f32[8,256,256]{2,1,0:T(8,128)S(1)}, f32[8,256,256]{2,1,0:T(8,128)}, u32[]{:S(2)}) copy-start(f32[8,256,256]{2,1,0:T(8,128)} %copy-done.5) | copy-start | bytes 6291460
  195.9 10.7 %copy-start.10 = (s32[1,16]{1,0:T(1,128)S(1)}, s32[1,16]{1,0:T(1,128)}, u32[]{:S(2)}) copy-start(s32[1,16]{1,0:T(1,128)} %param.10) | copy-start | bytes 196
  214.3 1.3 copy-start.4
  215.6 1.0 copy-start.7
  216.6 51.8 %all-to-all-start.1 = ((bf16[16,256,256]{2,1,0:T(8,128)(2,1)}), bf16[16,256,256]{2,1,0:T(8,128)(2,1)}, u32[]{:S(2)}, u32[]{:S(2)}) async-start(bf16[16,256,256]{2,1,0:T(8,128)(2,1)} %copy-done.4), calls=%async_computation.1 | async-start | bytes 4194304 | tf_op jit(solution)/shard_map/all_to_all | solution.py:327
  268.3 52.4 %all-to-all-start.2 = ((f16[16,256,256]{2,1,0:T(8,128)(2,1)}), f16[16,256,256]{2,1,0:T(8,128)(2,1)}, u32[]{:S(2)}, u32[]{:S(2)}) async-start(f16[16,256,256]{2,1,0:T(8,128)(2,1)} %convert_element_type.193), calls=%async_computation.2 | async-start | bytes 4194304 | tf_op jit(solution)/shard_map/all_to_all | solution.py:327
  293.1 1.3 copy-start.2
  320.8 2.2 copy-start.3
  320.8 2.5 copy-start.8

commit v5 on v4

--- a/solution.py
+++ b/solution.py
@@ -11,7 +11,9 @@
 TILE = 256
 ITERS = 2
 WINDOW = 8
+AFTER = 3
 FLIGHT = 8
+HOLD = 12
 BATCH = 4
 VMEM = 40 * 1024 * 1024
 
@@ -41,11 +43,11 @@
         store.wait()
 
 
-def batch_kernel(table, tiles, bias, meta, own, gin, *rest, slots, begin, scale):
+def batch_kernel(table, tiles, bias, meta, own, *rest, slots, begun, scale):
     size = len(slots)
     erem, lrem = rest[:size], rest[size : 2 * size]
     kout, gout, pouts = rest[-2 - size], rest[-1 - size], rest[-size:]
-    gout[...] = gin[...]
+    gout[...] = rest[2 * size][...] if begun else own[...].astype(jnp.float32)
     for k, slot in enumerate(slots):
         pouts[k][...] = jnp.zeros_like(pouts[k])
         row = meta[table[slot, PEER]][:1]
@@ -82,12 +84,12 @@
     lax.fori_loop(0, table[slot, COUNT], pair, 0)
 
 
-def gather_kernel(table, kref, lrem, gout):
+def gather_kernel(table, kref, lrem, labels, gout):
     slot = pl.program_id(0)
 
     @pl.when(slot == 0)
     def _():
-        gout[...] = jnp.zeros_like(gout)
+        gout[...] = labels[...]
 
     def pair(g, carry):
         gout[table[slot, LIST + g]] += jnp.dot(kref[g], lrem[0], preferred_element_type=jnp.float32)
@@ -97,44 +99,65 @@
 
 
 def update_kernel(owners, mine, gathered, classes, *rest, count, first):
-    tile = pl.program_id(0)
     backs, rest = rest[:count], rest[count:]
     if first:
-        degree, out, send, total, rounded, sem = rest
+        shares, out, send, total, arrived, arrive, rounded, leave = rest
     else:
-        old, degree, out, total = rest
+        shares, out, total, arrived, arrive = rest
+    tile = pl.program_id(0)
+
+    def load(k):
+        source = backs[k] if first else backs[0].at[k]
+        return pltpu.make_async_copy(source, arrived.at[k], arrive.at[k])
+
+    def store(k):
+        return pltpu.make_async_copy(rounded.at[mine[k]], send.at[k], leave.at[k])
+
+    slots = range(owners.shape[0])
+
+    @pl.when(tile == 0)
+    def _():
+        for k in slots:
+
+            @pl.when(owners[k] >= 0)
+            def _(k=k):
+                load(k).start()
+
     total[...] = gathered[0]
-    for k in range(owners.shape[0]):
+    for k in slots:
 
         @pl.when(owners[k] == tile)
-        def _():
-            total[...] += backs[k][...] if first else backs[0][k]
+        def _(k=k):
+            load(k).wait()
+            total[...] += arrived[k]
 
     summed = total[...]
-    ids = classes[0]
-    target = (ids == lax.broadcasted_iota(jnp.int32, (TILE, C), 1).astype(jnp.float32)).astype(jnp.float32)
+    diagonal = lax.broadcasted_iota(jnp.int32, (TILE, TILE), 0) == lax.broadcasted_iota(
+        jnp.int32, (TILE, TILE), 1
+    )
+    ids = jnp.sum(jnp.where(diagonal, classes[0], 0.0), axis=1, keepdims=True)
+    hot = ids == lax.broadcasted_iota(jnp.int32, (TILE, C), 1).astype(jnp.float32)
     if first:
-        degree[0] = 1.0 + jnp.sum(summed, axis=1, keepdims=True)
-        labels = jnp.where(ids < 0, 1.0 / C, target)
+        share = mixing / jnp.sum(summed, axis=1, keepdims=True)
+        shares[0] = jnp.sum(jnp.where(diagonal, share, 0.0), axis=0, keepdims=True)
     else:
-        labels = old[0]
-    blended = (labels + summed) * (mixing / degree[0]) + (1.0 - mixing) * target
+        share = jnp.sum(jnp.where(diagonal, shares[0], 0.0), axis=1, keepdims=True)
+    blended = summed * share + jnp.where(hot, 1.0 - mixing, 0.0)
     squared = blended * blended
     labels = squared * (1.0 / jnp.sum(squared, axis=1, keepdims=True))
     out[0] = labels
     if first:
         rounded[tile] = labels.astype(jnp.bfloat16)
+        for k in range(send.shape[0]):
+
+            @pl.when(mine[k] == tile)
+            def _(k=k):
+                store(k).start()
 
         @pl.when(tile == pl.num_programs(0) - 1)
         def _():
-            copies = [
-                pltpu.make_async_copy(rounded.at[mine[k]], send.at[k], sem.at[k])
-                for k in range(send.shape[0])
-            ]
-            for copy in copies:
-                copy.start()
-            for copy in copies:
-                copy.wait()
+            for k in range(send.shape[0]):
+                store(k).wait()
 
 
 def body(embed, seed_mask, seed_class, partner, pair_local, pair_peer):
@@ -209,7 +232,8 @@
     bias = (1.0 - norms * (1.0 / features)) * (sharpness * LOG2E)
     classes = jnp.where(seed_mask == 1, seed_class, -1).reshape(tile_count, TILE).astype(jnp.float32)
     meta = jnp.stack([bias, classes], axis=1)
-    meta_in = lax.all_to_all(meta[mine], "shard", split_axis=0, concat_axis=0, tiled=True)
+    meta_out, flying[AFTER] = lax.optimization_barrier((meta[mine], flying[AFTER]))
+    meta_in = lax.all_to_all(meta_out, "shard", split_axis=0, concat_axis=0, tiled=True)
     class_ids = jnp.arange(C, dtype=jnp.float32)
 
     def first_labels(ids):
@@ -219,7 +243,7 @@
     own = first_labels(classes)
     own_in = first_labels(meta_in[:, 1])
     bias_column = bias[:, :, None]
-    class_column = classes[:, :, None]
+    class_rows = classes[:, None, :]
 
     block = (1, TILE, C)
     store = (tile_count, TILE, TILE)
@@ -237,17 +261,21 @@
     def batch_call(index, erem, kernels, gathered):
         slots = batches[index]
         size = len(slots)
-        begun = [] if kernels is None else [kernels]
-        args = [tiles, bias_column, meta_in, own, gathered] + erem + [own_in] * size
-        in_specs = [full(a) for a in args[: 5 + size]] + [by_peer(s) for s in slots]
+        args = [tiles, bias_column, meta_in, own] + erem + [own_in] * size
+        in_specs = [full(a) for a in args[: 4 + size]] + [by_peer(s) for s in slots]
+        aliases = {}
+        if index:
+            args += [gathered, kernels]
+            in_specs += [full(tile_sums), ANY]
+            aliases = {len(args): 0}
         return pl.pallas_call(
             lambda *refs: batch_kernel(
-                *refs, slots=slots, begin=slots[0], scale=2.0 * sharpness * LOG2E / features
+                *refs, slots=slots, begun=index > 0, scale=2.0 * sharpness * LOG2E / features
             ),
             grid_spec=pltpu.PrefetchScalarGridSpec(
                 num_scalar_prefetch=1,
                 grid=(1,),
-                in_specs=in_specs + [ANY] * len(begun),
+                in_specs=in_specs,
                 out_specs=[
                     pl.BlockSpec((BATCH * tile_count, TILE, TILE), lambda g, t: (index, 0, 0)),
                     full(tile_sums),
@@ -255,11 +283,11 @@
                 + [full(sums)] * size,
             ),
             out_shape=[kernel_store, tile_sums] + [sums] * size,
-            input_output_aliases={6 + 2 * size: 0} if begun else {},
+            input_output_aliases=aliases,
             compiler_params=pltpu.CompilerParams(vmem_limit_bytes=VMEM),
             cost_estimate=pl.CostEstimate(flops=int(1e10), bytes_accessed=int(3e7), transcendentals=0),
             name="batch",
-        )(table, *args, *begun)
+        )(table, *args)
 
     def push_call(kernels, own):
         return pl.pallas_call(
@@ -276,7 +304,7 @@
             name="push",
         )(table, kernels, own)
 
-    def gather_call(kernels, incoming):
+    def gather_call(kernels, incoming, labels):
         return pl.pallas_call(
             gather_kernel,
             grid_spec=pltpu.PrefetchScalarGridSpec(
@@ -285,6 +313,7 @@
                 in_specs=[
                     pl.BlockSpec(store, lambda g, t: (g, 0, 0)),
                     pl.BlockSpec(block, lambda g, t: (t[g, PEER], 0, 0)),
+                    full(labels),
                 ],
                 out_specs=full(tile_sums),
             ),
@@ -292,19 +321,23 @@
             compiler_params=pltpu.CompilerParams(vmem_limit_bytes=VMEM),
             cost_estimate=pl.CostEstimate(flops=int(2e10), bytes_accessed=int(6e7), transcendentals=0),
             name="gather",
-        )(table, kernels, incoming)
+        )(table, kernels, incoming, labels)
 
     def update_call(owners, gathered, backs, state):
         first = state is None
         by_tile = pl.BlockSpec(block, lambda g, o, m: (g, 0, 0))
-        column = pl.BlockSpec((1, TILE, 1), lambda g, o, m: (g, 0, 0))
-        column_shape = jax.ShapeDtypeStruct((tile_count, TILE, 1), jnp.float32)
-        back_specs = [pl.BlockSpec(b.shape, lambda g, o, m, d=len(b.shape): (0,) * d) for b in backs]
+        row = pl.BlockSpec((1, 1, TILE), lambda g, o, m: (g, 0, 0))
         out_shape, out_specs = [tile_sums], [by_tile]
-        scratch = [pltpu.VMEM((TILE, C), jnp.float32)]
+        slots = owners.shape[0]
+        scratch = [
+            pltpu.VMEM((TILE, C), jnp.float32),
+            pltpu.VMEM((slots, TILE, C), jnp.float32),
+            pltpu.SemaphoreType.DMA((slots,)),
+        ]
         if first:
-            send = jax.ShapeDtypeStruct((n, TILE, C), jnp.bfloat16)
-            out_shape, out_specs = [column_shape, tile_sums, send], [column, by_tile, ANY]
+            row_shape = jax.ShapeDtypeStruct((tile_count, 1, TILE), jnp.float32)
+            out_shape = [row_shape, tile_sums, pltpu.HBM((n, TILE, C), jnp.bfloat16)]
+            out_specs = [row, by_tile, pl.BlockSpec(memory_space=pltpu.HBM)]
             scratch += [
                 pltpu.VMEM((tile_count, TILE, C), jnp.bfloat16),
                 pltpu.SemaphoreType.DMA((n,)),
@@ -314,39 +347,39 @@
             grid_spec=pltpu.PrefetchScalarGridSpec(
                 num_scalar_prefetch=2,
                 grid=(tile_count,),
-                in_specs=[by_tile, column] + back_specs + ([] if first else [by_tile, column]),
+                in_specs=[by_tile, row] + [ANY] * len(backs) + ([] if first else [row]),
                 out_specs=out_specs,
                 scratch_shapes=scratch,
             ),
             out_shape=out_shape,
             compiler_params=pltpu.CompilerParams(vmem_limit_bytes=VMEM),
             name="update",
-        )(owners, mine, gathered, class_column, *backs, *([] if first else state))
+        )(owners, mine, gathered, class_rows, *backs, *([] if first else [state]))
 
     def exchange(array):
         return lax.all_to_all(array, "shard", split_axis=0, concat_axis=0, tiled=True)
 
-    kernels, gathered = None, jnp.zeros(tile_sums.shape, tile_sums.dtype)
+    kernels = gathered = None
     pushes = []
     for b, slots in enumerate(batches):
         kernels, gathered, *done = batch_call(b, [flying[k] for k in slots], kernels, gathered)
         pushes += done
     for k in range(slot_count):
         out = pushes[k].astype(jnp.float16)
-        ahead = slot_count + k - FLIGHT
+        ahead = slot_count + k - FLIGHT if k >= FLIGHT else min(HOLD + k, slot_count - 1)
         out, flying[ahead] = lax.optimization_barrier((out, flying[ahead]))
         flying.append(swap(out, k))
     backs = [back.astype(jnp.float32) for back in flying[slot_count:]]
-    degree, labels, send = update_call(mine_x, gathered, backs, None)
+    shares, labels, send = update_call(mine_x, gathered, backs, None)
 
     incoming = exchange(send)
     rounded = labels.astype(jnp.bfloat16)
     pushes = push_call(kernels, rounded)
     pushes, incoming = lax.optimization_barrier((pushes.astype(jnp.float16), incoming))
     back = exchange(pushes).astype(jnp.float32)
-    gathered = gather_call(kernels, incoming)
+    gathered = gather_call(kernels, incoming, labels)
     owners = jnp.where(shard_ids == me, -1, mine)
-    (labels,) = update_call(owners, gathered, [back], [labels, degree])
+    (labels,) = update_call(owners, gathered, [back], shares)
     return labels.reshape(embed.shape[0], C)
 
 

time: 331 us -> 319 us (0.964)
  waiting for transfers between devices: 136 us -> 123 us
    all_to_all x1, waiting for transfers between devices: 15.4 us -> 1.38 us  [body(): lax.all_to_all(meta_out, 'shard', split_axis=0, concat_axis=0, tiled=True)]
    ppermute x30, starting transfers between devices: 42.5 us -> 46.6 us  [swap(): return lax.ppermute(value, 'shard', [(q, q ^ order[k]) for q in range(n)])]
    pallas_call x4, Pallas kernels: 50.8 us -> 54.7 us  [batch_call(): pl.pallas_call(lambda *refs: batch_kernel(*refs, slots=slots, begun=index...]
  transfers between devices with their start and end apart: 33 -> 33, of which waited for: 12 -> 16; matrix products, arithmetic and copies ran while one was open for 4% -> 3% of each run, Pallas kernels for 29% -> 32%
where the time goes in v5:
time: 319 us; the launch traced here: 318 us
  waiting for transfers between devices  123 us (39%)
  Pallas kernels  117 us (37%)
  starting transfers between devices  60.4 us (19%)
  other arithmetic  8.83 us (3%)
  local copies, waits for them, and re-layouts  7.62 us (2%)
    ppermute x30, waiting for transfers between devices, swap(): return lax.ppermute(value, 'shard', [(q, q ^ order[k]) for q in range(n)])  72.5 us
    pallas_call x4, Pallas kernels, batch_call(): pl.pallas_call(lambda *refs: batch_kernel(*refs, slots=slots, begun=index...  54.7 us
    all_to_all x2, waiting for transfers between devices, exchange(): lax.all_to_all(array, 'shard', split_axis=0, concat_axis=0, tiled=True)  49.4 us
    ppermute x30, starting transfers between devices, swap(): return lax.ppermute(value, 'shard', [(q, q ^ order[k]) for q in range(n)])  46.6 us
    pallas_call x1, Pallas kernels, push_call(): pl.pallas_call(push_kernel, grid_spec=pltpu.PrefetchScalarGridSpec(num_sc...  22 us
    pallas_call x1, Pallas kernels, gather_call(): pl.pallas_call(gather_kernel, grid_spec=pltpu.PrefetchScalarGridSpec(num_...  20.2 us
    pallas_call x2, Pallas kernels, update_call(): pl.pallas_call(lambda *refs: update_kernel(*refs, count=len(backs), first...  11.7 us
    all_to_all x2, starting transfers between devices, exchange(): lax.all_to_all(array, 'shard', split_axis=0, concat_axis=0, tiled=True)  9.86 us
  transfers between devices with their start and end apart: 33, of which 16 were waited for; matrix products, arithmetic and copies ran while one was open for 3% of the time, Pallas kernels for 32%

profile of v5, /device:TPU:13, one launch (start us, length us, event | category | flops | bytes accessed | tf_op | source)
XLA Modules:
  0.0 318.0 jit_solution(3017810720419932059)
XLA Ops:
  0.0 4.4 %take.3 = (bf16[256,768]{1,0:T(8,128)(2,1)}, bf16[256,768]{1,0:T(8,128)(2,1)}, bf16[256,768]{1,0:T(8,128)(2,1)}, bf16[256,768]{1,0:T(8,128)(2,1)}, bf16[256,768]...) custom-call(s32[16]{0:T(128)} %bitcast.29, s32[1]{0:T(128)} %bitcast.9.refs_1_, ...), custom_call_target="tpu_custom_call" | custom-call | tf_op jit(solution)/shard_map/take/pallas_call | solution.py:206
  4.5 0.2 collective-permute-start
  4.7 3.3 %collective-permute-start.1 = (bf16[256,768]{1,0:T(8,128)(2,1)}, bf16[256,768]{1,0:T(8,128)(2,1)}, u32[]{:S(2)}, u32[]{:S(2)}) collective-permute-start(bf16[256,768]{1,0:T(8,128)(2,1)} %get-tuple-element.86), channel_id=1, source_target_pairs={{0,10},{1,11},{2,8},{3,9},{4,14},{5,15},{6,12},{7,13},{8,2},{9,3},... | collective-permute-start | bytes 1179656 | tf_op jit(solution)/shard_map/ppermute | solution.py:202
  8.0 1.4 collective-permute-start.3
  9.5 0.1 collective-permute-start.5
  9.6 2.3 collective-permute-start.7
  11.9 0.7 multiply_reduce_fusion
  12.7 0.4 and_reduce_fusion
  13.4 0.2 select_reduce_fusion.1.refs_0_
  13.6 18.5 %collective-permute-done.refs_8_ = bf16[256,768]{1,0:T(8,128)(2,1)} collective-permute-done((bf16[256,768]{1,0:T(8,128)(2,1)}, bf16[256,768]{1,0:T(8,128)(2,1)}, u32[]{:S(2)}, u32[]{:S(2)}) %collective-permute-start) | collective-permute-done | bytes 393248 | tf_op jit(solution)/shard_map/ppermute | solution.py:202
  32.0 2.1 collective-permute-start.9
  34.1 8.1 %collective-permute-done.1.refs_5_ = bf16[256,768]{1,0:T(8,128)(2,1)} collective-permute-done((bf16[256,768]{1,0:T(8,128)(2,1)}, bf16[256,768]{1,0:T(8,128)(2,1)}, u32[]{:S(2)}, u32[]{:S(2)}) %collective-permute-start.1) | collective-permute-done | bytes 393248 | tf_op jit(solution)/shard_map/ppermute | solution.py:202
  42.2 3.6 %collective-permute-start.11 = (bf16[256,768]{1,0:T(8,128)(2,1)}, bf16[256,768]{1,0:T(8,128)(2,1)}, u32[]{:S(2)}, u32[]{:S(2)}) collective-permute-start(bf16[256,768]{1,0:T(8,128)(2,1)} %get-tuple-element.101), channel_id=1, source_target_pairs={{0,9},{1,8},{2,11},{3,10},{4,13},{5,12},{6,15},{7,14},{8,1},{9,0},... | collective-permute-start | bytes 1179656 | tf_op jit(solution)/shard_map/ppermute | solution.py:202
  45.8 1.8 mul.54.refs_2_
  47.7 4.1 %take.2 = (bf16[256,768]{1,0:T(8,128)(2,1)}, bf16[256,768]{1,0:T(8,128)(2,1)}, bf16[256,768]{1,0:T(8,128)(2,1)}, bf16[256,768]{1,0:T(8,128)(2,1)}, bf16[256,768]...) custom-call(s32[16]{0:T(128)} %bitcast.30, s32[1]{0:T(128)} %bitcast.9.refs_1_, ...), custom_call_target="tpu_custom_call" | custom-call | tf_op jit(solution)/shard_map/take/pallas_call | solution.py:206
  52.2 1.2 gather_fusion
  53.4 1.5 select_convert_fusion.1.refs_4_
  54.9 4.0 %all-to-all-start = ((f32[16,2,256]{2,1,0:T(2,128)}), f32[16,2,256]{2,1,0:T(2,128)S(1)}, u32[]{:S(2)}, u32[]{:S(2)}) async-start(f32[16,2,256]{2,1,0:T(2,128)} %gather_fusion), calls=%async_computation | async-start | bytes 65536 | tf_op jit(solution)/shard_map/all_to_all | solution.py:236
  58.9 0.3 collective-permute-start.14
  59.2 3.0 collective-permute-start.13
  62.2 5.7 %collective-permute-done.7.refs_5_ = bf16[256,768]{1,0:T(8,128)(2,1)} collective-permute-done((bf16[256,768]{1,0:T(8,128)(2,1)}, bf16[256,768]{1,0:T(8,128)(2,1)}, u32[]{:S(2)}, u32[]{:S(2)}) %collective-permute-start.7) | collective-permute-done | bytes 393248 | tf_op jit(solution)/shard_map/ppermute | solution.py:202
  67.8 1.5 collective-permute-start.8
  69.3 6.9 %collective-permute-done.11.refs_7_ = bf16[256,768]{1,0:T(8,128)(2,1)} collective-permute-done((bf16[256,768]{1,0:T(8,128)(2,1)}, bf16[256,768]{1,0:T(8,128)(2,1)}, u32[]{:S(2)}, u32[]{:S(2)}) %collective-permute-start.11) | collective-permute-done | bytes 393248 | tf_op jit(solution)/shard_map/ppermute | solution.py:202
  76.2 0.7 collective-permute-start.10
  76.9 1.4 all-to-all-done.refs_3_
  78.3 1.4 select_convert_fusion.refs_9_.refs_10_.refs_11_.refs_12_.refs_8_
  79.8 1.2 copy-done.4
  81.0 1.2 copy-done.5
  82.2 12.6 %batch.4 = (bf16[128,256,256]{2,1,0:T(8,128)(2,1)}, f32[8,256,256]{2,1,0:T(8,128)S(1)}, f32[256,256]{1,0:T(8,128)S(1)}, f32[256,256]{1,0:T(8,128)S(1)}, f32[256,256]{1,0:T(8,128)S(1)}, /*index=5*/f32[256,256]{1,0:T(8,128)S(1)}) custom-call(s32[15,11]{1,0:T(8,128)S(1)} %pad_add_fusion.refs_0_.table, bf16[8,256,768]{2,1,0:T(8,128)(2,1)S(1)} %bitcast.22, ...), custom_call_target="tpu_custom_call" | custom-call | flops 10000000000 | bytes 30000000 | tf_op jit(solution)/shard_map/batch/pallas_call | solution.py:271
  94.8 6.1 %collective-permute-done.14.refs_8_ = bf16[256,768]{1,0:T(8,128)(2,1)} collective-permute-done((bf16[256,768]{1,0:T(8,128)(2,1)}, bf16[256,768]{1,0:T(8,128)(2,1)}, u32[]{:S(2)}, u32[]{:S(2)}) %collective-permute-start.14) | collective-permute-done | bytes 393248 | tf_op jit(solution)/shard_map/ppermute | solution.py:202
  100.8 2.5 collective-permute-start.12
  103.3 12.6 %batch.5 = (bf16[128,256,256]{2,1,0:T(8,128)(2,1)}, f32[8,256,256]{2,1,0:T(8,128)S(1)}, f32[256,256]{1,0:T(8,128)S(1)}, f32[256,256]{1,0:T(8,128)S(1)}, f32[256,256]{1,0:T(8,128)S(1)}, /*index=5*/f32[256,256]{1,0:T(8,128)S(1)}) custom-call(s32[15,11]{1,0:T(8,128)S(1)} %pad_add_fusion.refs_0_.table, ...), custom_call_target="tpu_custom_call", output_to_operand_aliasing={{0}: (14, {})} | custom-call | flops 10000000000 | bytes 30000000 | tf_op jit(solution)/shard_map/batch/pallas_call | solution.py:271
  116.1 1.6 collective-permute-done.13.refs_8_
  117.7 5.3 %collective-permute-start.4 = (bf16[256,768]{1,0:T(8,128)(2,1)S(1)}, bf16[256,768]{1,0:T(8,128)(2,1)S(1)}, u32[]{:S(2)}, u32[]{:S(2)}) collective-permute-start(bf16[256,768]{1,0:T(8,128)(2,1)S(1)} %copy-done.12), channel_id=1, source_target_pairs={{0,7},{1,6},{2,5},{3,4},{4,3},{5,2},{6,1},{7,0},{8,15},{9,14},{10,... | collective-permute-start | bytes 1179656 | tf_op jit(solution)/shard_map/ppermute | solution.py:202
  123.0 0.3 collective-permute-start.6
  123.3 2.8 collective-permute-done.10.refs_6_
  126.2 2.8 collective-permute-done.12.refs_7_
  129.0 2.8 collective-permute-start.21
  131.9 14.9 %batch.6 = (bf16[128,256,256]{2,1,0:T(8,128)(2,1)}, f32[8,256,256]{2,1,0:T(8,128)S(1)}, f32[256,256]{1,0:T(8,128)S(1)}, f32[256,256]{1,0:T(8,128)S(1)}, f32[256,256]{1,0:T(8,128)S(1)}, /*index=5*/f32[256,256]{1,0:T(8,128)S(1)}) custom-call(s32[15,11]{1,0:T(8,128)S(1)} %pad_add_fusion.refs_0_.table, ...), custom_call_target="tpu_custom_call", output_to_operand_aliasing={{0}: (14, {})} | custom-call | flops 10000000000 | bytes 30000000 | tf_op jit(solution)/shard_map/batch/pallas_call | solution.py:271
  146.7 3.5 %collective-permute-done.6.refs_7_ = bf16[256,768]{1,0:T(8,128)(2,1)S(1)} collective-permute-done((bf16[256,768]{1,0:T(8,128)(2,1)S(1)}, bf16[256,768]{1,0:T(8,128)(2,1)S(1)}, u32[]{:S(2)}, u32[]{:S(2)}) %collective-permute-start.6) | collective-permute-done | bytes 393248 | tf_op jit(solution)/shard_map/ppermute | solution.py:202
  150.2 0.4 collective-permute-start.20
  150.6 3.7 %collective-permute-start.17 = (f16[256,256]{1,0:T(8,128)(2,1)S(1)}, f16[256,256]{1,0:T(8,128)(2,1)S(1)}, u32[]{:S(2)}, u32[]{:S(2)}) collective-permute-start(f16[256,256]{1,0:T(8,128)(2,1)S(1)} %convert_element_type.161), channel_id=1, source_target_pairs={{0,9},{1,8},{2,11},{3,10},{4,13},{5,12},{6,15},{7,14},{8,1},{9,0},... | collective-permute-start | bytes 393224 | tf_op jit(solution)/shard_map/ppermute | solution.py:202
  154.3 14.7 %batch.7 = (bf16[128,256,256]{2,1,0:T(8,128)(2,1)}, f32[8,256,256]{2,1,0:T(8,128)S(1)}, f32[256,256]{1,0:T(8,128)S(1)}, f32[256,256]{1,0:T(8,128)S(1)}, f32[256,256]{1,0:T(8,128)S(1)}) custom-call(s32[15,11]{1,0:T(8,128)S(1)} %pad_add_fusion.refs_0_.table, bf16[8,256,768]{2,1,0:T(8,128)(2,1)S(1)} %bitcast.25, ...), custom_call_target="tpu_custom_call", output_to_operand_aliasing={{0}: (12, {})} | custom-call | flops 10000000000 | bytes 30000000 | tf_op jit(solution)/shard_map/batch/pallas_call | solution.py:271
  169.4 4.3 %collective-permute-start.29 = (f16[256,256]{1,0:T(8,128)(2,1)S(1)}, f16[256,256]{1,0:T(8,128)(2,1)S(1)}, u32[]{:S(2)}, u32[]{:S(2)}) collective-permute-start(f16[256,256]{1,0:T(8,128)(2,1)S(1)} %convert_element_type.172), channel_id=1, source_target_pairs={{0,15},{1,14},{2,13},{3,12},{4,11},{5,10},{6,9},{7,8},{8,7},{9,6},... | collective-permute-start | bytes 393224 | tf_op jit(solution)/shard_map/ppermute | solution.py:202
  173.8 0.5 collective-permute-start.28
  174.3 0.5 collective-permute-done.15
  174.7 0.7 collective-permute-start.27
  175.5 4.4 %collective-permute-start.25 = (f16[256,256]{1,0:T(8,128)(2,1)S(1)}, f16[256,256]{1,0:T(8,128)(2,1)S(1)}, u32[]{:S(2)}, u32[]{:S(2)}) collective-permute-start(f16[256,256]{1,0:T(8,128)(2,1)S(1)} %convert_element_type.160), channel_id=1, source_target_pairs={{0,13},{1,12},{2,15},{3,14},{4,9},{5,8},{6,11},{7,10},{8,5},{9,4},... | collective-permute-start | bytes 393224 | tf_op jit(solution)/shard_map/ppermute | solution.py:202
  179.9 0.8 collective-permute-start.24
  180.6 2.1 collective-permute-start.23
  183.0 2.3 collective-permute-done.28
  185.4 9.4 %collective-permute-done.25 = f16[256,256]{1,0:T(8,128)(2,1)S(1)} collective-permute-done((f16[256,256]{1,0:T(8,128)(2,1)S(1)}, f16[256,256]{1,0:T(8,128)(2,1)S(1)}, u32[]{:S(2)}, u32[]{:S(2)}) %collective-permute-start.25) | collective-permute-done | bytes 131104 | tf_op jit(solution)/shard_map/ppermute | solution.py:202
  194.8 4.5 %collective-permute-done.23 = f16[256,256]{1,0:T(8,128)(2,1)S(1)} collective-permute-done((f16[256,256]{1,0:T(8,128)(2,1)S(1)}, f16[256,256]{1,0:T(8,128)(2,1)S(1)}, u32[]{:S(2)}, u32[]{:S(2)}) %collective-permute-start.23) | collective-permute-done | bytes 131104 | tf_op jit(solution)/shard_map/ppermute | solution.py:202
  199.3 5.6 %update.2 = (f32[8,1,256]{2,1,0:T(1,128)S(1)}, f32[8,256,256]{2,1,0:T(8,128)S(1)}, bf16[16,256,256]{2,1,0:T(8,128)(2,1)}) custom-call(s32[15]{0:T(128)S(1)} %select_reduce_fusion.1.refs_0_, s32[16]{0:T(128)S(1)} %bitcast.32, f32[8,256,256]{2,1,0:T(8,128)S(1)} %get-tuple-element.119.refs_2_, f32[8,1,256]{2,1,0:T(1,128)S(1)} %bitcast.27, ...), custom_call_target="tpu_custom_call" | custom-call | tf_op jit(solution)/shard_map/update/pallas_call | solution.py:345
  205.0 4.9 %all-to-all-start.1 = ((bf16[16,256,256]{2,1,0:T(8,128)(2,1)}), bf16[16,256,256]{2,1,0:T(8,128)(2,1)}, u32[]{:S(2)}, u32[]{:S(2)}) async-start(bf16[16,256,256]{2,1,0:T(8,128)(2,1)} %get-tuple-element.153), calls=%async_computation.1 | async-start | bytes 4194304 | tf_op jit(solution)/shard_map/all_to_all | solution.py:360
  210.0 22.0 %push.1 = f32[16,256,256]{2,1,0:T(8,128)S(1)} custom-call(s32[15,11]{1,0:T(8,128)S(1)} %pad_add_fusion.refs_0_.table, bf16[128,256,256]{2,1,0:T(8,128)(2,1)} %get-tuple-element.118.kref, bf16[8,256,256]{2,1,0:T(8,128)(2,1)S(1)} %convert_element_type.184.own), custom_call_target="tpu_custom_call" | custom-call | flops 20000000000 | bytes 60000000 | tf_op jit(solution)/shard_map/push/pallas_call | solution.py:293
  232.1 1.7 convert_element_type.185
  233.8 23.6 %all-to-all-done.1.lrem = bf16[16,256,256]{2,1,0:T(8,128)(2,1)} async-done(((bf16[16,256,256]{2,1,0:T(8,128)(2,1)}), bf16[16,256,256]{2,1,0:T(8,128)(2,1)}, u32[]{:S(2)}, u32[]{:S(2)}) %all-to-all-start.1) | async-done | bytes 2097184 | tf_op jit(solution)/shard_map/all_to_all | solution.py:360
  257.4 4.9 %all-to-all-start.2 = ((f16[16,256,256]{2,1,0:T(8,128)(2,1)}), f16[16,256,256]{2,1,0:T(8,128)(2,1)}, u32[]{:S(2)}, u32[]{:S(2)}) async-start(f16[16,256,256]{2,1,0:T(8,128)(2,1)} %convert_element_type.185), calls=%async_computation.2 | async-start | bytes 4194304 | tf_op jit(solution)/shard_map/all_to_all | solution.py:360
  262.4 1.6 copy-done.3
  263.9 20.2 %gather.7.refs_2_ = f32[8,256,256]{2,1,0:T(8,128)S(1)} custom-call(s32[15,11]{1,0:T(8,128)S(1)} %pad_add_fusion.refs_0_.table, bf16[128,256,256]{2,1,0:T(8,128)(2,1)} %get-tuple-element.118.kref, bf16[16,256,256]{2,1,0:T(8,128)(2,1)} %all-to-all-done.1.lrem, f32[8,256,256]{2,1,0:T(8,128)S(1)} %copy-done.3), custom_call_target="tpu_custom_call" | custom-call | flops 20000000000 | bytes 60000000 | tf_op jit(solution)/shard_map/gather/pallas_call | solution.py:308
  284.1 25.7 %all-to-all-done.2 = f16[16,256,256]{2,1,0:T(8,128)(2,1)} async-done(((f16[16,256,256]{2,1,0:T(8,128)(2,1)}), f16[16,256,256]{2,1,0:T(8,128)(2,1)}, u32[]{:S(2)}, u32[]{:S(2)}) %all-to-all-start.2) | async-done | bytes 2097184 | tf_op jit(solution)/shard_map/all_to_all | solution.py:360
  309.9 2.0 convert_element_type.186.refs_4_
  311.8 6.0 %update.3 = f32[8,256,256]{2,1,0:T(8,128)} custom-call(s32[16]{0:T(128)S(1)} %compare_select_fusion.1.refs_0_, s32[16]{0:T(128)S(1)} %bitcast.33, f32[8,256,256]{2,1,0:T(8,128)S(1)} %gather.7.refs_2_, f32[8,1,256]{2,1,0:T(1,128)S(1)} %bitcast.28, f32[16,256,256]{2,1,0:T(8,128)S(1)} %convert_element_type.186.refs_4_, f32[8,1,256]{2,1,0:T(1,128)S(1)} %get-tuple-element.156.refs_5_), custom_call_target="tpu_custom_call" | custom-call | tf_op jit(solution)/shard_map/update/pallas_call | solution.py:345
  (108 shorter events, 2.0 us)
Async XLA Ops:
  0.0 11.8 %copy-start.6 = (s32[1,16]{1,0:T(1,128)S(1)}, s32[1,16]{1,0:T(1,128)}, u32[]{:S(2)}) copy-start(s32[1,16]{1,0:T(1,128)} %param.10) | copy-start | bytes 196
  0.0 11.9 %copy-start = (bf16[2048,768]{1,0:T(8,128)(2,1)S(1)}, bf16[2048,768]{1,0:T(8,128)(2,1)}, u32[]{:S(2)}) copy-start(bf16[2048,768]{1,0:T(8,128)(2,1)} %param.7) | copy-start | bytes 9437188
  4.4 8.1 %copy-start.15 = (s32[64]{0:T(128)S(1)}, s32[64]{0:T(128)}, u32[]{:S(2)}) copy-start(s32[64]{0:T(128)} %param.11) | copy-start | bytes 772
  4.5 8.1 %copy-start.11 = (s32[15]{0:T(128)S(1)}, s32[15]{0:T(128)}, u32[]{:S(2)}) copy-start(s32[15]{0:T(128)} %constant.9.clone) | copy-start | bytes 184
  4.5 8.1 %copy-start.10 = (s32[64]{0:T(128)S(1)}, s32[64]{0:T(128)}, u32[]{:S(2)}) copy-start(s32[64]{0:T(128)} %param.12) | copy-start | bytes 772
  4.5 8.8 %copy-start.8 = (s32[2048]{0:T(1024)S(1)}, s32[2048]{0:T(1024)}, u32[]{:S(2)}) copy-start(s32[2048]{0:T(1024)} %param.9) | copy-start | bytes 24580
  4.5 8.8 %copy-start.9 = (s32[2048]{0:T(1024)S(1)}, s32[2048]{0:T(1024)}, u32[]{:S(2)}) copy-start(s32[2048]{0:T(1024)} %param.8) | copy-start | bytes 24580
  4.5 27.5 %collective-permute-start = (bf16[256,768]{1,0:T(8,128)(2,1)}, bf16[256,768]{1,0:T(8,128)(2,1)}, u32[]{:S(2)}, u32[]{:S(2)}) collective-permute-start(bf16[256,768]{1,0:T(8,128)(2,1)} %get-tuple-element.82), channel_id=1, source_target_pairs={{0,2},{1,3},{2,0},{3,1},{4,6},{5,7},{6,4},{7,5},{8,10},{9,11},{10,... | collective-permute-start | bytes 1179656 | tf_op jit(solution)/shard_map/ppermute | solution.py:202
  4.7 37.5 %collective-permute-start.1 = (bf16[256,768]{1,0:T(8,128)(2,1)}, bf16[256,768]{1,0:T(8,128)(2,1)}, u32[]{:S(2)}, u32[]{:S(2)}) collective-permute-start(bf16[256,768]{1,0:T(8,128)(2,1)} %get-tuple-element.86), channel_id=1, source_target_pairs={{0,10},{1,11},{2,8},{3,9},{4,14},{5,15},{6,12},{7,13},{8,2},{9,3},... | collective-permute-start | bytes 1179656 | tf_op jit(solution)/shard_map/ppermute | solution.py:202
  8.0 50.9 %collective-permute-start.3 = (bf16[256,768]{1,0:T(8,128)(2,1)}, bf16[256,768]{1,0:T(8,128)(2,1)}, u32[]{:S(2)}, u32[]{:S(2)}) collective-permute-start(bf16[256,768]{1,0:T(8,128)(2,1)} %get-tuple-element.89), channel_id=1, source_target_pairs={{0,3},{1,2},{2,1},{3,0},{4,7},{5,6},{6,5},{7,4},{8,11},{9,10},{10,... | collective-permute-start | bytes 1179656 | tf_op jit(solution)/shard_map/ppermute | solution.py:202
  9.5 49.7 %collective-permute-start.5 = (bf16[256,768]{1,0:T(8,128)(2,1)}, bf16[256,768]{1,0:T(8,128)(2,1)}, u32[]{:S(2)}, u32[]{:S(2)}) collective-permute-start(bf16[256,768]{1,0:T(8,128)(2,1)} %get-tuple-element.92), channel_id=1, source_target_pairs={{0,11},{1,10},{2,9},{3,8},{4,15},{5,14},{6,13},{7,12},{8,3},{9,2},... | collective-permute-start | bytes 1179656 | tf_op jit(solution)/shard_map/ppermute | solution.py:202
  9.6 58.2 %collective-permute-start.7 = (bf16[256,768]{1,0:T(8,128)(2,1)}, bf16[256,768]{1,0:T(8,128)(2,1)}, u32[]{:S(2)}, u32[]{:S(2)}) collective-permute-start(bf16[256,768]{1,0:T(8,128)(2,1)} %get-tuple-element.95), channel_id=1, source_target_pairs={{0,8},{1,9},{2,10},{3,11},{4,12},{5,13},{6,14},{7,15},{8,0},{9,1},... | collective-permute-start | bytes 1179656 | tf_op jit(solution)/shard_map/ppermute | solution.py:202
  32.0 35.8 %collective-permute-start.9 = (bf16[256,768]{1,0:T(8,128)(2,1)}, bf16[256,768]{1,0:T(8,128)(2,1)}, u32[]{:S(2)}, u32[]{:S(2)}) collective-permute-start(bf16[256,768]{1,0:T(8,128)(2,1)} %get-tuple-element.98), channel_id=1, source_target_pairs={{0,1},{1,0},{2,3},{3,2},{4,5},{5,4},{6,7},{7,6},{8,9},{9,8},{10,11... | collective-permute-start | bytes 1179656 | tf_op jit(solution)/shard_map/ppermute | solution.py:202
  42.2 34.1 %collective-permute-start.11 = (bf16[256,768]{1,0:T(8,128)(2,1)}, bf16[256,768]{1,0:T(8,128)(2,1)}, u32[]{:S(2)}, u32[]{:S(2)}) collective-permute-start(bf16[256,768]{1,0:T(8,128)(2,1)} %get-tuple-element.101), channel_id=1, source_target_pairs={{0,9},{1,8},{2,11},{3,10},{4,13},{5,12},{6,15},{7,14},{8,1},{9,0},... | collective-permute-start | bytes 1179656 | tf_op jit(solution)/shard_map/ppermute | solution.py:202
  51.8 28.0 %copy-start.1 = (bf16[2048,768]{1,0:T(8,128)(2,1)S(1)}, bf16[2048,768]{1,0:T(8,128)(2,1)}, u32[]{:S(2)}) copy-start(bf16[2048,768]{1,0:T(8,128)(2,1)} %param.7) | copy-start | bytes 9437188
  54.9 23.4 %all-to-all-start = ((f32[16,2,256]{2,1,0:T(2,128)}), f32[16,2,256]{2,1,0:T(2,128)S(1)}, u32[]{:S(2)}, u32[]{:S(2)}) async-start(f32[16,2,256]{2,1,0:T(2,128)} %gather_fusion), calls=%async_computation | async-start | bytes 65536 | tf_op jit(solution)/shard_map/all_to_all | solution.py:236
  58.9 41.9 %collective-permute-start.14 = (bf16[256,768]{1,0:T(8,128)(2,1)}, bf16[256,768]{1,0:T(8,128)(2,1)}, u32[]{:S(2)}, u32[]{:S(2)}) collective-permute-start(bf16[256,768]{1,0:T(8,128)(2,1)} %get-tuple-element.107), channel_id=1, source_target_pairs={{0,4},{1,5},{2,6},{3,7},{4,0},{5,1},{6,2},{7,3},{8,12},{9,13},{10,... | collective-permute-start | bytes 1179656 | tf_op jit(solution)/shard_map/ppermute | solution.py:202
  59.2 58.5 %collective-permute-start.13 = (bf16[256,768]{1,0:T(8,128)(2,1)}, bf16[256,768]{1,0:T(8,128)(2,1)}, u32[]{:S(2)}, u32[]{:S(2)}) collective-permute-start(bf16[256,768]{1,0:T(8,128)(2,1)} %get-tuple-element.103), channel_id=1, source_target_pairs={{0,6},{1,7},{2,4},{3,5},{4,2},{5,3},{6,0},{7,1},{8,14},{9,15},{10,... | collective-permute-start | bytes 1179656 | tf_op jit(solution)/shard_map/ppermute | solution.py:202
  67.8 82.8 %collective-permute-start.2 = (bf16[256,768]{1,0:T(8,128)(2,1)}, bf16[256,768]{1,0:T(8,128)(2,1)}, u32[]{:S(2)}, u32[]{:S(2)}) collective-permute-start(bf16[256,768]{1,0:T(8,128)(2,1)} %get-tuple-element.87), channel_id=1, source_target_pairs={{0,14},{1,15},{2,12},{3,13},{4,10},{5,11},{6,8},{7,9},{8,6},{9,7},... | collective-permute-start | bytes 1179656 | tf_op jit(solution)/shard_map/ppermute | solution.py:202
  67.8 55.2 %collective-permute-start.8 = (bf16[256,768]{1,0:T(8,128)(2,1)}, bf16[256,768]{1,0:T(8,128)(2,1)}, u32[]{:S(2)}, u32[]{:S(2)}) collective-permute-start(bf16[256,768]{1,0:T(8,128)(2,1)} %get-tuple-element.96), channel_id=1, source_target_pairs={{0,12},{1,13},{2,14},{3,15},{4,8},{5,9},{6,10},{7,11},{8,4},{9,5},... | collective-permute-start | bytes 1179656 | tf_op jit(solution)/shard_map/ppermute | solution.py:202
  76.2 49.9 %collective-permute-start.10 = (bf16[256,768]{1,0:T(8,128)(2,1)}, bf16[256,768]{1,0:T(8,128)(2,1)}, u32[]{:S(2)}, u32[]{:S(2)}) collective-permute-start(bf16[256,768]{1,0:T(8,128)(2,1)} %get-tuple-element.99), channel_id=1, source_target_pairs={{0,5},{1,4},{2,7},{3,6},{4,1},{5,0},{6,3},{7,2},{8,13},{9,12},{10,... | collective-permute-start | bytes 1179656 | tf_op jit(solution)/shard_map/ppermute | solution.py:202
  79.7 1.2 copy-start.4
  81.0 1.2 copy-start.5
  82.2 18.6 %copy-start.14 = (bf16[256,768]{1,0:T(8,128)(2,1)S(1)}, bf16[256,768]{1,0:T(8,128)(2,1)}, u32[]{:S(2)}) copy-start(bf16[256,768]{1,0:T(8,128)(2,1)} %get-tuple-element.102) | copy-start | bytes 1179652
  100.8 28.2 %collective-permute-start.12 = (bf16[256,768]{1,0:T(8,128)(2,1)S(1)}, bf16[256,768]{1,0:T(8,128)(2,1)S(1)}, u32[]{:S(2)}, u32[]{:S(2)}) collective-permute-start(bf16[256,768]{1,0:T(8,128)(2,1)S(1)} %copy-done.14), channel_id=1, source_target_pairs={{0,13},{1,12},{2,15},{3,14},{4,9},{5,8},{6,11},{7,10},{8,5},{9,4},... | collective-permute-start | bytes 1179656 | tf_op jit(solution)/shard_map/ppermute | solution.py:202
  115.9 1.8 copy-start.12
  115.9 7.1 %copy-start.13 = (bf16[256,768]{1,0:T(8,128)(2,1)S(1)}, bf16[256,768]{1,0:T(8,128)(2,1)}, u32[]{:S(2)}) copy-start(bf16[256,768]{1,0:T(8,128)(2,1)} %get-tuple-element.93) | copy-start | bytes 1179652
  117.7 32.9 %collective-permute-start.4 = (bf16[256,768]{1,0:T(8,128)(2,1)S(1)}, bf16[256,768]{1,0:T(8,128)(2,1)S(1)}, u32[]{:S(2)}, u32[]{:S(2)}) collective-permute-start(bf16[256,768]{1,0:T(8,128)(2,1)S(1)} %copy-done.12), channel_id=1, source_target_pairs={{0,7},{1,6},{2,5},{3,4},{4,3},{5,2},{6,1},{7,0},{8,15},{9,14},{10,... | collective-permute-start | bytes 1179656 | tf_op jit(solution)/shard_map/ppermute | solution.py:202
  123.0 27.2 %collective-permute-start.6 = (bf16[256,768]{1,0:T(8,128)(2,1)S(1)}, bf16[256,768]{1,0:T(8,128)(2,1)S(1)}, u32[]{:S(2)}, u32[]{:S(2)}) collective-permute-start(bf16[256,768]{1,0:T(8,128)(2,1)S(1)} %copy-done.13), channel_id=1, source_target_pairs={{0,15},{1,14},{2,13},{3,12},{4,11},{5,10},{6,9},{7,8},{8,7},{9,6},... | collective-permute-start | bytes 1179656 | tf_op jit(solution)/shard_map/ppermute | solution.py:202
  126.1 42.9 %collective-permute-start.18 = (f16[256,256]{1,0:T(8,128)(2,1)S(1)}, f16[256,256]{1,0:T(8,128)(2,1)S(1)}, u32[]{:S(2)}, u32[]{:S(2)}) collective-permute-start(f16[256,256]{1,0:T(8,128)(2,1)S(1)} %convert_element_type.164), channel_id=1, source_target_pairs={{0,2},{1,3},{2,0},{3,1},{4,6},{5,7},{6,4},{7,5},{8,10},{9,11},{10,... | collective-permute-start | bytes 393224 | tf_op jit(solution)/shard_map/ppermute | solution.py:202
  129.0 40.1 %collective-permute-start.21 = (f16[256,256]{1,0:T(8,128)(2,1)S(1)}, f16[256,256]{1,0:T(8,128)(2,1)S(1)}, u32[]{:S(2)}, u32[]{:S(2)}) collective-permute-start(f16[256,256]{1,0:T(8,128)(2,1)S(1)} %convert_element_type.173), channel_id=1, source_target_pairs={{0,11},{1,10},{2,9},{3,8},{4,15},{5,14},{6,13},{7,12},{8,3},{9,2},... | collective-permute-start | bytes 393224 | tf_op jit(solution)/shard_map/ppermute | solution.py:202
  150.2 19.0 %collective-permute-start.20 = (f16[256,256]{1,0:T(8,128)(2,1)S(1)}, f16[256,256]{1,0:T(8,128)(2,1)S(1)}, u32[]{:S(2)}, u32[]{:S(2)}) collective-permute-start(f16[256,256]{1,0:T(8,128)(2,1)S(1)} %convert_element_type.170), channel_id=1, source_target_pairs={{0,3},{1,2},{2,1},{3,0},{4,7},{5,6},{6,5},{7,4},{8,11},{9,10},{10,... | collective-permute-start | bytes 393224 | tf_op jit(solution)/shard_map/ppermute | solution.py:202
  150.6 18.7 %collective-permute-start.19 = (f16[256,256]{1,0:T(8,128)(2,1)S(1)}, f16[256,256]{1,0:T(8,128)(2,1)S(1)}, u32[]{:S(2)}, u32[]{:S(2)}) collective-permute-start(f16[256,256]{1,0:T(8,128)(2,1)S(1)} %convert_element_type.167), channel_id=1, source_target_pairs={{0,10},{1,11},{2,8},{3,9},{4,14},{5,15},{6,12},{7,13},{8,2},{9,3},... | collective-permute-start | bytes 393224 | tf_op jit(solution)/shard_map/ppermute | solution.py:202
  150.6 18.8 %collective-permute-start.17 = (f16[256,256]{1,0:T(8,128)(2,1)S(1)}, f16[256,256]{1,0:T(8,128)(2,1)S(1)}, u32[]{:S(2)}, u32[]{:S(2)}) collective-permute-start(f16[256,256]{1,0:T(8,128)(2,1)S(1)} %convert_element_type.161), channel_id=1, source_target_pairs={{0,9},{1,8},{2,11},{3,10},{4,13},{5,12},{6,15},{7,14},{8,1},{9,0},... | collective-permute-start | bytes 393224 | tf_op jit(solution)/shard_map/ppermute | solution.py:202
  169.0 4.8 %collective-permute-start.16 = (f16[256,256]{1,0:T(8,128)(2,1)S(1)}, f16[256,256]{1,0:T(8,128)(2,1)S(1)}, u32[]{:S(2)}, u32[]{:S(2)}) collective-permute-start(f16[256,256]{1,0:T(8,128)(2,1)S(1)} %convert_element_type.158), channel_id=1, source_target_pairs={{0,1},{1,0},{2,3},{3,2},{4,5},{5,4},{6,7},{7,6},{8,9},{9,8},{10,11... | collective-permute-start | bytes 393224 | tf_op jit(solution)/shard_map/ppermute | solution.py:202
  169.1 5.6 %collective-permute-start.15 = (f16[256,256]{1,0:T(8,128)(2,1)S(1)}, f16[256,256]{1,0:T(8,128)(2,1)S(1)}, u32[]{:S(2)}, u32[]{:S(2)}) collective-permute-start(f16[256,256]{1,0:T(8,128)(2,1)S(1)} %convert_element_type.155), channel_id=1, source_target_pairs={{0,8},{1,9},{2,10},{3,11},{4,12},{5,13},{6,14},{7,15},{8,0},{9,1},... | collective-permute-start | bytes 393224 | tf_op jit(solution)/shard_map/ppermute | solution.py:202
  169.2 6.3 %collective-permute-start.22 = (f16[256,256]{1,0:T(8,128)(2,1)S(1)}, f16[256,256]{1,0:T(8,128)(2,1)S(1)}, u32[]{:S(2)}, u32[]{:S(2)}) collective-permute-start(f16[256,256]{1,0:T(8,128)(2,1)S(1)} %convert_element_type.175), channel_id=1, source_target_pairs={{0,4},{1,5},{2,6},{3,7},{4,0},{5,1},{6,2},{7,3},{8,12},{9,13},{10,... | collective-permute-start | bytes 393224 | tf_op jit(solution)/shard_map/ppermute | solution.py:202
  169.3 10.5 %collective-permute-start.26 = (f16[256,256]{1,0:T(8,128)(2,1)S(1)}, f16[256,256]{1,0:T(8,128)(2,1)S(1)}, u32[]{:S(2)}, u32[]{:S(2)}) collective-permute-start(f16[256,256]{1,0:T(8,128)(2,1)S(1)} %convert_element_type.163), channel_id=1, source_target_pairs={{0,6},{1,7},{2,4},{3,5},{4,2},{5,3},{6,0},{7,1},{8,14},{9,15},{10,... | collective-permute-start | bytes 393224 | tf_op jit(solution)/shard_map/ppermute | solution.py:202
  169.4 11.2 %collective-permute-start.29 = (f16[256,256]{1,0:T(8,128)(2,1)S(1)}, f16[256,256]{1,0:T(8,128)(2,1)S(1)}, u32[]{:S(2)}, u32[]{:S(2)}) collective-permute-start(f16[256,256]{1,0:T(8,128)(2,1)S(1)} %convert_element_type.172), channel_id=1, source_target_pairs={{0,15},{1,14},{2,13},{3,12},{4,11},{5,10},{6,9},{7,8},{8,7},{9,6},... | collective-permute-start | bytes 393224 | tf_op jit(solution)/shard_map/ppermute | solution.py:202
  173.8 11.5 %collective-permute-start.28 = (f16[256,256]{1,0:T(8,128)(2,1)S(1)}, f16[256,256]{1,0:T(8,128)(2,1)S(1)}, u32[]{:S(2)}, u32[]{:S(2)}) collective-permute-start(f16[256,256]{1,0:T(8,128)(2,1)S(1)} %convert_element_type.169), channel_id=1, source_target_pairs={{0,7},{1,6},{2,5},{3,4},{4,3},{5,2},{6,1},{7,0},{8,15},{9,14},{10,... | collective-permute-start | bytes 393224 | tf_op jit(solution)/shard_map/ppermute | solution.py:202
  174.7 10.6 %collective-permute-start.27 = (f16[256,256]{1,0:T(8,128)(2,1)S(1)}, f16[256,256]{1,0:T(8,128)(2,1)S(1)}, u32[]{:S(2)}, u32[]{:S(2)}) collective-permute-start(f16[256,256]{1,0:T(8,128)(2,1)S(1)} %convert_element_type.166), channel_id=1, source_target_pairs={{0,14},{1,15},{2,12},{3,13},{4,10},{5,11},{6,8},{7,9},{8,6},{9,7},... | collective-permute-start | bytes 393224 | tf_op jit(solution)/shard_map/ppermute | solution.py:202
  175.5 19.3 %collective-permute-start.25 = (f16[256,256]{1,0:T(8,128)(2,1)S(1)}, f16[256,256]{1,0:T(8,128)(2,1)S(1)}, u32[]{:S(2)}, u32[]{:S(2)}) collective-permute-start(f16[256,256]{1,0:T(8,128)(2,1)S(1)} %convert_element_type.160), channel_id=1, source_target_pairs={{0,13},{1,12},{2,15},{3,14},{4,9},{5,8},{6,11},{7,10},{8,5},{9,4},... | collective-permute-start | bytes 393224 | tf_op jit(solution)/shard_map/ppermute | solution.py:202
  179.9 14.9 %collective-permute-start.24 = (f16[256,256]{1,0:T(8,128)(2,1)S(1)}, f16[256,256]{1,0:T(8,128)(2,1)S(1)}, u32[]{:S(2)}, u32[]{:S(2)}) collective-permute-start(f16[256,256]{1,0:T(8,128)(2,1)S(1)} %convert_element_type.157), channel_id=1, source_target_pairs={{0,5},{1,4},{2,7},{3,6},{4,1},{5,0},{6,3},{7,2},{8,13},{9,12},{10,... | collective-permute-start | bytes 393224 | tf_op jit(solution)/shard_map/ppermute | solution.py:202
  180.6 18.7 %collective-permute-start.23 = (f16[256,256]{1,0:T(8,128)(2,1)S(1)}, f16[256,256]{1,0:T(8,128)(2,1)S(1)}, u32[]{:S(2)}, u32[]{:S(2)}) collective-permute-start(f16[256,256]{1,0:T(8,128)(2,1)S(1)} %convert_element_type.154), channel_id=1, source_target_pairs={{0,12},{1,13},{2,14},{3,15},{4,8},{5,9},{6,10},{7,11},{8,4},{9,5},... | collective-permute-start | bytes 393224 | tf_op jit(solution)/shard_map/ppermute | solution.py:202
  182.8 16.5 %copy-start.7 = (s32[1,16]{1,0:T(1,128)S(1)}, s32[1,16]{1,0:T(1,128)}, u32[]{:S(2)}) copy-start(s32[1,16]{1,0:T(1,128)} %param.10) | copy-start | bytes 196
  205.0 5.0 %copy-start.2 = (f32[8,256,256]{2,1,0:T(8,128)}, f32[8,256,256]{2,1,0:T(8,128)S(1)}, u32[]{:S(2)}) copy-start(f32[8,256,256]{2,1,0:T(8,128)S(1)} %get-tuple-element.152.labels) | copy-start | bytes 6291460
  205.0 52.5 %all-to-all-start.1 = ((bf16[16,256,256]{2,1,0:T(8,128)(2,1)}), bf16[16,256,256]{2,1,0:T(8,128)(2,1)}, u32[]{:S(2)}, u32[]{:S(2)}) async-start(bf16[16,256,256]{2,1,0:T(8,128)(2,1)} %get-tuple-element.153), calls=%async_computation.1 | async-start | bytes 4194304 | tf_op jit(solution)/shard_map/all_to_all | solution.py:360
  257.4 52.4 %all-to-all-start.2 = ((f16[16,256,256]{2,1,0:T(8,128)(2,1)}), f16[16,256,256]{2,1,0:T(8,128)(2,1)}, u32[]{:S(2)}, u32[]{:S(2)}) async-start(f16[16,256,256]{2,1,0:T(8,128)(2,1)} %convert_element_type.185), calls=%async_computation.2 | async-start | bytes 4194304 | tf_op jit(solution)/shard_map/all_to_all | solution.py:360
  262.3 1.6 copy-start.3

commit v6 on v5

--- a/solution.py
+++ b/solution.py
@@ -11,9 +11,10 @@
 TILE = 256
 ITERS = 2
 WINDOW = 8
+FIRST = 2
 AFTER = 3
 FLIGHT = 8
-HOLD = 12
+HOLD = 11
 BATCH = 4
 VMEM = 40 * 1024 * 1024
 
@@ -220,7 +221,7 @@
             name="take",
         )(mine, me.reshape(1), tiles)
 
-    outgoing = list(take(list(range(WINDOW)))) + list(take(list(range(WINDOW, slot_count))))
+    outgoing = list(take(list(range(FIRST)))) + list(take(list(range(FIRST, slot_count))))
     flying = []
     for k in range(slot_count):
         out = outgoing[k]

time: 319 us -> 320 us (level)
  starting transfers between devices: 60.4 us -> 74.4 us
  waiting for transfers between devices: 123 us -> 112 us
    ppermute x30, waiting for transfers between devices: 72.5 us -> 62.6 us  [swap(): return lax.ppermute(value, 'shard', [(q, q ^ order[k]) for q in range(n)])]
    ppermute x30, starting transfers between devices: 46.6 us -> 55.1 us  [swap(): return lax.ppermute(value, 'shard', [(q, q ^ order[k]) for q in range(n)])]
  transfers between devices with their start and end apart: 33 -> 33, of which waited for: 16 -> 15; matrix products, arithmetic and copies ran while one was open for 3% -> 3% of each run, Pallas kernels for 32% -> 32%
where the time goes in v6:
time: 320 us
  Pallas kernels  118 us (37%)
  waiting for transfers between devices  112 us (35%)
  starting transfers between devices  74.4 us (23%)
  other arithmetic  8.83 us (3%)
  local copies, waits for them, and re-layouts  6.02 us (2%)
    ppermute x30, waiting for transfers between devices, swap(): return lax.ppermute(value, 'shard', [(q, q ^ order[k]) for q in range(n)])  62.6 us
    ppermute x30, starting transfers between devices, swap(): return lax.ppermute(value, 'shard', [(q, q ^ order[k]) for q in range(n)])  55.1 us
    pallas_call x4, Pallas kernels, batch_call(): pl.pallas_call(lambda *refs: batch_kernel(*refs, slots=slots, begun=index...  54.7 us
    all_to_all x2, waiting for transfers between devices, exchange(): lax.all_to_all(array, 'shard', split_axis=0, concat_axis=0, tiled=True)  48 us
    pallas_call x1, Pallas kernels, push_call(): pl.pallas_call(push_kernel, grid_spec=pltpu.PrefetchScalarGridSpec(num_sc...  22.7 us
    pallas_call x1, Pallas kernels, gather_call(): pl.pallas_call(gather_kernel, grid_spec=pltpu.PrefetchScalarGridSpec(num_...  20.9 us
    all_to_all x2, starting transfers between devices, exchange(): lax.all_to_all(array, 'shard', split_axis=0, concat_axis=0, tiled=True)  13 us
    pallas_call x2, Pallas kernels, update_call(): pl.pallas_call(lambda *refs: update_kernel(*refs, count=len(backs), first...  11.6 us
  transfers between devices with their start and end apart: 33, of which 15 were waited for; matrix products, arithmetic and copies ran while one was open for 3% of the time, Pallas kernels for 32%

profile of v6, /device:TPU:13, one launch (start us, length us, event | category | flops | bytes accessed | tf_op | source)
XLA Modules:
  0.0 320.0 jit_solution(2391230839248630644)
XLA Ops:
  0.0 2.6 take.3
  2.6 2.4 collective-permute-start.7
  5.0 1.0 collective-permute-start.9
  5.9 5.4 %take.2 = (bf16[256,768]{1,0:T(8,128)(2,1)}, bf16[256,768]{1,0:T(8,128)(2,1)}, bf16[256,768]{1,0:T(8,128)(2,1)}, bf16[256,768]{1,0:T(8,128)(2,1)}, bf16[256,768]...) custom-call(s32[16]{0:T(128)} %bitcast.30, ...), custom_call_target="tpu_custom_call" | custom-call | tf_op jit(solution)/shard_map/take/pallas_call | solution.py:207
  11.4 0.3 collective-permute-start
  11.7 1.0 collective-permute-start.1
  12.8 1.2 collective-permute-start.3
  14.0 0.7 multiply_reduce_fusion
  14.8 0.4 and_reduce_fusion
  15.2 0.1 copy.31
  15.5 0.2 select_reduce_fusion.1.refs_0_
  15.7 15.2 %collective-permute-done.7.refs_5_ = bf16[256,768]{1,0:T(8,128)(2,1)} collective-permute-done((bf16[256,768]{1,0:T(8,128)(2,1)}, bf16[256,768]{1,0:T(8,128)(2,1)}, u32[]{:S(2)}, u32[]{:S(2)}) %collective-permute-start.7) | collective-permute-done | bytes 393248 | tf_op jit(solution)/shard_map/ppermute | solution.py:203
  30.9 3.5 %collective-permute-start.5 = (bf16[256,768]{1,0:T(8,128)(2,1)}, bf16[256,768]{1,0:T(8,128)(2,1)}, u32[]{:S(2)}, u32[]{:S(2)}) collective-permute-start(bf16[256,768]{1,0:T(8,128)(2,1)} %get-tuple-element.93), channel_id=1, source_target_pairs={{0,11},{1,10},{2,9},{3,8},{4,15},{5,14},{6,13},{7,12},{8,3},{9,2},... | collective-permute-start | bytes 1179656 | tf_op jit(solution)/shard_map/ppermute | solution.py:203
  34.5 1.8 mul.54.refs_2_
  36.4 0.1 copy.35
  36.7 1.2 gather_fusion
  37.9 1.5 select_convert_fusion.1.refs_4_
  39.4 6.3 %all-to-all-start = ((f32[16,2,256]{2,1,0:T(2,128)}), f32[16,2,256]{2,1,0:T(2,128)S(1)}, u32[]{:S(2)}, u32[]{:S(2)}) async-start(f32[16,2,256]{2,1,0:T(2,128)} %gather_fusion), calls=%async_computation | async-start | bytes 65536 | tf_op jit(solution)/shard_map/all_to_all | solution.py:237
  45.8 0.3 collective-permute-start.14
  46.1 10.4 %collective-permute-done.1.refs_5_ = bf16[256,768]{1,0:T(8,128)(2,1)} collective-permute-done((bf16[256,768]{1,0:T(8,128)(2,1)}, bf16[256,768]{1,0:T(8,128)(2,1)}, u32[]{:S(2)}, u32[]{:S(2)}) %collective-permute-start.1) | collective-permute-done | bytes 393248 | tf_op jit(solution)/shard_map/ppermute | solution.py:203
  56.5 2.2 collective-permute-start.10
  58.7 1.6 collective-permute-start.8
  60.4 4.6 %collective-permute-done.5.refs_7_ = bf16[256,768]{1,0:T(8,128)(2,1)} collective-permute-done((bf16[256,768]{1,0:T(8,128)(2,1)}, bf16[256,768]{1,0:T(8,128)(2,1)}, u32[]{:S(2)}, u32[]{:S(2)}) %collective-permute-start.5) | collective-permute-done | bytes 393248 | tf_op jit(solution)/shard_map/ppermute | solution.py:203
  64.9 3.0 collective-permute-start.13
  67.9 13.9 %collective-permute-done.11.refs_7_ = bf16[256,768]{1,0:T(8,128)(2,1)} collective-permute-done((bf16[256,768]{1,0:T(8,128)(2,1)}, bf16[256,768]{1,0:T(8,128)(2,1)}, u32[]{:S(2)}, u32[]{:S(2)}) %collective-permute-start.11) | collective-permute-done | bytes 393248 | tf_op jit(solution)/shard_map/ppermute | solution.py:203
  81.8 1.5 all-to-all-done.refs_3_
  83.3 1.4 select_convert_fusion.refs_9_.refs_10_.refs_11_.refs_12_.refs_8_
  84.8 13.2 %batch.4 = (bf16[128,256,256]{2,1,0:T(8,128)(2,1)}, f32[8,256,256]{2,1,0:T(8,128)S(1)}, f32[256,256]{1,0:T(8,128)S(1)}, f32[256,256]{1,0:T(8,128)S(1)}, f32[256,256]{1,0:T(8,128)S(1)}, /*index=5*/f32[256,256]{1,0:T(8,128)S(1)}) custom-call(s32[15,11]{1,0:T(8,128)S(1)} %pad_add_fusion.refs_0_.table, bf16[8,256,768]{2,1,0:T(8,128)(2,1)S(1)} %bitcast.22, ...), custom_call_target="tpu_custom_call" | custom-call | flops 10000000000 | bytes 30000000 | tf_op jit(solution)/shard_map/batch/pallas_call | solution.py:272
  97.9 4.2 %collective-permute-start.12 = (bf16[256,768]{1,0:T(8,128)(2,1)S(1)}, bf16[256,768]{1,0:T(8,128)(2,1)S(1)}, u32[]{:S(2)}, u32[]{:S(2)}) collective-permute-start(bf16[256,768]{1,0:T(8,128)(2,1)S(1)} %copy-done.12), channel_id=1, source_target_pairs={{0,13},{1,12},{2,15},{3,14},{4,9},{5,8},{6,11},{7,10},{8,5},{9,4},... | collective-permute-start | bytes 1179656 | tf_op jit(solution)/shard_map/ppermute | solution.py:203
  102.1 13.8 %batch.5 = (bf16[128,256,256]{2,1,0:T(8,128)(2,1)}, f32[8,256,256]{2,1,0:T(8,128)S(1)}, f32[256,256]{1,0:T(8,128)S(1)}, f32[256,256]{1,0:T(8,128)S(1)}, f32[256,256]{1,0:T(8,128)S(1)}, /*index=5*/f32[256,256]{1,0:T(8,128)S(1)}) custom-call(s32[15,11]{1,0:T(8,128)S(1)} %pad_add_fusion.refs_0_.table, ...), custom_call_target="tpu_custom_call", output_to_operand_aliasing={{0}: (14, {})} | custom-call | flops 10000000000 | bytes 30000000 | tf_op jit(solution)/shard_map/batch/pallas_call | solution.py:272
  116.2 0.8 copy-done.10
  116.9 4.9 %collective-permute-start.4 = (bf16[256,768]{1,0:T(8,128)(2,1)S(1)}, bf16[256,768]{1,0:T(8,128)(2,1)S(1)}, u32[]{:S(2)}, u32[]{:S(2)}) collective-permute-start(bf16[256,768]{1,0:T(8,128)(2,1)S(1)} %copy-done.10), channel_id=1, source_target_pairs={{0,7},{1,6},{2,5},{3,4},{4,3},{5,2},{6,1},{7,0},{8,15},{9,14},{10,... | collective-permute-start | bytes 1179656 | tf_op jit(solution)/shard_map/ppermute | solution.py:203
  121.9 4.7 %collective-permute-start.21 = (f16[256,256]{1,0:T(8,128)(2,1)S(1)}, f16[256,256]{1,0:T(8,128)(2,1)S(1)}, u32[]{:S(2)}, u32[]{:S(2)}) collective-permute-start(f16[256,256]{1,0:T(8,128)(2,1)S(1)} %convert_element_type.173), channel_id=1, source_target_pairs={{0,11},{1,10},{2,9},{3,8},{4,15},{5,14},{6,13},{7,12},{8,3},{9,2},... | collective-permute-start | bytes 393224 | tf_op jit(solution)/shard_map/ppermute | solution.py:203
  126.6 14.3 %batch.6 = (bf16[128,256,256]{2,1,0:T(8,128)(2,1)}, f32[8,256,256]{2,1,0:T(8,128)S(1)}, f32[256,256]{1,0:T(8,128)S(1)}, f32[256,256]{1,0:T(8,128)S(1)}, f32[256,256]{1,0:T(8,128)S(1)}, /*index=5*/f32[256,256]{1,0:T(8,128)S(1)}) custom-call(s32[15,11]{1,0:T(8,128)S(1)} %pad_add_fusion.refs_0_.table, ...), custom_call_target="tpu_custom_call", output_to_operand_aliasing={{0}: (14, {})} | custom-call | flops 10000000000 | bytes 30000000 | tf_op jit(solution)/shard_map/batch/pallas_call | solution.py:272
  140.9 6.6 %collective-permute-done.6.refs_7_ = bf16[256,768]{1,0:T(8,128)(2,1)S(1)} collective-permute-done((bf16[256,768]{1,0:T(8,128)(2,1)S(1)}, bf16[256,768]{1,0:T(8,128)(2,1)S(1)}, u32[]{:S(2)}, u32[]{:S(2)}) %collective-permute-start.6) | collective-permute-done | bytes 393248 | tf_op jit(solution)/shard_map/ppermute | solution.py:203
  147.5 0.7 collective-permute-start.18
  148.2 9.9 %collective-permute-start.17 = (f16[256,256]{1,0:T(8,128)(2,1)S(1)}, f16[256,256]{1,0:T(8,128)(2,1)S(1)}, u32[]{:S(2)}, u32[]{:S(2)}) collective-permute-start(f16[256,256]{1,0:T(8,128)(2,1)S(1)} %convert_element_type.161), channel_id=1, source_target_pairs={{0,9},{1,8},{2,11},{3,10},{4,13},{5,12},{6,15},{7,14},{8,1},{9,0},... | collective-permute-start | bytes 393224 | tf_op jit(solution)/shard_map/ppermute | solution.py:203
  158.1 13.5 %batch.7 = (bf16[128,256,256]{2,1,0:T(8,128)(2,1)}, f32[8,256,256]{2,1,0:T(8,128)S(1)}, f32[256,256]{1,0:T(8,128)S(1)}, f32[256,256]{1,0:T(8,128)S(1)}, f32[256,256]{1,0:T(8,128)S(1)}) custom-call(s32[15,11]{1,0:T(8,128)S(1)} %pad_add_fusion.refs_0_.table, bf16[8,256,768]{2,1,0:T(8,128)(2,1)S(1)} %bitcast.25, ...), custom_call_target="tpu_custom_call", output_to_operand_aliasing={{0}: (12, {})} | custom-call | flops 10000000000 | bytes 30000000 | tf_op jit(solution)/shard_map/batch/pallas_call | solution.py:272
  171.8 0.1 collective-permute-start.15
  172.0 1.1 collective-permute-start.29
  173.1 3.6 %collective-permute-start.28 = (f16[256,256]{1,0:T(8,128)(2,1)S(1)}, f16[256,256]{1,0:T(8,128)(2,1)S(1)}, u32[]{:S(2)}, u32[]{:S(2)}) collective-permute-start(f16[256,256]{1,0:T(8,128)(2,1)S(1)} %convert_element_type.169), channel_id=1, source_target_pairs={{0,7},{1,6},{2,5},{3,4},{4,3},{5,2},{6,1},{7,0},{8,15},{9,14},{10,... | collective-permute-start | bytes 393224 | tf_op jit(solution)/shard_map/ppermute | solution.py:203
  176.9 0.5 collective-permute-done.15
  177.4 0.7 collective-permute-start.26
  178.1 4.4 %collective-permute-start.25 = (f16[256,256]{1,0:T(8,128)(2,1)S(1)}, f16[256,256]{1,0:T(8,128)(2,1)S(1)}, u32[]{:S(2)}, u32[]{:S(2)}) collective-permute-start(f16[256,256]{1,0:T(8,128)(2,1)S(1)} %convert_element_type.160), channel_id=1, source_target_pairs={{0,13},{1,12},{2,15},{3,14},{4,9},{5,8},{6,11},{7,10},{8,5},{9,4},... | collective-permute-start | bytes 393224 | tf_op jit(solution)/shard_map/ppermute | solution.py:203
  182.5 2.7 collective-permute-start.24
  185.2 0.6 collective-permute-done.28
  185.8 1.3 collective-permute-start.23
  187.3 1.1 collective-permute-done.27
  188.4 2.6 collective-permute-done.26
  191.1 1.9 collective-permute-done.25
  193.0 2.9 collective-permute-done.24
  196.0 2.2 collective-permute-done.23
  198.2 5.7 %update.2 = (f32[8,1,256]{2,1,0:T(1,128)S(1)}, f32[8,256,256]{2,1,0:T(8,128)S(1)}, bf16[16,256,256]{2,1,0:T(8,128)(2,1)}) custom-call(s32[15]{0:T(128)S(1)} %select_reduce_fusion.1.refs_0_, s32[16]{0:T(128)S(1)} %bitcast.32, f32[8,256,256]{2,1,0:T(8,128)S(1)} %get-tuple-element.120.refs_2_, f32[8,1,256]{2,1,0:T(1,128)S(1)} %bitcast.27, ...), custom_call_target="tpu_custom_call" | custom-call | tf_op jit(solution)/shard_map/update/pallas_call | solution.py:346
  203.9 8.1 %all-to-all-start.1 = ((bf16[16,256,256]{2,1,0:T(8,128)(2,1)}), bf16[16,256,256]{2,1,0:T(8,128)(2,1)}, u32[]{:S(2)}, u32[]{:S(2)}) async-start(bf16[16,256,256]{2,1,0:T(8,128)(2,1)} %get-tuple-element.155), calls=%async_computation.1 | async-start | bytes 4194304 | tf_op jit(solution)/shard_map/all_to_all | solution.py:361
  212.0 0.1 convert_element_type.184.own
  212.1 22.7 %push.1 = f32[16,256,256]{2,1,0:T(8,128)S(1)} custom-call(s32[15,11]{1,0:T(8,128)S(1)} %pad_add_fusion.refs_0_.table, bf16[128,256,256]{2,1,0:T(8,128)(2,1)} %get-tuple-element.119.kref, bf16[8,256,256]{2,1,0:T(8,128)(2,1)S(1)} %convert_element_type.184.own), custom_call_target="tpu_custom_call" | custom-call | flops 20000000000 | bytes 60000000 | tf_op jit(solution)/shard_map/push/pallas_call | solution.py:294
  234.8 1.7 convert_element_type.185
  236.5 23.0 %all-to-all-done.1.lrem = bf16[16,256,256]{2,1,0:T(8,128)(2,1)} async-done(((bf16[16,256,256]{2,1,0:T(8,128)(2,1)}), bf16[16,256,256]{2,1,0:T(8,128)(2,1)}, u32[]{:S(2)}, u32[]{:S(2)}) %all-to-all-start.1) | async-done | bytes 2097184 | tf_op jit(solution)/shard_map/all_to_all | solution.py:361
  259.5 4.9 %all-to-all-start.2 = ((f16[16,256,256]{2,1,0:T(8,128)(2,1)}), f16[16,256,256]{2,1,0:T(8,128)(2,1)}, u32[]{:S(2)}, u32[]{:S(2)}) async-start(f16[16,256,256]{2,1,0:T(8,128)(2,1)} %convert_element_type.185), calls=%async_computation.2 | async-start | bytes 4194304 | tf_op jit(solution)/shard_map/all_to_all | solution.py:361
  264.4 1.6 copy-done.2
  266.0 20.9 %gather.7.refs_2_ = f32[8,256,256]{2,1,0:T(8,128)S(1)} custom-call(s32[15,11]{1,0:T(8,128)S(1)} %pad_add_fusion.refs_0_.table, bf16[128,256,256]{2,1,0:T(8,128)(2,1)} %get-tuple-element.119.kref, bf16[16,256,256]{2,1,0:T(8,128)(2,1)} %all-to-all-done.1.lrem, f32[8,256,256]{2,1,0:T(8,128)S(1)} %copy-done.2), custom_call_target="tpu_custom_call" | custom-call | flops 20000000000 | bytes 60000000 | tf_op jit(solution)/shard_map/gather/pallas_call | solution.py:309
  286.9 25.1 %all-to-all-done.2 = f16[16,256,256]{2,1,0:T(8,128)(2,1)} async-done(((f16[16,256,256]{2,1,0:T(8,128)(2,1)}), f16[16,256,256]{2,1,0:T(8,128)(2,1)}, u32[]{:S(2)}, u32[]{:S(2)}) %all-to-all-start.2) | async-done | bytes 2097184 | tf_op jit(solution)/shard_map/all_to_all | solution.py:361
  311.9 2.0 convert_element_type.186.refs_4_
  313.9 6.0 %update.3 = f32[8,256,256]{2,1,0:T(8,128)} custom-call(s32[16]{0:T(128)S(1)} %compare_select_fusion.1.refs_0_, s32[16]{0:T(128)S(1)} %bitcast.33, f32[8,256,256]{2,1,0:T(8,128)S(1)} %gather.7.refs_2_, f32[8,1,256]{2,1,0:T(1,128)S(1)} %bitcast.28, f32[16,256,256]{2,1,0:T(8,128)S(1)} %convert_element_type.186.refs_4_, f32[8,1,256]{2,1,0:T(1,128)S(1)} %get-tuple-element.158.refs_5_), custom_call_target="tpu_custom_call" | custom-call | tf_op jit(solution)/shard_map/update/pallas_call | solution.py:346
  (104 shorter events, 1.6 us)
Async XLA Ops:
  2.6 11.4 %copy-start.5 = (s32[1,16]{1,0:T(1,128)S(1)}, s32[1,16]{1,0:T(1,128)}, u32[]{:S(2)}) copy-start(s32[1,16]{1,0:T(1,128)} %param.10) | copy-start | bytes 196
  2.6 11.4 %copy-start = (bf16[2048,768]{1,0:T(8,128)(2,1)S(1)}, bf16[2048,768]{1,0:T(8,128)(2,1)}, u32[]{:S(2)}) copy-start(bf16[2048,768]{1,0:T(8,128)(2,1)} %param.7) | copy-start | bytes 9437188
  2.6 28.3 %collective-permute-start.7 = (bf16[256,768]{1,0:T(8,128)(2,1)}, bf16[256,768]{1,0:T(8,128)(2,1)}, u32[]{:S(2)}, u32[]{:S(2)}) collective-permute-start(bf16[256,768]{1,0:T(8,128)(2,1)} %get-tuple-element.96), channel_id=1, source_target_pairs={{0,8},{1,9},{2,10},{3,11},{4,12},{5,13},{6,14},{7,15},{8,0},{9,1},... | collective-permute-start | bytes 1179656 | tf_op jit(solution)/shard_map/ppermute | solution.py:203
  5.0 40.8 %collective-permute-start.9 = (bf16[256,768]{1,0:T(8,128)(2,1)}, bf16[256,768]{1,0:T(8,128)(2,1)}, u32[]{:S(2)}, u32[]{:S(2)}) collective-permute-start(bf16[256,768]{1,0:T(8,128)(2,1)} %get-tuple-element.99), channel_id=1, source_target_pairs={{0,1},{1,0},{2,3},{3,2},{4,5},{5,4},{6,7},{7,6},{8,9},{9,8},{10,11... | collective-permute-start | bytes 1179656 | tf_op jit(solution)/shard_map/ppermute | solution.py:203
  11.4 3.3 %copy-start.13 = (s32[64]{0:T(128)S(1)}, s32[64]{0:T(128)}, u32[]{:S(2)}) copy-start(s32[64]{0:T(128)} %param.11) | copy-start | bytes 772
  11.4 3.3 %copy-start.9 = (s32[15]{0:T(128)S(1)}, s32[15]{0:T(128)}, u32[]{:S(2)}) copy-start(s32[15]{0:T(128)} %constant.9.clone) | copy-start | bytes 184
  11.4 3.3 %copy-start.8 = (s32[64]{0:T(128)S(1)}, s32[64]{0:T(128)}, u32[]{:S(2)}) copy-start(s32[64]{0:T(128)} %param.12) | copy-start | bytes 772
  11.4 4.0 %copy-start.6 = (s32[2048]{0:T(1024)S(1)}, s32[2048]{0:T(1024)}, u32[]{:S(2)}) copy-start(s32[2048]{0:T(1024)} %param.9) | copy-start | bytes 24580
  11.4 4.0 %copy-start.7 = (s32[2048]{0:T(1024)S(1)}, s32[2048]{0:T(1024)}, u32[]{:S(2)}) copy-start(s32[2048]{0:T(1024)} %param.8) | copy-start | bytes 24580
  11.4 23.0 %collective-permute-start = (bf16[256,768]{1,0:T(8,128)(2,1)}, bf16[256,768]{1,0:T(8,128)(2,1)}, u32[]{:S(2)}, u32[]{:S(2)}) collective-permute-start(bf16[256,768]{1,0:T(8,128)(2,1)} %get-tuple-element.83), channel_id=1, source_target_pairs={{0,2},{1,3},{2,0},{3,1},{4,6},{5,7},{6,4},{7,5},{8,10},{9,11},{10,... | collective-permute-start | bytes 1179656 | tf_op jit(solution)/shard_map/ppermute | solution.py:203
  11.7 44.8 %collective-permute-start.1 = (bf16[256,768]{1,0:T(8,128)(2,1)}, bf16[256,768]{1,0:T(8,128)(2,1)}, u32[]{:S(2)}, u32[]{:S(2)}) collective-permute-start(bf16[256,768]{1,0:T(8,128)(2,1)} %get-tuple-element.87), channel_id=1, source_target_pairs={{0,10},{1,11},{2,8},{3,9},{4,14},{5,15},{6,12},{7,13},{8,2},{9,3},... | collective-permute-start | bytes 1179656 | tf_op jit(solution)/shard_map/ppermute | solution.py:203
  12.8 46.0 %collective-permute-start.3 = (bf16[256,768]{1,0:T(8,128)(2,1)}, bf16[256,768]{1,0:T(8,128)(2,1)}, u32[]{:S(2)}, u32[]{:S(2)}) collective-permute-start(bf16[256,768]{1,0:T(8,128)(2,1)} %get-tuple-element.90), channel_id=1, source_target_pairs={{0,3},{1,2},{2,1},{3,0},{4,7},{5,6},{6,5},{7,4},{8,11},{9,10},{10,... | collective-permute-start | bytes 1179656 | tf_op jit(solution)/shard_map/ppermute | solution.py:203
  30.9 34.1 %collective-permute-start.5 = (bf16[256,768]{1,0:T(8,128)(2,1)}, bf16[256,768]{1,0:T(8,128)(2,1)}, u32[]{:S(2)}, u32[]{:S(2)}) collective-permute-start(bf16[256,768]{1,0:T(8,128)(2,1)} %get-tuple-element.93), channel_id=1, source_target_pairs={{0,11},{1,10},{2,9},{3,8},{4,15},{5,14},{6,13},{7,12},{8,3},{9,2},... | collective-permute-start | bytes 1179656 | tf_op jit(solution)/shard_map/ppermute | solution.py:203
  34.4 47.4 %collective-permute-start.11 = (bf16[256,768]{1,0:T(8,128)(2,1)}, bf16[256,768]{1,0:T(8,128)(2,1)}, u32[]{:S(2)}, u32[]{:S(2)}) collective-permute-start(bf16[256,768]{1,0:T(8,128)(2,1)} %get-tuple-element.102), channel_id=1, source_target_pairs={{0,9},{1,8},{2,11},{3,10},{4,13},{5,12},{6,15},{7,14},{8,1},{9,0},... | collective-permute-start | bytes 1179656 | tf_op jit(solution)/shard_map/ppermute | solution.py:203
  39.4 43.9 %all-to-all-start = ((f32[16,2,256]{2,1,0:T(2,128)}), f32[16,2,256]{2,1,0:T(2,128)S(1)}, u32[]{:S(2)}, u32[]{:S(2)}) async-start(f32[16,2,256]{2,1,0:T(2,128)} %gather_fusion), calls=%async_computation | async-start | bytes 65536 | tf_op jit(solution)/shard_map/all_to_all | solution.py:237
  45.8 52.2 %collective-permute-start.14 = (bf16[256,768]{1,0:T(8,128)(2,1)}, bf16[256,768]{1,0:T(8,128)(2,1)}, u32[]{:S(2)}, u32[]{:S(2)}) collective-permute-start(bf16[256,768]{1,0:T(8,128)(2,1)} %get-tuple-element.108), channel_id=1, source_target_pairs={{0,4},{1,5},{2,6},{3,7},{4,0},{5,1},{6,2},{7,3},{8,12},{9,13},{10,... | collective-permute-start | bytes 1179656 | tf_op jit(solution)/shard_map/ppermute | solution.py:203
  56.5 59.6 %collective-permute-start.10 = (bf16[256,768]{1,0:T(8,128)(2,1)}, bf16[256,768]{1,0:T(8,128)(2,1)}, u32[]{:S(2)}, u32[]{:S(2)}) collective-permute-start(bf16[256,768]{1,0:T(8,128)(2,1)} %get-tuple-element.100), channel_id=1, source_target_pairs={{0,5},{1,4},{2,7},{3,6},{4,1},{5,0},{6,3},{7,2},{8,13},{9,12},{10,... | collective-permute-start | bytes 1179656 | tf_op jit(solution)/shard_map/ppermute | solution.py:203
  58.7 63.2 %collective-permute-start.8 = (bf16[256,768]{1,0:T(8,128)(2,1)}, bf16[256,768]{1,0:T(8,128)(2,1)}, u32[]{:S(2)}, u32[]{:S(2)}) collective-permute-start(bf16[256,768]{1,0:T(8,128)(2,1)} %get-tuple-element.97), channel_id=1, source_target_pairs={{0,12},{1,13},{2,14},{3,15},{4,8},{5,9},{6,10},{7,11},{8,4},{9,5},... | collective-permute-start | bytes 1179656 | tf_op jit(solution)/shard_map/ppermute | solution.py:203
  64.9 57.0 %collective-permute-start.13 = (bf16[256,768]{1,0:T(8,128)(2,1)}, bf16[256,768]{1,0:T(8,128)(2,1)}, u32[]{:S(2)}, u32[]{:S(2)}) collective-permute-start(bf16[256,768]{1,0:T(8,128)(2,1)} %get-tuple-element.104), channel_id=1, source_target_pairs={{0,6},{1,7},{2,4},{3,5},{4,2},{5,3},{6,0},{7,1},{8,14},{9,15},{10,... | collective-permute-start | bytes 1179656 | tf_op jit(solution)/shard_map/ppermute | solution.py:203
  81.8 66.4 %collective-permute-start.2 = (bf16[256,768]{1,0:T(8,128)(2,1)}, bf16[256,768]{1,0:T(8,128)(2,1)}, u32[]{:S(2)}, u32[]{:S(2)}) collective-permute-start(bf16[256,768]{1,0:T(8,128)(2,1)} %get-tuple-element.88), channel_id=1, source_target_pairs={{0,14},{1,15},{2,12},{3,13},{4,10},{5,11},{6,8},{7,9},{8,6},{9,7},... | collective-permute-start | bytes 1179656 | tf_op jit(solution)/shard_map/ppermute | solution.py:203
  83.2 1.5 copy-start.3
  83.2 1.5 copy-start.4
  84.8 13.2 %copy-start.12 = (bf16[256,768]{1,0:T(8,128)(2,1)S(1)}, bf16[256,768]{1,0:T(8,128)(2,1)}, u32[]{:S(2)}) copy-start(bf16[256,768]{1,0:T(8,128)(2,1)} %get-tuple-element.103) | copy-start | bytes 1179652
  97.9 28.7 %collective-permute-start.12 = (bf16[256,768]{1,0:T(8,128)(2,1)S(1)}, bf16[256,768]{1,0:T(8,128)(2,1)S(1)}, u32[]{:S(2)}, u32[]{:S(2)}) collective-permute-start(bf16[256,768]{1,0:T(8,128)(2,1)S(1)} %copy-done.12), channel_id=1, source_target_pairs={{0,13},{1,12},{2,15},{3,14},{4,9},{5,8},{6,11},{7,10},{8,5},{9,4},... | collective-permute-start | bytes 1179656 | tf_op jit(solution)/shard_map/ppermute | solution.py:203
  115.9 1.0 copy-start.10
  115.9 5.9 %copy-start.11 = (bf16[256,768]{1,0:T(8,128)(2,1)S(1)}, bf16[256,768]{1,0:T(8,128)(2,1)}, u32[]{:S(2)}) copy-start(bf16[256,768]{1,0:T(8,128)(2,1)} %get-tuple-element.94) | copy-start | bytes 1179652
  116.9 30.6 %collective-permute-start.4 = (bf16[256,768]{1,0:T(8,128)(2,1)S(1)}, bf16[256,768]{1,0:T(8,128)(2,1)S(1)}, u32[]{:S(2)}, u32[]{:S(2)}) collective-permute-start(bf16[256,768]{1,0:T(8,128)(2,1)S(1)} %copy-done.10), channel_id=1, source_target_pairs={{0,7},{1,6},{2,5},{3,4},{4,3},{5,2},{6,1},{7,0},{8,15},{9,14},{10,... | collective-permute-start | bytes 1179656 | tf_op jit(solution)/shard_map/ppermute | solution.py:203
  121.9 25.6 %collective-permute-start.6 = (bf16[256,768]{1,0:T(8,128)(2,1)S(1)}, bf16[256,768]{1,0:T(8,128)(2,1)S(1)}, u32[]{:S(2)}, u32[]{:S(2)}) collective-permute-start(bf16[256,768]{1,0:T(8,128)(2,1)S(1)} %copy-done.11), channel_id=1, source_target_pairs={{0,15},{1,14},{2,13},{3,12},{4,11},{5,10},{6,9},{7,8},{8,7},{9,6},... | collective-permute-start | bytes 1179656 | tf_op jit(solution)/shard_map/ppermute | solution.py:203
  121.9 49.8 %collective-permute-start.21 = (f16[256,256]{1,0:T(8,128)(2,1)S(1)}, f16[256,256]{1,0:T(8,128)(2,1)S(1)}, u32[]{:S(2)}, u32[]{:S(2)}) collective-permute-start(f16[256,256]{1,0:T(8,128)(2,1)S(1)} %convert_element_type.173), channel_id=1, source_target_pairs={{0,11},{1,10},{2,9},{3,8},{4,15},{5,14},{6,13},{7,12},{8,3},{9,2},... | collective-permute-start | bytes 393224 | tf_op jit(solution)/shard_map/ppermute | solution.py:203
  126.6 45.1 %collective-permute-start.20 = (f16[256,256]{1,0:T(8,128)(2,1)S(1)}, f16[256,256]{1,0:T(8,128)(2,1)S(1)}, u32[]{:S(2)}, u32[]{:S(2)}) collective-permute-start(f16[256,256]{1,0:T(8,128)(2,1)S(1)} %convert_element_type.170), channel_id=1, source_target_pairs={{0,3},{1,2},{2,1},{3,0},{4,7},{5,6},{6,5},{7,4},{8,11},{9,10},{10,... | collective-permute-start | bytes 393224 | tf_op jit(solution)/shard_map/ppermute | solution.py:203
  147.5 24.4 %collective-permute-start.19 = (f16[256,256]{1,0:T(8,128)(2,1)S(1)}, f16[256,256]{1,0:T(8,128)(2,1)S(1)}, u32[]{:S(2)}, u32[]{:S(2)}) collective-permute-start(f16[256,256]{1,0:T(8,128)(2,1)S(1)} %convert_element_type.167), channel_id=1, source_target_pairs={{0,10},{1,11},{2,8},{3,9},{4,14},{5,15},{6,12},{7,13},{8,2},{9,3},... | collective-permute-start | bytes 393224 | tf_op jit(solution)/shard_map/ppermute | solution.py:203
  147.5 24.5 %collective-permute-start.18 = (f16[256,256]{1,0:T(8,128)(2,1)S(1)}, f16[256,256]{1,0:T(8,128)(2,1)S(1)}, u32[]{:S(2)}, u32[]{:S(2)}) collective-permute-start(f16[256,256]{1,0:T(8,128)(2,1)S(1)} %convert_element_type.164), channel_id=1, source_target_pairs={{0,2},{1,3},{2,0},{3,1},{4,6},{5,7},{6,4},{7,5},{8,10},{9,11},{10,... | collective-permute-start | bytes 393224 | tf_op jit(solution)/shard_map/ppermute | solution.py:203
  148.2 24.9 %collective-permute-start.17 = (f16[256,256]{1,0:T(8,128)(2,1)S(1)}, f16[256,256]{1,0:T(8,128)(2,1)S(1)}, u32[]{:S(2)}, u32[]{:S(2)}) collective-permute-start(f16[256,256]{1,0:T(8,128)(2,1)S(1)} %convert_element_type.161), channel_id=1, source_target_pairs={{0,9},{1,8},{2,11},{3,10},{4,13},{5,12},{6,15},{7,14},{8,1},{9,0},... | collective-permute-start | bytes 393224 | tf_op jit(solution)/shard_map/ppermute | solution.py:203
  171.7 5.1 %collective-permute-start.16 = (f16[256,256]{1,0:T(8,128)(2,1)S(1)}, f16[256,256]{1,0:T(8,128)(2,1)S(1)}, u32[]{:S(2)}, u32[]{:S(2)}) collective-permute-start(f16[256,256]{1,0:T(8,128)(2,1)S(1)} %convert_element_type.158), channel_id=1, source_target_pairs={{0,1},{1,0},{2,3},{3,2},{4,5},{5,4},{6,7},{7,6},{8,9},{9,8},{10,11... | collective-permute-start | bytes 393224 | tf_op jit(solution)/shard_map/ppermute | solution.py:203
  171.8 5.6 %collective-permute-start.15 = (f16[256,256]{1,0:T(8,128)(2,1)S(1)}, f16[256,256]{1,0:T(8,128)(2,1)S(1)}, u32[]{:S(2)}, u32[]{:S(2)}) collective-permute-start(f16[256,256]{1,0:T(8,128)(2,1)S(1)} %convert_element_type.155), channel_id=1, source_target_pairs={{0,8},{1,9},{2,10},{3,11},{4,12},{5,13},{6,14},{7,15},{8,0},{9,1},... | collective-permute-start | bytes 393224 | tf_op jit(solution)/shard_map/ppermute | solution.py:203
  171.9 6.2 %collective-permute-start.22 = (f16[256,256]{1,0:T(8,128)(2,1)S(1)}, f16[256,256]{1,0:T(8,128)(2,1)S(1)}, u32[]{:S(2)}, u32[]{:S(2)}) collective-permute-start(f16[256,256]{1,0:T(8,128)(2,1)S(1)} %convert_element_type.175), channel_id=1, source_target_pairs={{0,4},{1,5},{2,6},{3,7},{4,0},{5,1},{6,2},{7,3},{8,12},{9,13},{10,... | collective-permute-start | bytes 393224 | tf_op jit(solution)/shard_map/ppermute | solution.py:203
  172.0 10.6 %collective-permute-start.29 = (f16[256,256]{1,0:T(8,128)(2,1)S(1)}, f16[256,256]{1,0:T(8,128)(2,1)S(1)}, u32[]{:S(2)}, u32[]{:S(2)}) collective-permute-start(f16[256,256]{1,0:T(8,128)(2,1)S(1)} %convert_element_type.172), channel_id=1, source_target_pairs={{0,15},{1,14},{2,13},{3,12},{4,11},{5,10},{6,9},{7,8},{8,7},{9,6},... | collective-permute-start | bytes 393224 | tf_op jit(solution)/shard_map/ppermute | solution.py:203
  173.1 12.7 %collective-permute-start.28 = (f16[256,256]{1,0:T(8,128)(2,1)S(1)}, f16[256,256]{1,0:T(8,128)(2,1)S(1)}, u32[]{:S(2)}, u32[]{:S(2)}) collective-permute-start(f16[256,256]{1,0:T(8,128)(2,1)S(1)} %convert_element_type.169), channel_id=1, source_target_pairs={{0,7},{1,6},{2,5},{3,4},{4,3},{5,2},{6,1},{7,0},{8,15},{9,14},{10,... | collective-permute-start | bytes 393224 | tf_op jit(solution)/shard_map/ppermute | solution.py:203
  176.8 11.6 %collective-permute-start.27 = (f16[256,256]{1,0:T(8,128)(2,1)S(1)}, f16[256,256]{1,0:T(8,128)(2,1)S(1)}, u32[]{:S(2)}, u32[]{:S(2)}) collective-permute-start(f16[256,256]{1,0:T(8,128)(2,1)S(1)} %convert_element_type.166), channel_id=1, source_target_pairs={{0,14},{1,15},{2,12},{3,13},{4,10},{5,11},{6,8},{7,9},{8,6},{9,7},... | collective-permute-start | bytes 393224 | tf_op jit(solution)/shard_map/ppermute | solution.py:203
  177.4 13.7 %collective-permute-start.26 = (f16[256,256]{1,0:T(8,128)(2,1)S(1)}, f16[256,256]{1,0:T(8,128)(2,1)S(1)}, u32[]{:S(2)}, u32[]{:S(2)}) collective-permute-start(f16[256,256]{1,0:T(8,128)(2,1)S(1)} %convert_element_type.163), channel_id=1, source_target_pairs={{0,6},{1,7},{2,4},{3,5},{4,2},{5,3},{6,0},{7,1},{8,14},{9,15},{10,... | collective-permute-start | bytes 393224 | tf_op jit(solution)/shard_map/ppermute | solution.py:203
  178.1 14.9 %collective-permute-start.25 = (f16[256,256]{1,0:T(8,128)(2,1)S(1)}, f16[256,256]{1,0:T(8,128)(2,1)S(1)}, u32[]{:S(2)}, u32[]{:S(2)}) collective-permute-start(f16[256,256]{1,0:T(8,128)(2,1)S(1)} %convert_element_type.160), channel_id=1, source_target_pairs={{0,13},{1,12},{2,15},{3,14},{4,9},{5,8},{6,11},{7,10},{8,5},{9,4},... | collective-permute-start | bytes 393224 | tf_op jit(solution)/shard_map/ppermute | solution.py:203
  182.5 13.4 %collective-permute-start.24 = (f16[256,256]{1,0:T(8,128)(2,1)S(1)}, f16[256,256]{1,0:T(8,128)(2,1)S(1)}, u32[]{:S(2)}, u32[]{:S(2)}) collective-permute-start(f16[256,256]{1,0:T(8,128)(2,1)S(1)} %convert_element_type.157), channel_id=1, source_target_pairs={{0,5},{1,4},{2,7},{3,6},{4,1},{5,0},{6,3},{7,2},{8,13},{9,12},{10,... | collective-permute-start | bytes 393224 | tf_op jit(solution)/shard_map/ppermute | solution.py:203
  185.8 12.4 %collective-permute-start.23 = (f16[256,256]{1,0:T(8,128)(2,1)S(1)}, f16[256,256]{1,0:T(8,128)(2,1)S(1)}, u32[]{:S(2)}, u32[]{:S(2)}) collective-permute-start(f16[256,256]{1,0:T(8,128)(2,1)S(1)} %convert_element_type.154), channel_id=1, source_target_pairs={{0,12},{1,13},{2,14},{3,15},{4,8},{5,9},{6,10},{7,11},{8,4},{9,5},... | collective-permute-start | bytes 393224 | tf_op jit(solution)/shard_map/ppermute | solution.py:203
  203.9 8.1 %copy-start.1 = (f32[8,256,256]{2,1,0:T(8,128)}, f32[8,256,256]{2,1,0:T(8,128)S(1)}, u32[]{:S(2)}) copy-start(f32[8,256,256]{2,1,0:T(8,128)S(1)} %get-tuple-element.154.labels) | copy-start | bytes 6291460
  203.9 55.6 %all-to-all-start.1 = ((bf16[16,256,256]{2,1,0:T(8,128)(2,1)}), bf16[16,256,256]{2,1,0:T(8,128)(2,1)}, u32[]{:S(2)}, u32[]{:S(2)}) async-start(bf16[16,256,256]{2,1,0:T(8,128)(2,1)} %get-tuple-element.155), calls=%async_computation.1 | async-start | bytes 4194304 | tf_op jit(solution)/shard_map/all_to_all | solution.py:361
  259.5 52.4 %all-to-all-start.2 = ((f16[16,256,256]{2,1,0:T(8,128)(2,1)}), f16[16,256,256]{2,1,0:T(8,128)(2,1)}, u32[]{:S(2)}, u32[]{:S(2)}) async-start(f16[16,256,256]{2,1,0:T(8,128)(2,1)} %convert_element_type.185), calls=%async_computation.2 | async-start | bytes 4194304 | tf_op jit(solution)/shard_map/all_to_all | solution.py:361
  264.4 1.6 copy-start.2
